TPU v7x, 128 devices: a whole 4x4x4 slice. The times are simulated.
128 devices in a mesh: layer: 8 (over y, core), feat: 16 (over z, x).
Axes of the slice: x: 4, y: 4, z: 4, core: 2. Of those that a mesh axis runs over, the one named last changes fastest.
Arguments:
- layer_input: bfloat16 [8, 512, 4096], P('layer', None, 'feat'), may hold values from -6 to 6
- enc_weight: bfloat16 [8, 4096, 2048], P('layer', None, 'feat'), may hold values from -0.09375 to 0.09375
- enc_bias: float32 [8, 2048], P('layer', 'feat'), may hold values from -3 to 3
- active: int32 [8, 512, 256], P('layer'), may hold values from 0 to 127
- dec_weight: bfloat16 [8, 8, 2048, 4096], P(None, 'layer', 'feat'), may hold values from -0.125 to 0.125
- dec_bias: float32 [8, 4096], P('layer'), may hold values from -3 to 3
- target: bfloat16 [8, 512, 4096], P('layer'), may hold values from -6 to 6
Outputs:
- rebuilt: float32 [8, 512, 4096], P('layer', None, 'feat')
- dec_grad: bfloat16 [8, 8, 2048, 4096], P(None, 'layer', 'feat')
- enc_grad: float32 [8, 4096, 2048], P('layer', None, 'feat')
Inputs may be any that keep to these rules, and one draw needn't show every extreme that they name: `active`: each entry is a feature's offset within its block of 128 features; entry j of a token names a feature of block j // 16; repeats may occur.
All inputs are finite; a program needn't handle non-finite values.
Results may differ from a plain program's by a relative error of at most 0.0053.
Values may be sent and summed in bfloat16 or wider, within the bound.
No kernel may reach another device: no remote copies, remote signals or barrier semaphores. Data moves between devices by JAX's collectives and lax.ppermute only.
A program may use at most 128 MiB of HBM per device.

v0:
```python
import jax
import jax.numpy as jnp
from jax import lax
from jax.sharding import PartitionSpec as P

FBLK = 128
PICKS = 16
TOK = 512


def local(layer_input, enc_weight, enc_bias, active, dec_weight, dec_bias, target):
    layers = dec_weight.shape[0]
    feat_dev = enc_weight.shape[2]
    model_width = target.shape[2]
    d_share = layer_input.shape[2]
    tok_rows = target.shape[1]
    loss_scale = TOK ** (-0.5)
    target_layer = lax.axis_index("layer")
    feat_index = lax.axis_index("feat")
    feat_start = feat_index * feat_dev
    d_start = feat_index * d_share
    inputs = lax.all_gather(layer_input, "feat", axis=2, tiled=True)[0]
    preact = (
        jnp.dot(inputs, enc_weight[0], preferred_element_type=jnp.float32) + enc_bias[0][None, :]
    )
    block_base = jnp.arange(active.shape[2], dtype=jnp.int32) // PICKS * FBLK
    feature_ids = active[0] + block_base[None, :] - feat_start
    local_feats = jnp.arange(feat_dev, dtype=jnp.int32)
    gates = jnp.any(feature_ids[:, :, None] == local_feats[None, None, :], axis=1).astype(
        jnp.float32
    )
    activity = (gates * preact).astype(jnp.bfloat16)
    sources = jnp.arange(layers, dtype=jnp.int32)
    live_rows = (sources <= target_layer).astype(jnp.bfloat16)
    all_activity = lax.all_gather(activity[None], "layer", axis=0, tiled=True)
    masked = all_activity * live_rows[:, None, None]
    flat_codes = jnp.transpose(masked, (1, 0, 2)).reshape(tok_rows, layers * feat_dev)
    flat_dec = dec_weight[:, 0].reshape(layers * feat_dev, model_width)
    partial_value = jnp.dot(flat_codes, flat_dec, preferred_element_type=jnp.float32)
    summed = lax.psum(partial_value, "feat")
    rebuilt_full = summed + dec_bias[0][None, :]
    errors = rebuilt_full - target[0].astype(jnp.float32)
    signal = (errors * loss_scale).astype(jnp.bfloat16)
    rebuilt = lax.dynamic_slice_in_dim(rebuilt_full, d_start, d_share, 1)
    dec_grad = jnp.einsum("stf,td->sfd", masked, signal, preferred_element_type=jnp.float32).astype(
        jnp.bfloat16
    )[:, None]
    dec_block = dec_weight[:, 0]
    term_rows = jnp.einsum("td,sfd->stf", signal, dec_block, preferred_element_type=jnp.float32)
    kept_rows = jnp.arange(1 * lax.axis_size("layer"), dtype=jnp.int32) <= target_layer
    code_grad = lax.psum_scatter(
        term_rows * kept_rows.astype(jnp.float32)[:, None, None],
        "layer",
        scatter_dimension=0,
        tiled=True,
    )[0]
    pre_grad = (gates * code_grad).astype(jnp.bfloat16)
    enc_grad = lax.dot_general(
        inputs, pre_grad, (((0,), (0,)), ((), ())), preferred_element_type=jnp.float32
    )
    return (rebuilt[None], dec_grad, enc_grad[None])


def solution(mesh):
    return jax.shard_map(
        local,
        mesh=mesh,
        in_specs=(
            P("layer", None, "feat"),
            P("layer", None, "feat"),
            P("layer", "feat"),
            P("layer", None, None),
            P(None, "layer", "feat", None),
            P("layer", None),
            P("layer", None, None),
        ),
        out_specs=(
            P("layer", None, "feat"),
            P(None, "layer", "feat", None),
            P("layer", None, "feat"),
        ),
        check_vma=False,
    )
```

profile of v0, /device:TPU:0, one launch (start us, length us, event | category | flops | bytes accessed | tf_op | source)
XLA Modules:
  0.0 310.7 jit_solution(1441788058988408123)
XLA Ops:
  7.2 0.0 copy-start
  7.2 0.0 all-gather.4.cloned.1.call-start
  7.2 0.7 all-gather.4.cloned.1.call-update
  7.9 0.0 all-gather.6.cloned.1.call-start
  8.0 1.1 fusion.21
  9.1 22.3 %fusion = pred[512,128]{1,0:T(8,128)(4,1)S(1)} fusion(s32[512,256]{1,0:T(8,128)S(1)} %fusion.21), kind=kLoop, calls=%fused_computation.1 | loop fusion | flops 33488896 | bytes 589824 | tf_op jit(solution)/shard_map/reduce_or | solution.py:29
  31.4 39.0 %all-gather.4.cloned.1.call-done = bf16[1,512,4096]{2,1,0:T(8,128)(2,1)} async-done(((bf16[1,512,256]{2,1,0:T(8,128)(2,1)}), bf16[1,512,4096]{2,1,0:T(8,128)(2,1)}) %all-gather.4.cloned.1.call-update) | async-done | bytes 4194320 | tf_op jit(solution)/shard_map/all_gather | solution.py:22
  70.4 0.0 copy-done
  70.4 4.1 %fusion.17 = bf16[512,128]{1,0:T(8,128)(2,1)} fusion(pred[512,128]{1,0:T(8,128)(4,1)S(1)} %fusion, bf16[1,512,4096]{2,1,0:T(8,128)(2,1)} %all-gather.4.cloned.1.call-done, bf16[1,4096,128]{2,1,0:T(8,128)(2,1)S(1)} %copy-done, f32[128]{0:T(128)} %bitcast.66), kind=kOutput, calls=%fused_computation.17 | convolution fusion | flops 537067520 | bytes 5440000 | tf_op jit(solution)/shard_map/dot_general | solution.py:24
  74.5 0.0 all-gather.6.cloned.1.call-update
  74.5 0.0 all-reduce.2.cloned.1.call-start
  74.6 22.7 %all-gather.6.cloned.1.call-done = bf16[4096,128]{1,0:T(8,128)(2,1)} async-done(((bf16[512,128]{1,0:T(8,128)(2,1)}), bf16[4096,128]{1,0:T(8,128)(2,1)}) %all-gather.6.cloned.1.call-update) | async-done | bytes 1048592 | tf_op jit(solution)/shard_map/all_gather | solution.py:35
  97.3 1.5 copy.13
  98.8 0.1 broadcast_multiply_fusion
  98.9 10.2 %fusion.29 = f32[512,4096]{1,0:T(8,128)} fusion(bf16[512,1024]{0,1:T(8,128)(2,1)S(1)} %bitcast.63, bf16[1024,4096]{1,0:T(8,128)(2,1)} %bitcast.62), kind=kOutput, calls=%fused_computation.34 | convolution fusion | flops 4294967296 | bytes 17825792 | tf_op jit(solution)/shard_map/dot_general | solution.py:39
  109.1 0.0 copy-start.2
  109.1 0.0 all-reduce.2.cloned.1.call-update
  109.2 0.0 reduce-scatter.2.cloned.1.call-start
  109.2 141.7 %all-reduce.2.cloned.1.call-done = f32[512,4096]{1,0:T(8,128)} async-done(((f32[512,4096]{1,0:T(8,128)}), f32[512,4096]{1,0:T(8,128)}) %all-reduce.2.cloned.1.call-update) | async-done | bytes 8388624 | tf_op jit(solution)/shard_map/psum | solution.py:40
  251.0 0.0 copy-done.2
  251.0 0.0 copy-start.3
  251.0 4.3 %broadcast_add_fusion = f32[512,4096]{1,0:T(8,128)S(1)} fusion(f32[512,4096]{1,0:T(8,128)} %all-reduce.2.cloned.1.call-done, f32[4096]{0:T(1024)S(1)} %bitcast.65), kind=kLoop, calls=%fused_computation.13 | loop fusion | flops 2097152 | bytes 16793600 | tf_op jit(solution)/shard_map/add | solution.py:41
  255.3 0.0 copy-start.1
  255.3 3.2 %copy-done.1 = f32[512,4096]{1,0:T(8,128)} copy-done((f32[512,4096]{1,0:T(8,128)}, f32[512,4096]{1,0:T(8,128)S(1)}, u32[]{:S(2)}) %copy-start.1) | copy-done | bytes 8388632
  258.6 0.0 copy-done.3
  258.6 8.1 %multiply_bitcast_fusion = f32[8,512,128]{2,1,0:T(8,128)} fusion(bf16[8,1,128,4096]{3,2,1,0:T(8,128)(2,1)} %param.11, f32[8]{0:T(128)S(1)} %compare_convert_fusion, f32[512,4096]{1,0:T(8,128)S(1)} %broadcast_add_fusion, bf16[1,512,4096]{2,1,0:T(8,128)(2,1)S(1)} %copy-done.3), kind=kOutput, calls=%fused_computation.14 | convolution fusion | flops 4303880192 | bytes 23068704 | tf_op jit(solution)/shard_map/td,sfd->stf/dot_general | solution.py:49
  266.7 0.0 reduce-scatter.2.cloned.1.call-update
  266.7 1.9 dynamic-slice_bitcast_fusion
  268.6 11.4 %convert_bitcast_fusion = bf16[8,1,128,4096]{3,2,1,0:T(8,128)(2,1)} fusion(bf16[8,512,128]{1,2,0:T(8,128)(2,1)S(1)} %broadcast_multiply_fusion, f32[512,4096]{1,0:T(8,128)} %copy-done.1, bf16[1,512,4096]{2,1,0:T(8,128)(2,1)} %param.13), kind=kOutput, calls=%fused_computation.7 | convolution fusion | flops 4307550208 | bytes 22020096 | tf_op jit(solution)/shard_map/stf,td->sfd/dot_general | solution.py:45
  279.9 19.4 %reduce-scatter.2.cloned.1.call-done = f32[1,512,128]{2,1,0:T(8,128)} async-done(((f32[8,512,128]{2,1,0:T(8,128)}), f32[1,512,128]{2,1,0:T(8,128)}) %reduce-scatter.2.cloned.1.call-update) | async-done | bytes 262160 | tf_op jit(solution)/shard_map/reduce_scatter | solution.py:51
  299.3 3.0 convolution_bitcast_fusion
  302.3 1.8 copy.15
  (3 shorter events, 0.0 us)
Async XLA Ops:
  7.2 63.2 %copy-start = (bf16[1,4096,128]{2,1,0:T(8,128)(2,1)S(1)}, bf16[1,4096,128]{2,1,0:T(8,128)(2,1)}, u32[]{:S(2)}) copy-start(bf16[1,4096,128]{2,1,0:T(8,128)(2,1)} %param.8) | copy-start | bytes 3145732
  7.2 63.2 %all-gather.4.cloned.1.call-start = ((), (), s32[]{:S(2)}) async-start(), calls=%async_computation.1 | async-start | bytes 4456448 | tf_op jit(solution)/shard_map/all_gather | solution.py:22
  7.9 89.4 %all-gather.6.cloned.1.call-start = ((), (), s32[]{:S(2)}) async-start(), calls=%async_computation.4 | async-start | bytes 1179648 | tf_op jit(solution)/shard_map/all_gather | solution.py:35
  74.5 176.5 %all-reduce.2.cloned.1.call-start = ((), (), s32[]{:S(2)}) async-start(), calls=%async_computation.2 | async-start | bytes 16777216 | tf_op jit(solution)/shard_map/psum | solution.py:40
  109.1 141.8 %copy-start.2 = (f32[1,4096]{1,0:T(1,128)S(1)}, f32[1,4096]{1,0:T(1,128)}, u32[]{:S(2)}) copy-start(f32[1,4096]{1,0:T(1,128)} %param.12) | copy-start | bytes 49156
  109.2 190.1 %reduce-scatter.2.cloned.1.call-start = ((), (), s32[]{:S(2)}) async-start(), calls=%async_computation.3 | async-start | bytes 2359296 | tf_op jit(solution)/shard_map/reduce_scatter | solution.py:51
  251.0 7.6 %copy-start.3 = (bf16[1,512,4096]{2,1,0:T(8,128)(2,1)S(1)}, bf16[1,512,4096]{2,1,0:T(8,128)(2,1)}, u32[]{:S(2)}) copy-start(bf16[1,512,4096]{2,1,0:T(8,128)(2,1)} %param.13) | copy-start | bytes 12582916
  255.3 3.2 %copy-start.1 = (f32[512,4096]{1,0:T(8,128)}, f32[512,4096]{1,0:T(8,128)S(1)}, u32[]{:S(2)}) copy-start(f32[512,4096]{1,0:T(8,128)S(1)} %broadcast_add_fusion) | copy-start | bytes 25165828
Sparse Core Ops, SparseCore 0:
  10.1 60.1 all-gather.3
  74.6 22.6 all-gather.5
  109.3 141.6 all-reduce.1
  266.8 32.4 reduce-scatter.1
where the time goes:
time: 311 us
  waiting for transfers between devices  224 us (72%)
  matrix products  36.8 us (12%)
  other arithmetic  27.9 us (9%)
  between operations  13.9 us (4%)
  local copies, waits for them, and re-layouts  8.41 us (3%)
    psum x1, waiting for transfers between devices, local(): summed = lax.psum(partial_value, 'feat')  142 us
    all_gather x1, waiting for transfers between devices, local(): inputs = lax.all_gather(layer_input, 'feat', axis=2, tiled=True)[0]  39 us
    all_gather x1, waiting for transfers between devices, local(): all_activity = lax.all_gather(activity[None], 'layer', axis=0, tiled=True)  22.7 us
    reduce_or x1, other arithmetic, local(): jnp.any(feature_ids[:, :, None] == local_feats[None, None, :], axis=1)  22.3 us
    reduce_scatter x1, waiting for transfers between devices, local(): lax.psum_scatter(term_rows * kept_rows.astype(jnp.float32)[:, None, None]...  19.4 us
    dot_general x1, matrix products, local(): jnp.einsum('stf,td->sfd', masked, signal, preferred_element_type=jnp.floa...  11.4 us
    dot_general x1, matrix products, local(): jnp.dot(flat_codes, flat_dec, preferred_element_type=jnp.float32)  10.2 us
    dot_general x1, matrix products, local(): jnp.einsum('td,sfd->stf', signal, dec_block, preferred_element_type=jnp.f...  8.09 us
  transfers between devices with their start and end apart: 4, of which 4 were waited for; matrix products, arithmetic and copies ran while one was open for 12% of the time, Pallas kernels for 0%

commit v1 on v0

v1 whole, which is shorter than its diff:
```python
import functools

import jax
import jax.numpy as jnp
from jax import lax
from jax.experimental import pallas as pl
from jax.experimental.pallas import tpu as pltpu
from jax.sharding import PartitionSpec as P

PICKS = 16
TOK = 512
AXES = ("layer", "feat")
OFFSETS = (0, -1, 1, 2)
BF16 = jnp.bfloat16
F32 = jnp.float32
PARAMS = pltpu.CompilerParams(vmem_limit_bytes=32 * 1024 * 1024)


def pairs_of(move):
    out = []
    for y in range(4):
        for c in range(2):
            for z in range(4):
                for x in range(4):
                    y2, c2, z2, x2 = move(y, c, z, x)
                    if 0 <= y2 < 4:
                        out.append(((y * 2 + c) * 16 + z * 4 + x, (y2 * 2 + c2) * 16 + (z2 % 4) * 4 + x2 % 4))
    return out


def short(value, step):
    move = lambda y, c, z, x: (y, c, z, x + step) if c == 0 else (y, c, z + step, x)
    return lax.ppermute(value, AXES, pairs_of(move))


def long(value, step):
    move = lambda y, c, z, x: (y, c, z + step, x) if c == 0 else (y, c, z, x + step)
    return lax.ppermute(value, AXES, pairs_of(move))


def chips_y(value, step):
    return lax.ppermute(value, AXES, pairs_of(lambda y, c, z, x: (y + step, c, z, x)))


def other_core(value):
    return lax.ppermute(value, AXES, pairs_of(lambda y, c, z, x: (y, 1 - c, z, x)))


def gather(block):
    r1 = short(block, 1)
    r2 = short(block, -1)
    r3 = short(block, 2)
    u = jnp.stack([block, r1])
    v = jnp.stack([r2, r3])
    u1, u2 = long(u, 1), long(u, -1)
    v1, v2 = long(v, 1), long(v, -1)
    u3, v3 = long(u1, 1), long(v2, -1)
    return u, v, u1, v1, u2, v2, u3, v3


def dot(a, b):
    return jnp.dot(a, b, preferred_element_type=F32)


def encode(scalars, pairs, first, weight, total, finish):
    n = len(pairs)

    def kernel(sc, *refs):
        pair_refs, w, rest = refs[:n], refs[n], refs[n + 1:]
        out = rest[-1]
        acc = jnp.zeros((TOK, 128), F32) if total is None else rest[0][...]
        for i in range(n):
            for k in range(2):
                row = pl.multiple_of(sc[(first + i) * 2 + k] * 256, 256)
                acc += dot(pair_refs[i][k], w[pl.ds(row, 256), :])
        if finish is None:
            out[...] = acc
        else:
            gates, bias = rest[-3], rest[-2]
            out[...] = (gates[...] * (acc + bias[...])).astype(BF16)

    args = list(pairs) + [weight] + ([] if total is None else [total]) + ([] if finish is None else list(finish))
    return pl.pallas_call(
        kernel,
        grid_spec=pltpu.PrefetchScalarGridSpec(
            num_scalar_prefetch=1, grid=(),
            in_specs=[pl.BlockSpec(memory_space=pltpu.VMEM)] * len(args),
            out_specs=pl.BlockSpec(memory_space=pltpu.VMEM),
        ),
        out_shape=jax.ShapeDtypeStruct((TOK, 128), F32 if finish is None else BF16),
        compiler_params=PARAMS,
        cost_estimate=pl.CostEstimate(flops=n * 2 * TOK * 256 * 128 * 2, bytes_accessed=n * 524288 + 1048576, transcendentals=0),
        name="encode",
    )(scalars, *args)


def decode(scalars, acts, dec, pair, add, dtype):
    def kernel(sc, a, w, *rest):
        out = rest[-1]
        y = sc[16]
        acc = rest[0][0].astype(F32) if add is not None else None
        for k in range(4):
            part = dot(a[(y - k) & 3], w[k])
            acc = part if acc is None else acc + part
        out[0] = acc.astype(dtype)

    args = [acts, dec] + ([] if add is None else [add])
    specs = [
        pl.BlockSpec((4, TOK, 256), lambda j, sc: (0, 0, 0)),
        pl.BlockSpec((4, 256, 256), lambda j, sc: (0, 0, sc[2 * pair + j])),
    ] + ([] if add is None else [pl.BlockSpec((1, TOK, 256), lambda j, sc: (j, 0, 0))])
    return pl.pallas_call(
        kernel,
        grid_spec=pltpu.PrefetchScalarGridSpec(
            num_scalar_prefetch=1, grid=(2,), in_specs=specs,
            out_specs=pl.BlockSpec((1, TOK, 256), lambda j, sc: (j, 0, 0)),
        ),
        out_shape=jax.ShapeDtypeStruct((2, TOK, 256), dtype),
        compiler_params=PARAMS,
        cost_estimate=pl.CostEstimate(flops=2 * TOK * 1024 * 512, bytes_accessed=3 * 1048576, transcendentals=0),
        name="decode",
    )(scalars, *args)


def decoder_grad(scalars, acts_t, pairs, first, out):
    n = len(pairs)

    def kernel(sc, a, *refs):
        result = refs[-1]
        y = sc[16]
        j = pl.program_id(0)
        for i in range(n):
            @pl.when(j // 2 == i)
            def _():
                s = refs[i][0]
                for k in range(4):
                    result[k] = dot(a[(y - k) & 3], s).astype(BF16)

    specs = [pl.BlockSpec((4, 256, TOK), lambda j, sc: (0, 0, 0))]
    for i in range(n):
        specs.append(pl.BlockSpec((1, TOK, 256), lambda j, sc, i=i: (jnp.clip(j - 2 * i, 0, 1), 0, 0)))
    args = [acts_t, *pairs]
    aliases = {}
    if out is not None:
        specs.append(pl.BlockSpec(memory_space=pl.ANY))
        args.append(out)
        aliases = {len(args): 0}
    return pl.pallas_call(
        kernel,
        grid_spec=pltpu.PrefetchScalarGridSpec(
            num_scalar_prefetch=1, grid=(2 * n,), in_specs=specs,
            out_specs=pl.BlockSpec((4, 256, 256), lambda j, sc: (0, 0, sc[2 * first + j])),
        ),
        out_shape=jax.ShapeDtypeStruct((4, 256, 4096), BF16),
        input_output_aliases=aliases,
        compiler_params=PARAMS,
        cost_estimate=pl.CostEstimate(flops=n * 2 * 2 * TOK * 1024 * 256, bytes_accessed=n * 2 * 524288, transcendentals=0),
        name="decoder_grad",
    )(scalars, *args)


def code_grad(scalars, pairs, first, dec, total, last):
    n = len(pairs)

    def kernel(sc, *refs):
        w, rest = refs[n], refs[n + 1:]
        acc = rest[-1]
        j = pl.program_id(0)

        @pl.when(j == 0)
        def _():
            for k in range(4):
                acc[k] = jnp.zeros((TOK, 256), F32) if total is None else rest[0][k]

        for i in range(n):
            @pl.when(j // 2 == i)
            def _():
                s = refs[i][0]
                for k in range(4):
                    acc[k] += lax.dot_general(s, w[k], (((1,), (1,)), ((), ())), preferred_element_type=F32)

        @pl.when(j == 2 * n - 1)
        def _():
            if last:
                keep, send = rest[-3], rest[-2]
                y, c = sc[16], sc[17]

                @pl.when(c == 0)
                def _():
                    for k in range(4):
                        keep[k] = acc[k, :, :128]
                        odd = acc[k, :, 128:]
                        send[k] = jnp.where(y == k, 0.0, odd).astype(BF16)

                @pl.when(c == 1)
                def _():
                    for k in range(4):
                        keep[k] = acc[k, :, 128:]
                        send[k] = acc[k, :, :128].astype(BF16)
            else:
                for k in range(4):
                    rest[-2][k] = acc[k]

    specs = []
    for i in range(n):
        specs.append(pl.BlockSpec((1, TOK, 256), lambda j, sc, i=i: (jnp.clip(j - 2 * i, 0, 1), 0, 0)))
    specs.append(pl.BlockSpec((4, 256, 256), lambda j, sc: (0, 0, sc[2 * first + j])))
    args = [*pairs, dec]
    whole = pl.BlockSpec((4, TOK, 256), lambda j, sc: (0, 0, 0))
    half = pl.BlockSpec((4, TOK, 128), lambda j, sc: (0, 0, 0))
    if total is not None:
        specs.append(whole)
        args.append(total)
    if last:
        out_specs = [half, half]
        out_shape = [jax.ShapeDtypeStruct((4, TOK, 128), F32), jax.ShapeDtypeStruct((4, TOK, 128), BF16)]
    else:
        out_specs = whole
        out_shape = jax.ShapeDtypeStruct((4, TOK, 256), F32)
    return pl.pallas_call(
        kernel,
        grid_spec=pltpu.PrefetchScalarGridSpec(
            num_scalar_prefetch=1, grid=(2 * n,), in_specs=specs, out_specs=out_specs,
            scratch_shapes=[pltpu.VMEM((4, TOK, 256), F32)],
        ),
        out_shape=out_shape,
        compiler_params=PARAMS,
        cost_estimate=pl.CostEstimate(flops=n * 2 * 2 * TOK * 1024 * 256, bytes_accessed=n * 2 * 524288, transcendentals=0),
        name="code_grad",
    )(scalars, *args)


def encoder_grad(scalars, pairs, grad):
    n = len(pairs)

    def kernel(sc, *refs):
        g, out = refs[n], refs[-1]
        j = pl.program_id(0)
        for i in range(n):
            @pl.when(j // 2 == i)
            def _():
                out[...] = lax.dot_general(refs[i][0], g[...], (((0,), (0,)), ((), ())), preferred_element_type=F32)

    specs = []
    for i in range(n):
        specs.append(pl.BlockSpec((1, TOK, 256), lambda j, sc, i=i: (jnp.clip(j - 2 * i, 0, 1), 0, 0)))
    specs.append(pl.BlockSpec((TOK, 128), lambda j, sc: (0, 0)))
    return pl.pallas_call(
        kernel,
        grid_spec=pltpu.PrefetchScalarGridSpec(
            num_scalar_prefetch=1, grid=(2 * n,), in_specs=specs,
            out_specs=pl.BlockSpec((256, 128), lambda j, sc: (sc[j], 0)),
        ),
        out_shape=jax.ShapeDtypeStruct((4096, 128), F32),
        compiler_params=PARAMS,
        cost_estimate=pl.CostEstimate(flops=n * 2 * 2 * TOK * 256 * 128, bytes_accessed=n * 2 * 262144, transcendentals=0),
        name="encoder_grad",
    )(scalars, *pairs, grad)


def local(layer_input, enc_weight, enc_bias, active, dec_weight, dec_bias, target):
    layer, feat = lax.axis_index("layer"), lax.axis_index("feat")
    y, c, z, x = layer // 2, layer % 2, feat // 4, feat % 4
    long_at, short_at = jnp.where(c == 0, z, x), jnp.where(c == 0, x, z)
    table = []
    for ob in OFFSETS:
        for oa in OFFSETS:
            at_b, at_a = (long_at + ob) % 4, (short_at + oa) % 4
            table.append(jnp.where(c == 0, at_b * 4 + at_a, at_a * 4 + at_b))
    scalars = jnp.stack(table + [y, c]).astype(jnp.int32)

    dec = dec_weight.reshape(4, 256, 4096)
    inputs = gather(layer_input[0])

    picks = lax.dynamic_slice_in_dim(active[0], feat * PICKS, PICKS, 1)
    gates = jnp.any(picks[:, :, None] == jnp.arange(128, dtype=jnp.int32)[None, None, :], axis=1).astype(F32)

    early = encode(scalars, inputs[:6], 0, enc_weight[0], None, None)
    act = encode(scalars, inputs[6:], 6, enc_weight[0], early, (gates, enc_bias))

    mine = jnp.stack([act, chips_y(act, 1), chips_y(act, 2), chips_y(act, 3)])
    other = other_core(mine)
    other = other.at[0].multiply((c == 1).astype(BF16))
    acts = jnp.where(c == 0, jnp.concatenate([mine, other], 2), jnp.concatenate([other, mine], 2))

    part = functools.partial(decode, scalars, acts, dec)
    from_left = long(part(6, None, BF16), 1)
    from_right = long(part(7, None, BF16), -1)
    v_left = long(part(5, None, BF16), 1)
    u_right = long(part(2, None, BF16), -1)
    u_own, v_own = part(0, None, F32), part(1, None, F32)
    acts_t = jnp.swapaxes(acts, 1, 2)
    u_left = long(part(4, from_left, BF16), 1)
    v_right = long(part(3, from_right, BF16), -1)
    u_sum = u_own + u_left.astype(F32) + u_right.astype(F32)
    v_sum = v_own + v_left.astype(F32) + v_right.astype(F32)
    s1 = short(u_sum[1].astype(BF16), -1)
    s3 = short(v_sum[1].astype(BF16), 2)
    s2 = short(v_sum[0].astype(BF16), 1)
    d_start = feat * 256
    bias = lax.dynamic_slice_in_dim(dec_bias, d_start, 256, 1)
    rebuilt = u_sum[0] + s1.astype(F32) + s2.astype(F32) + s3.astype(F32) + bias
    wanted = lax.dynamic_slice_in_dim(target[0], d_start, 256, 1).astype(F32)
    signal = ((rebuilt - wanted) * (TOK ** -0.5)).astype(BF16)

    sig = gather(signal)
    code = code_grad(scalars, sig[:2], 0, dec, None, False)
    dec_out = decoder_grad(scalars, acts_t, sig[:2], 0, None)
    code = code_grad(scalars, sig[2:6], 2, dec, code, False)
    dec_out = decoder_grad(scalars, acts_t, sig[2:6], 2, dec_out)
    keep, send = code_grad(scalars, sig[6:], 6, dec, code, True)
    keep = keep + other_core(send).astype(F32)
    slot = lambda o: lax.dynamic_index_in_dim(keep, (y - o) % 4, 0, keepdims=False)
    back = [chips_y(slot(o).astype(BF16), -o) for o in (1, 2, 3)]
    dec_out = decoder_grad(scalars, acts_t, sig[6:], 6, dec_out)
    total = slot(0) + back[0].astype(F32) + back[1].astype(F32) + back[2].astype(F32)
    pre = (gates * total).astype(BF16)
    enc_out = encoder_grad(scalars, inputs, pre)
    return rebuilt[None], dec_out.reshape(8, 1, 128, 4096), enc_out[None]


def solution(mesh):
    return jax.shard_map(
        local,
        mesh=mesh,
        in_specs=(
            P("layer", None, "feat"),
            P("layer", None, "feat"),
            P("layer", "feat"),
            P("layer", None, None),
            P(None, "layer", "feat", None),
            P("layer", None),
            P("layer", None, None),
        ),
        out_specs=(
            P("layer", None, "feat"),
            P(None, "layer", "feat", None),
            P("layer", None, "feat"),
        ),
        check_vma=False,
    )
```

time: 311 us -> 186 us (0.60)
  waiting for transfers between devices: 224 us -> 45.9 us
  Pallas kernels: 0 us -> 55.6 us
  starting transfers between devices: 0.16 us -> 52 us
  matrix products: 36.8 us -> 0 us
  other arithmetic: 27.9 us -> 14.7 us
  between operations: 13.9 us -> 1.24 us
  local copies, waits for them, and re-layouts: 8.41 us -> 13.3 us
    psum x1 -> x0, waiting for transfers between devices: 142 us -> none  [local(): summed = lax.psum(partial_value, 'feat')]
    all_gather x2 -> x0, waiting for transfers between devices: 61.7 us -> none  [the longest x1 39 us: local(): inputs = lax.all_gather(layer_input, 'feat', axis=2, tiled=True)[0]]
    pallas_call x0 -> x17, Pallas kernels: none -> 55.6 us  [the longest x3 13 us: decoder_grad(): pl.pallas_call(kernel, grid_spec=pltpu.PrefetchScalarGridSpec(num_scalar_...]
    ppermute x0 -> x35, starting transfers between devices: none -> 52 us  [the longest x18 25.1 us: long(): return lax.ppermute(value, AXES, pairs_of(move))]
    ppermute x0 -> x35, waiting for transfers between devices: none -> 45.9 us  [the longest x18 22.4 us: long(): return lax.ppermute(value, AXES, pairs_of(move))]
    dot_general x5 -> x0, matrix products: 36.8 us -> none  [the longest x1 11.4 us: local(): jnp.einsum('stf,td->sfd', masked, signal, preferred_element_type=jnp.floa...]
    reduce_scatter x1 -> x0, waiting for transfers between devices: 19.4 us -> none  [local(): lax.psum_scatter(term_rows * kept_rows.astype(jnp.float32)[:, None, None]...]
    reduce_or x1, other arithmetic: 22.3 us -> 5.77 us  [local(): jnp.any(picks[:, :, None] == jnp.arange(128, dtype=jnp.int32)[None, None,...]
  transfers between devices with their start and end apart: 4 -> 35, of which waited for: 4 -> 16; matrix products, arithmetic and copies ran while one was open for 12% -> 6% of each run, Pallas kernels for 0% -> 20%
where the time goes in v1:
time: 186 us; the launch traced here: 183 us
  Pallas kernels  55.6 us (30%)
  starting transfers between devices  52 us (28%)
  waiting for transfers between devices  45.9 us (25%)
  other arithmetic  14.7 us (8%)
  local copies, waits for them, and re-layouts  13.3 us (7%)
    ppermute x18, starting transfers between devices, long(): return lax.ppermute(value, AXES, pairs_of(move))  25.1 us
    ppermute x18, waiting for transfers between devices, long(): return lax.ppermute(value, AXES, pairs_of(move))  22.4 us
    ppermute x9, waiting for transfers between devices, short(): return lax.ppermute(value, AXES, pairs_of(move))  18.9 us
    ppermute x9, starting transfers between devices, short(): return lax.ppermute(value, AXES, pairs_of(move))  13.9 us
    pallas_call x3, Pallas kernels, decoder_grad(): pl.pallas_call(kernel, grid_spec=pltpu.PrefetchScalarGridSpec(num_scalar_...  13 us
    pallas_call x8, Pallas kernels, decode(): pl.pallas_call(kernel, grid_spec=pltpu.PrefetchScalarGridSpec(num_scalar_...  13 us
    ppermute x6, starting transfers between devices, chips_y(): lax.ppermute(value, AXES, pairs_of(lambda y, c, z, x: (y + step, c, z, x)))  13 us
    pallas_call x3, Pallas kernels, code_grad(): pl.pallas_call(kernel, grid_spec=pltpu.PrefetchScalarGridSpec(num_scalar_...  12.6 us
  transfers between devices with their start and end apart: 35, of which 16 were waited for; matrix products, arithmetic and copies ran while one was open for 6% of the time, Pallas kernels for 20%

profile of v1, /device:TPU:0, one launch (start us, length us, event | category | flops | bytes accessed | tf_op | source)
XLA Modules:
  0.0 182.8 jit_solution(17684836493840152012)
XLA Ops:
  0.7 1.6 collective-permute-start
  2.3 2.7 %collective-permute-start.4 = (bf16[512,256]{1,0:T(8,128)(2,1)}, bf16[512,256]{1,0:T(8,128)(2,1)S(1)}, u32[]{:S(2)}, u32[]{:S(2)}) collective-permute-start(bf16[512,256]{1,0:T(8,128)(2,1)} %bitcast.111), channel_id=1, source_target_pairs={{0,2},{1,3},{2,0},{3,1},{4,6},{5,7},{6,4},{7,5},{8,10},{9,11},{10,... | collective-permute-start | bytes 786440 | tf_op jit(solution)/shard_map/ppermute | solution.py:33
  6.5 2.1 %collective-permute-done = bf16[512,256]{1,0:T(8,128)(2,1)S(1)} collective-permute-done((bf16[512,256]{1,0:T(8,128)(2,1)}, bf16[512,256]{1,0:T(8,128)(2,1)S(1)}, u32[]{:S(2)}, u32[]{:S(2)}) %collective-permute-start) | collective-permute-done | bytes 262176 | tf_op jit(solution)/shard_map/ppermute | solution.py:33
  9.5 2.1 %collective-permute-start.1 = (bf16[2,512,256]{2,1,0:T(8,128)(2,1)S(1)}, bf16[2,512,256]{2,1,0:T(8,128)(2,1)S(1)}, u32[]{:S(2)}, u32[]{:S(2)}) collective-permute-start(bf16[2,512,256]{2,1,0:T(8,128)(2,1)S(1)} %pad_maximum_fusion.refs_0_), channel_id=1, source_target_pairs={{0,4},{1,5},{2,6},{3,7},{4,8},{5,9},{6,10},{7,11},{8,12},{9,13},{1... | collective-permute-start | bytes 1572872 | tf_op jit(solution)/shard_map/ppermute | solution.py:38
  12.5 4.2 %collective-permute-start.5 = (bf16[2,512,256]{2,1,0:T(8,128)(2,1)S(1)}, bf16[2,512,256]{2,1,0:T(8,128)(2,1)}, u32[]{:S(2)}, u32[]{:S(2)}) collective-permute-start(bf16[2,512,256]{2,1,0:T(8,128)(2,1)S(1)} %pad_maximum_fusion.1.refs_1_), channel_id=1, source_target_pairs={{0,12},{1,13},{2,14},{3,15},{4,0},{5,1},{6,2},{7,3},{8,4},{9,5},{1... | collective-permute-start | bytes 1572872 | tf_op jit(solution)/shard_map/ppermute | solution.py:38
  17.1 1.6 collective-permute-start.7
  18.7 2.2 %collective-permute-done.1.refs_2_ = bf16[2,512,256]{2,1,0:T(8,128)(2,1)S(1)} collective-permute-done((bf16[2,512,256]{2,1,0:T(8,128)(2,1)S(1)}, bf16[2,512,256]{2,1,0:T(8,128)(2,1)S(1)}, u32[]{:S(2)}, u32[]{:S(2)}) %collective-permute-start.1) | collective-permute-done | bytes 524320 | tf_op jit(solution)/shard_map/ppermute | solution.py:38
  20.9 2.5 %collective-permute-done.5.refs_5_ = bf16[2,512,256]{2,1,0:T(8,128)(2,1)} collective-permute-done((bf16[2,512,256]{2,1,0:T(8,128)(2,1)S(1)}, bf16[2,512,256]{2,1,0:T(8,128)(2,1)}, u32[]{:S(2)}, u32[]{:S(2)}) %collective-permute-start.5) | collective-permute-done | bytes 524320 | tf_op jit(solution)/shard_map/ppermute | solution.py:38
  23.4 3.8 %collective-permute-start.6 = (bf16[2,512,256]{2,1,0:T(8,128)(2,1)}, bf16[2,512,256]{2,1,0:T(8,128)(2,1)}, u32[]{:S(2)}, u32[]{:S(2)}) collective-permute-start(bf16[2,512,256]{2,1,0:T(8,128)(2,1)} %collective-permute-done.5.refs_5_), channel_id=1, source_target_pairs={{0,12},{1,13},{2,14},{3,15},{4,0},{5,1},{6,2},{7,3},{8,4},{9,5},{1... | collective-permute-start | bytes 1572872 | tf_op jit(solution)/shard_map/ppermute | solution.py:38
  27.3 5.8 %fusion = pred[512,128]{1,0:T(8,128)(4,1)S(1)} fusion(s32[512,16]{1,0:T(8,128)S(1)} %dynamic-slice_bitcast_fusion), kind=kLoop, calls=%fused_computation.1 | loop fusion | flops 2031616 | bytes 98304 | tf_op jit(solution)/shard_map/reduce_or | solution.py:276
  33.9 2.9 %encode.2.refs_3_ = f32[512,128]{1,0:T(8,128)S(1)} custom-call(s32[18]{0:T(128)S(1)} %stack.123.sc, bf16[2,512,256]{2,1,0:T(8,128)(2,1)S(1)} %pad_maximum_fusion.refs_0_, bf16[2,512,256]{2,1,0:T(8,128)(2,1)S(1)} %pad_maximum_fusion.1.refs_1_, bf16[2,512,256]{2,1,0:T(8,128)(2,1)S(1)} %collective-permute-done.1.refs_2_, ...), custom_call_target="tpu_custom_call" | custom-call | flops 402653184 | bytes 4194304 | tf_op jit(solution)/shard_map/encode/pallas_call | solution.py:83
  36.8 2.2 %encode.3 = bf16[512,128]{1,0:T(8,128)(2,1)S(1)} custom-call(s32[18]{0:T(128)S(1)} %stack.123.sc, bf16[2,512,256]{2,1,0:T(8,128)(2,1)} %collective-permute-done.2.refs_0_.refs_6_, bf16[2,512,256]{2,1,0:T(8,128)(2,1)} %collective-permute-done.6.refs_1_.refs_7_, bf16[4096,128]{1,0:T(8,128)(2,1)S(1)} %bitcast.94, f32[512,128]{1,0:T(8,128)S(1)} %encode.2.refs_3_, ...), custom_call_target="tpu_custom_call" | custom-call | flops 134217728 | bytes 2097152 | tf_op jit(solution)/shard_map/encode/pallas_call | solution.py:83
  39.2 4.9 %collective-permute-start.11 = (bf16[512,128]{0,1:T(8,128)(2,1)S(1)}, bf16[512,128]{0,1:T(8,128)(2,1)S(1)}, u32[]{:S(2)}, u32[]{:S(2)}) collective-permute-start(bf16[512,128]{0,1:T(8,128)(2,1)S(1)} %copy.25), channel_id=1, source_target_pairs={{0,96},{1,97},{2,98},{3,99},{4,100},{5,101},{6,102},{7,103},{8,104... | collective-permute-start | bytes 393224 | tf_op jit(solution)/shard_map/ppermute | solution.py:42
  45.4 2.8 %collective-permute-start.9 = (bf16[512,128]{0,1:T(8,128)(2,1)S(1)}, bf16[512,128]{0,1:T(8,128)(2,1)S(1)}, u32[]{:S(2)}, u32[]{:S(2)}) collective-permute-start(bf16[512,128]{0,1:T(8,128)(2,1)S(1)} %copy.25), channel_id=1, source_target_pairs={{0,32},{1,33},{2,34},{3,35},{4,36},{5,37},{6,38},{7,39},{8,40},{9,... | collective-permute-start | bytes 393224 | tf_op jit(solution)/shard_map/ppermute | solution.py:42
  48.2 2.4 %collective-permute-done.9 = bf16[512,128]{0,1:T(8,128)(2,1)S(1)} collective-permute-done((bf16[512,128]{0,1:T(8,128)(2,1)S(1)}, bf16[512,128]{0,1:T(8,128)(2,1)S(1)}, u32[]{:S(2)}, u32[]{:S(2)}) %collective-permute-start.9) | collective-permute-done | bytes 131104 | tf_op jit(solution)/shard_map/ppermute | solution.py:42
  51.5 2.1 %collective-permute-done.12 = bf16[4,512,128]{1,2,0:T(8,128)(2,1)S(1)} collective-permute-done((bf16[4,512,128]{1,2,0:T(8,128)(2,1)}, bf16[4,512,128]{1,2,0:T(8,128)(2,1)S(1)}, u32[]{:S(2)}, u32[]{:S(2)}) %collective-permute-start.12) | collective-permute-done | bytes 524320 | tf_op jit(solution)/shard_map/ppermute | solution.py:46
  57.4 3.4 %copy-done.1 = bf16[8,1,128,4096]{3,2,1,0:T(8,128)(2,1)S(1)} copy-done((bf16[8,1,128,4096]{3,2,1,0:T(8,128)(2,1)S(1)}, bf16[8,1,128,4096]{3,2,1,0:T(8,128)(2,1)}, u32[]{:S(2)}) %copy-start.1) | copy-done | bytes 8388632
  60.8 1.6 decode.14
  62.4 1.6 collective-permute-start.18
  64.0 1.6 decode.13
  65.7 1.6 decode.9
  67.9 3.7 %collective-permute-done.18.rest_0_ = bf16[2,512,256]{2,1,0:T(8,128)(2,1)S(1)} collective-permute-done((bf16[2,512,256]{2,1,0:T(8,128)(2,1)S(1)}, bf16[2,512,256]{2,1,0:T(8,128)(2,1)S(1)}, u32[]{:S(2)}, u32[]{:S(2)}) %collective-permute-start.18) | collective-permute-done | bytes 524320 | tf_op jit(solution)/shard_map/ppermute | solution.py:38
  71.7 1.6 decode.15
  73.3 2.8 %collective-permute-start.19 = (bf16[2,512,256]{2,1,0:T(8,128)(2,1)S(1)}, bf16[2,512,256]{2,1,0:T(8,128)(2,1)S(1)}, u32[]{:S(2)}, u32[]{:S(2)}) collective-permute-start(bf16[2,512,256]{2,1,0:T(8,128)(2,1)S(1)} %decode.15), channel_id=1, source_target_pairs={{0,12},{1,13},{2,14},{3,15},{4,0},{5,1},{6,2},{7,3},{8,4},{9,5},{1... | collective-permute-start | bytes 1572872 | tf_op jit(solution)/shard_map/ppermute | solution.py:38
  76.1 1.6 decode.11
  78.0 1.6 decode.12
  79.7 1.6 decode.8
  81.3 1.6 decode.10
  82.9 2.1 %collective-permute-start.14 = (bf16[2,512,256]{2,1,0:T(8,128)(2,1)S(1)}, bf16[2,512,256]{2,1,0:T(8,128)(2,1)S(1)}, u32[]{:S(2)}, u32[]{:S(2)}) collective-permute-start(bf16[2,512,256]{2,1,0:T(8,128)(2,1)S(1)} %decode.10), channel_id=1, source_target_pairs={{0,4},{1,5},{2,6},{3,7},{4,8},{5,9},{6,10},{7,11},{8,12},{9,13},{1... | collective-permute-start | bytes 1572872 | tf_op jit(solution)/shard_map/ppermute | solution.py:38
  86.0 2.4 %collective-permute-done.15 = bf16[2,512,256]{2,1,0:T(8,128)(2,1)S(1)} collective-permute-done((bf16[2,512,256]{2,1,0:T(8,128)(2,1)S(1)}, bf16[2,512,256]{2,1,0:T(8,128)(2,1)S(1)}, u32[]{:S(2)}, u32[]{:S(2)}) %collective-permute-start.15) | collective-permute-done | bytes 524320 | tf_op jit(solution)/shard_map/ppermute | solution.py:38
  88.4 5.0 %collective-permute-done.14 = bf16[2,512,256]{2,1,0:T(8,128)(2,1)S(1)} collective-permute-done((bf16[2,512,256]{2,1,0:T(8,128)(2,1)S(1)}, bf16[2,512,256]{2,1,0:T(8,128)(2,1)S(1)}, u32[]{:S(2)}, u32[]{:S(2)}) %collective-permute-start.14) | collective-permute-done | bytes 524320 | tf_op jit(solution)/shard_map/ppermute | solution.py:38
  94.3 2.4 %collective-permute-start.16 = (bf16[512,256]{1,0:T(8,128)(2,1)}, bf16[512,256]{1,0:T(8,128)(2,1)}, u32[]{:S(2)}, u32[]{:S(2)}) collective-permute-start(bf16[512,256]{1,0:T(8,128)(2,1)} %fusion.7), channel_id=1, source_target_pairs={{0,3},{1,0},{2,1},{3,2},{4,7},{5,4},{6,5},{7,6},{8,11},{9,8},{10,9... | collective-permute-start | bytes 786440 | tf_op jit(solution)/shard_map/ppermute | solution.py:33
  96.7 2.4 %collective-permute-start.21 = (bf16[512,256]{1,0:T(8,128)(2,1)}, bf16[512,256]{1,0:T(8,128)(2,1)}, u32[]{:S(2)}, u32[]{:S(2)}) collective-permute-start(bf16[512,256]{1,0:T(8,128)(2,1)} %get-tuple-element.31), channel_id=1, source_target_pairs={{0,2},{1,3},{2,0},{3,1},{4,6},{5,7},{6,4},{7,5},{8,10},{9,11},{10,... | collective-permute-start | bytes 786440 | tf_op jit(solution)/shard_map/ppermute | solution.py:33
  101.0 6.5 %collective-permute-done.20 = bf16[512,256]{1,0:T(8,128)(2,1)} collective-permute-done((bf16[512,256]{1,0:T(8,128)(2,1)}, bf16[512,256]{1,0:T(8,128)(2,1)}, u32[]{:S(2)}, u32[]{:S(2)}) %collective-permute-start.20) | collective-permute-done | bytes 262176 | tf_op jit(solution)/shard_map/ppermute | solution.py:33
  107.4 2.2 %fusion.6 = (bf16[512,256]{1,0:T(8,128)(2,1)S(1)}, f32[1,512,256]{2,1,0:T(8,128)}) fusion(bf16[1,512,4096]{2,1,0:T(8,128)(2,1)} %param.15, s32[]{:T(128)S(6)} %select_n.229, f32[256]{0:T(256)S(1)} %bitcast.119, bf16[512,256]{1,0:T(8,128)(2,1)} %collective-permute-done.21, bf16[512,256]{1,0:T(8,128)(2,1)} %collective-permute-done.20, ...), kind=kLoop, calls=%fused_computation.19 | loop fusion | flops 1441792 | bytes 2360324 | tf_op jit(solution)/shard_map/convert_element_type | solution.py:304
  109.6 2.2 %collective-permute-start.26 = (bf16[512,256]{1,0:T(8,128)(2,1)S(1)}, bf16[512,256]{1,0:T(8,128)(2,1)S(1)}, u32[]{:S(2)}, u32[]{:S(2)}) collective-permute-start(bf16[512,256]{1,0:T(8,128)(2,1)S(1)} %get-tuple-element.25), channel_id=1, source_target_pairs={{0,2},{1,3},{2,0},{3,1},{4,6},{5,7},{6,4},{7,5},{8,10},{9,11},{10,... | collective-permute-start | bytes 786440 | tf_op jit(solution)/shard_map/ppermute | solution.py:33
  112.8 6.8 %collective-permute-done.22 = bf16[512,256]{1,0:T(8,128)(2,1)S(1)} collective-permute-done((bf16[512,256]{1,0:T(8,128)(2,1)S(1)}, bf16[512,256]{1,0:T(8,128)(2,1)S(1)}, u32[]{:S(2)}, u32[]{:S(2)}) %collective-permute-start.22) | collective-permute-done | bytes 262176 | tf_op jit(solution)/shard_map/ppermute | solution.py:33
  123.1 3.0 %collective-permute-start.30 = (bf16[2,512,256]{2,1,0:T(8,128)(2,1)S(1)}, bf16[2,512,256]{2,1,0:T(8,128)(2,1)S(1)}, u32[]{:S(2)}, u32[]{:S(2)}) collective-permute-start(bf16[2,512,256]{2,1,0:T(8,128)(2,1)S(1)} %pad_maximum_fusion.3.refs_0_), channel_id=1, source_target_pairs={{0,12},{1,13},{2,14},{3,15},{4,0},{5,1},{6,2},{7,3},{8,4},{9,5},{1... | collective-permute-start | bytes 1572872 | tf_op jit(solution)/shard_map/ppermute | solution.py:38
  126.1 4.1 %collective-permute-done.23.refs_0_ = bf16[2,512,256]{2,1,0:T(8,128)(2,1)S(1)} collective-permute-done((bf16[2,512,256]{2,1,0:T(8,128)(2,1)S(1)}, bf16[2,512,256]{2,1,0:T(8,128)(2,1)S(1)}, u32[]{:S(2)}, u32[]{:S(2)}) %collective-permute-start.23) | collective-permute-done | bytes 524320 | tf_op jit(solution)/shard_map/ppermute | solution.py:38
  130.1 2.5 %collective-permute-done.27.refs_3_ = bf16[2,512,256]{2,1,0:T(8,128)(2,1)S(1)} collective-permute-done((bf16[2,512,256]{2,1,0:T(8,128)(2,1)S(1)}, bf16[2,512,256]{2,1,0:T(8,128)(2,1)S(1)}, u32[]{:S(2)}, u32[]{:S(2)}) %collective-permute-start.27) | collective-permute-done | bytes 524320 | tf_op jit(solution)/shard_map/ppermute | solution.py:38
  133.5 3.4 %copy-done.2 = bf16[8,1,128,4096]{3,2,1,0:T(8,128)(2,1)S(1)} copy-done((bf16[8,1,128,4096]{3,2,1,0:T(8,128)(2,1)S(1)}, bf16[8,1,128,4096]{3,2,1,0:T(8,128)(2,1)}, u32[]{:S(2)}) %copy-start.2) | copy-done | bytes 8388632
  136.9 3.1 %code_grad.3.refs_5_ = f32[4,512,256]{2,1,0:T(8,128)S(1)} custom-call(s32[18]{0:T(128)S(1)} %stack.123.sc, bf16[2,512,256]{2,1,0:T(8,128)(2,1)S(1)} %pad_maximum_fusion.3.refs_0_, bf16[2,512,256]{2,1,0:T(8,128)(2,1)S(1)} %pad_maximum_fusion.4.refs_1_, bf16[4,256,4096]{2,1,0:T(8,128)(2,1)S(1)} %bitcast.90), custom_call_target="tpu_custom_call" | custom-call | flops 1073741824 | bytes 2097152 | tf_op jit(solution)/shard_map/code_grad/pallas_call | solution.py:220
  140.1 5.6 %code_grad.4.refs_3_ = f32[4,512,256]{2,1,0:T(8,128)S(1)} custom-call(s32[18]{0:T(128)S(1)} %stack.123.sc, bf16[2,512,256]{2,1,0:T(8,128)(2,1)S(1)} %collective-permute-done.23.refs_0_, bf16[2,512,256]{2,1,0:T(8,128)(2,1)S(1)} %collective-permute-done.29.refs_1_, bf16[2,512,256]{2,1,0:T(8,128)(2,1)S(1)} %collective-permute-done.30.refs_2_, ...), custom_call_target="tpu_custom_call" | custom-call | flops 2147483648 | bytes 4194304 | tf_op jit(solution)/shard_map/code_grad/pallas_call | solution.py:220
  145.7 3.9 %code_grad.5 = (f32[4,512,128]{2,1,0:T(8,128)S(1)}, bf16[4,512,128]{2,1,0:T(8,128)(2,1)}) custom-call(s32[18]{0:T(128)S(1)} %stack.123.sc, bf16[2,512,256]{2,1,0:T(8,128)(2,1)S(1)} %collective-permute-done.24.refs_0_, bf16[2,512,256]{2,1,0:T(8,128)(2,1)S(1)} %collective-permute-done.28.refs_1_, bf16[4,256,4096]{2,1,0:T(8,128)(2,1)S(1)} %bitcast.92, ...), custom_call_target="tpu_custom_call" | custom-call | flops 1073741824 | bytes 2097152 | tf_op jit(solution)/shard_map/code_grad/pallas_call | solution.py:220
  152.3 3.5 %decoder_grad.3.refs_4_ = bf16[4,256,4096]{2,1,0:T(8,128)(2,1)} custom-call(s32[18]{0:T(128)S(1)} %stack.123.sc, bf16[4,256,512]{2,1,0:T(8,128)(2,1)S(1)} %fusion.17.a, bf16[2,512,256]{2,1,0:T(8,128)(2,1)S(1)} %pad_maximum_fusion.3.refs_0_, bf16[2,512,256]{2,1,0:T(8,128)(2,1)S(1)} %pad_maximum_fusion.4.refs_1_), custom_call_target="tpu_custom_call" | custom-call | flops 1073741824 | bytes 2097152 | tf_op jit(solution)/shard_map/decoder_grad/pallas_call | solution.py:148
  161.2 6.0 %decoder_grad.4.refs_2_ = bf16[4,256,4096]{2,1,0:T(8,128)(2,1)} custom-call(s32[18]{0:T(128)S(1)} %stack.123.sc, bf16[4,256,512]{2,1,0:T(8,128)(2,1)S(1)} %fusion.17.a, bf16[2,512,256]{2,1,0:T(8,128)(2,1)S(1)} %copy-done.5, bf16[2,512,256]{2,1,0:T(8,128)(2,1)S(1)} %copy-done.11, bf16[2,512,256]{2,1,0:T(8,128)(2,1)S(1)} %copy-done.9, ...), custom_call_target="tpu_custom_call", output_to_operand_aliasing={{}: (6, {})} | custom-call | flops 2147483648 | bytes 4194304 | tf_op jit(solution)/shard_map/decoder_grad/pallas_call | solution.py:148
  167.3 3.5 %decoder_grad.5 = bf16[4,256,4096]{2,1,0:T(8,128)(2,1)} custom-call(s32[18]{0:T(128)S(1)} %stack.123.sc, bf16[4,256,512]{2,1,0:T(8,128)(2,1)S(1)} %fusion.17.a, bf16[2,512,256]{2,1,0:T(8,128)(2,1)S(1)} %copy-done.13, bf16[2,512,256]{2,1,0:T(8,128)(2,1)S(1)} %copy-done.15, bf16[4,256,4096]{2,1,0:T(8,128)(2,1)} %decoder_grad.4.refs_2_), custom_call_target="tpu_custom_call", output_to_operand_aliasing={{}: (4, {})} | custom-call | flops 1073741824 | bytes 2097152 | tf_op jit(solution)/shard_map/decoder_grad/pallas_call | solution.py:148
  170.9 11.8 %encoder_grad.1 = f32[4096,128]{1,0:T(8,128)} custom-call(s32[18]{0:T(128)S(1)} %stack.123.sc, bf16[2,512,256]{2,1,0:T(8,128)(2,1)S(1)} %pad_maximum_fusion.refs_0_, bf16[2,512,256]{2,1,0:T(8,128)(2,1)S(1)} %pad_maximum_fusion.1.refs_1_, bf16[2,512,256]{2,1,0:T(8,128)(2,1)S(1)} %collective-permute-done.1.refs_2_, ...), custom_call_target="tpu_custom_call" | custom-call | flops 536870912 | bytes 4194304 | tf_op jit(solution)/shard_map/encoder_grad/pallas_call | solution.py:248
  (108 shorter events, 28.8 us)
Async XLA Ops:
  0.6 26.5 %copy-start = (s32[1,512,256]{2,1,0:T(8,128)S(1)}, s32[1,512,256]{2,1,0:T(8,128)}, u32[]{:S(2)}) copy-start(s32[1,512,256]{2,1,0:T(8,128)} %param.12) | copy-start | bytes 1572868
  0.6 33.3 %copy-start.3 = (bf16[1,4096,128]{2,1,0:T(8,128)(2,1)S(1)}, bf16[1,4096,128]{2,1,0:T(8,128)(2,1)}, u32[]{:S(2)}) copy-start(bf16[1,4096,128]{2,1,0:T(8,128)(2,1)} %param.10) | copy-start | bytes 3145732
  0.7 7.9 %collective-permute-start = (bf16[512,256]{1,0:T(8,128)(2,1)}, bf16[512,256]{1,0:T(8,128)(2,1)S(1)}, u32[]{:S(2)}, u32[]{:S(2)}) collective-permute-start(bf16[512,256]{1,0:T(8,128)(2,1)} %bitcast.110), channel_id=1, source_target_pairs={{0,1},{1,2},{2,3},{3,0},{4,5},{5,6},{6,7},{7,4},{8,9},{9,10},{10,1... | collective-permute-start | bytes 786440 | tf_op jit(solution)/shard_map/ppermute | solution.py:33
  2.3 10.1 %collective-permute-start.4 = (bf16[512,256]{1,0:T(8,128)(2,1)}, bf16[512,256]{1,0:T(8,128)(2,1)S(1)}, u32[]{:S(2)}, u32[]{:S(2)}) collective-permute-start(bf16[512,256]{1,0:T(8,128)(2,1)} %bitcast.111), channel_id=1, source_target_pairs={{0,2},{1,3},{2,0},{3,1},{4,6},{5,7},{6,4},{7,5},{8,10},{9,11},{10,... | collective-permute-start | bytes 786440 | tf_op jit(solution)/shard_map/ppermute | solution.py:33
  5.0 7.4 %collective-permute-start.3 = (bf16[512,256]{1,0:T(8,128)(2,1)}, bf16[512,256]{1,0:T(8,128)(2,1)S(1)}, u32[]{:S(2)}, u32[]{:S(2)}) collective-permute-start(bf16[512,256]{1,0:T(8,128)(2,1)} %bitcast.112), channel_id=1, source_target_pairs={{0,3},{1,0},{2,1},{3,2},{4,7},{5,4},{6,5},{7,6},{8,11},{9,8},{10,9... | collective-permute-start | bytes 786440 | tf_op jit(solution)/shard_map/ppermute | solution.py:33
  9.5 11.3 %collective-permute-start.1 = (bf16[2,512,256]{2,1,0:T(8,128)(2,1)S(1)}, bf16[2,512,256]{2,1,0:T(8,128)(2,1)S(1)}, u32[]{:S(2)}, u32[]{:S(2)}) collective-permute-start(bf16[2,512,256]{2,1,0:T(8,128)(2,1)S(1)} %pad_maximum_fusion.refs_0_), channel_id=1, source_target_pairs={{0,4},{1,5},{2,6},{3,7},{4,8},{5,9},{6,10},{7,11},{8,12},{9,13},{1... | collective-permute-start | bytes 1572872 | tf_op jit(solution)/shard_map/ppermute | solution.py:38
  12.5 10.9 %collective-permute-start.5 = (bf16[2,512,256]{2,1,0:T(8,128)(2,1)S(1)}, bf16[2,512,256]{2,1,0:T(8,128)(2,1)}, u32[]{:S(2)}, u32[]{:S(2)}) collective-permute-start(bf16[2,512,256]{2,1,0:T(8,128)(2,1)S(1)} %pad_maximum_fusion.1.refs_1_), channel_id=1, source_target_pairs={{0,12},{1,13},{2,14},{3,15},{4,0},{5,1},{6,2},{7,3},{8,4},{9,5},{1... | collective-permute-start | bytes 1572872 | tf_op jit(solution)/shard_map/ppermute | solution.py:38
  16.7 17.2 %collective-permute-start.8 = (bf16[2,512,256]{2,1,0:T(8,128)(2,1)S(1)}, bf16[2,512,256]{2,1,0:T(8,128)(2,1)}, u32[]{:S(2)}, u32[]{:S(2)}) collective-permute-start(bf16[2,512,256]{2,1,0:T(8,128)(2,1)S(1)} %pad_maximum_fusion.refs_0_), channel_id=1, source_target_pairs={{0,12},{1,13},{2,14},{3,15},{4,0},{5,1},{6,2},{7,3},{8,4},{9,5},{1... | collective-permute-start | bytes 1572872 | tf_op jit(solution)/shard_map/ppermute | solution.py:38
  17.1 16.8 %collective-permute-start.7 = (bf16[2,512,256]{2,1,0:T(8,128)(2,1)S(1)}, bf16[2,512,256]{2,1,0:T(8,128)(2,1)}, u32[]{:S(2)}, u32[]{:S(2)}) collective-permute-start(bf16[2,512,256]{2,1,0:T(8,128)(2,1)S(1)} %pad_maximum_fusion.1.refs_1_), channel_id=1, source_target_pairs={{0,4},{1,5},{2,6},{3,7},{4,8},{5,9},{6,10},{7,11},{8,12},{9,13},{1... | collective-permute-start | bytes 1572872 | tf_op jit(solution)/shard_map/ppermute | solution.py:38
  20.9 15.9 %collective-permute-start.2 = (bf16[2,512,256]{2,1,0:T(8,128)(2,1)S(1)}, bf16[2,512,256]{2,1,0:T(8,128)(2,1)}, u32[]{:S(2)}, u32[]{:S(2)}) collective-permute-start(bf16[2,512,256]{2,1,0:T(8,128)(2,1)S(1)} %collective-permute-done.1.refs_2_), channel_id=1, source_target_pairs={{0,4},{1,5},{2,6},{3,7},{4,8},{5,9},{6,10},{7,11},{8,12},{9,13},{1... | collective-permute-start | bytes 1572872 | tf_op jit(solution)/shard_map/ppermute | solution.py:38
  23.4 13.5 %collective-permute-start.6 = (bf16[2,512,256]{2,1,0:T(8,128)(2,1)}, bf16[2,512,256]{2,1,0:T(8,128)(2,1)}, u32[]{:S(2)}, u32[]{:S(2)}) collective-permute-start(bf16[2,512,256]{2,1,0:T(8,128)(2,1)} %collective-permute-done.5.refs_5_), channel_id=1, source_target_pairs={{0,12},{1,13},{2,14},{3,15},{4,0},{5,1},{6,2},{7,3},{8,4},{9,5},{1... | collective-permute-start | bytes 1572872 | tf_op jit(solution)/shard_map/ppermute | solution.py:38
  39.2 9.0 %collective-permute-start.11 = (bf16[512,128]{0,1:T(8,128)(2,1)S(1)}, bf16[512,128]{0,1:T(8,128)(2,1)S(1)}, u32[]{:S(2)}, u32[]{:S(2)}) collective-permute-start(bf16[512,128]{0,1:T(8,128)(2,1)S(1)} %copy.25), channel_id=1, source_target_pairs={{0,96},{1,97},{2,98},{3,99},{4,100},{5,101},{6,102},{7,103},{8,104... | collective-permute-start | bytes 393224 | tf_op jit(solution)/shard_map/ppermute | solution.py:42
  44.1 4.1 %collective-permute-start.10 = (bf16[512,128]{0,1:T(8,128)(2,1)S(1)}, bf16[512,128]{0,1:T(8,128)(2,1)S(1)}, u32[]{:S(2)}, u32[]{:S(2)}) collective-permute-start(bf16[512,128]{0,1:T(8,128)(2,1)S(1)} %copy.25), channel_id=1, source_target_pairs={{0,64},{1,65},{2,66},{3,67},{4,68},{5,69},{6,70},{7,71},{8,72},{9,... | collective-permute-start | bytes 393224 | tf_op jit(solution)/shard_map/ppermute | solution.py:42
  45.4 5.3 %collective-permute-start.9 = (bf16[512,128]{0,1:T(8,128)(2,1)S(1)}, bf16[512,128]{0,1:T(8,128)(2,1)S(1)}, u32[]{:S(2)}, u32[]{:S(2)}) collective-permute-start(bf16[512,128]{0,1:T(8,128)(2,1)S(1)} %copy.25), channel_id=1, source_target_pairs={{0,32},{1,33},{2,34},{3,35},{4,36},{5,37},{6,38},{7,39},{8,40},{9,... | collective-permute-start | bytes 393224 | tf_op jit(solution)/shard_map/ppermute | solution.py:42
  51.5 2.1 %collective-permute-start.12 = (bf16[4,512,128]{1,2,0:T(8,128)(2,1)}, bf16[4,512,128]{1,2,0:T(8,128)(2,1)S(1)}, u32[]{:S(2)}, u32[]{:S(2)}) collective-permute-start(bf16[4,512,128]{1,2,0:T(8,128)(2,1)} %pad_maximum_fusion.2), channel_id=1, source_target_pairs={{0,16},{1,17},{2,18},{3,19},{4,20},{5,21},{6,22},{7,23},{8,24},{9,... | collective-permute-start | bytes 1572872 | tf_op jit(solution)/shard_map/ppermute | solution.py:46
  62.4 9.3 %collective-permute-start.18 = (bf16[2,512,256]{2,1,0:T(8,128)(2,1)S(1)}, bf16[2,512,256]{2,1,0:T(8,128)(2,1)S(1)}, u32[]{:S(2)}, u32[]{:S(2)}) collective-permute-start(bf16[2,512,256]{2,1,0:T(8,128)(2,1)S(1)} %decode.14), channel_id=1, source_target_pairs={{0,12},{1,13},{2,14},{3,15},{4,0},{5,1},{6,2},{7,3},{8,4},{9,5},{1... | collective-permute-start | bytes 1572872 | tf_op jit(solution)/shard_map/ppermute | solution.py:38
  67.3 14.0 %collective-permute-start.13 = (bf16[2,512,256]{2,1,0:T(8,128)(2,1)S(1)}, bf16[2,512,256]{2,1,0:T(8,128)(2,1)S(1)}, u32[]{:S(2)}, u32[]{:S(2)}) collective-permute-start(bf16[2,512,256]{2,1,0:T(8,128)(2,1)S(1)} %decode.9), channel_id=1, source_target_pairs={{0,4},{1,5},{2,6},{3,7},{4,8},{5,9},{6,10},{7,11},{8,12},{9,13},{1... | collective-permute-start | bytes 1572872 | tf_op jit(solution)/shard_map/ppermute | solution.py:38
  67.8 17.2 %collective-permute-start.17 = (bf16[2,512,256]{2,1,0:T(8,128)(2,1)S(1)}, bf16[2,512,256]{2,1,0:T(8,128)(2,1)S(1)}, u32[]{:S(2)}, u32[]{:S(2)}) collective-permute-start(bf16[2,512,256]{2,1,0:T(8,128)(2,1)S(1)} %decode.13), channel_id=1, source_target_pairs={{0,4},{1,5},{2,6},{3,7},{4,8},{5,9},{6,10},{7,11},{8,12},{9,13},{1... | collective-permute-start | bytes 1572872 | tf_op jit(solution)/shard_map/ppermute | solution.py:38
  73.3 11.7 %collective-permute-start.19 = (bf16[2,512,256]{2,1,0:T(8,128)(2,1)S(1)}, bf16[2,512,256]{2,1,0:T(8,128)(2,1)S(1)}, u32[]{:S(2)}, u32[]{:S(2)}) collective-permute-start(bf16[2,512,256]{2,1,0:T(8,128)(2,1)S(1)} %decode.15), channel_id=1, source_target_pairs={{0,12},{1,13},{2,14},{3,15},{4,0},{5,1},{6,2},{7,3},{8,4},{9,5},{1... | collective-permute-start | bytes 1572872 | tf_op jit(solution)/shard_map/ppermute | solution.py:38
  77.8 10.7 %collective-permute-start.15 = (bf16[2,512,256]{2,1,0:T(8,128)(2,1)S(1)}, bf16[2,512,256]{2,1,0:T(8,128)(2,1)S(1)}, u32[]{:S(2)}, u32[]{:S(2)}) collective-permute-start(bf16[2,512,256]{2,1,0:T(8,128)(2,1)S(1)} %decode.11), channel_id=1, source_target_pairs={{0,12},{1,13},{2,14},{3,15},{4,0},{5,1},{6,2},{7,3},{8,4},{9,5},{1... | collective-permute-start | bytes 1572872 | tf_op jit(solution)/shard_map/ppermute | solution.py:38
  82.9 10.5 %collective-permute-start.14 = (bf16[2,512,256]{2,1,0:T(8,128)(2,1)S(1)}, bf16[2,512,256]{2,1,0:T(8,128)(2,1)S(1)}, u32[]{:S(2)}, u32[]{:S(2)}) collective-permute-start(bf16[2,512,256]{2,1,0:T(8,128)(2,1)S(1)} %decode.10), channel_id=1, source_target_pairs={{0,4},{1,5},{2,6},{3,7},{4,8},{5,9},{6,10},{7,11},{8,12},{9,13},{1... | collective-permute-start | bytes 1572872 | tf_op jit(solution)/shard_map/ppermute | solution.py:38
  94.3 6.7 %collective-permute-start.16 = (bf16[512,256]{1,0:T(8,128)(2,1)}, bf16[512,256]{1,0:T(8,128)(2,1)}, u32[]{:S(2)}, u32[]{:S(2)}) collective-permute-start(bf16[512,256]{1,0:T(8,128)(2,1)} %fusion.7), channel_id=1, source_target_pairs={{0,3},{1,0},{2,1},{3,2},{4,7},{5,4},{6,5},{7,6},{8,11},{9,8},{10,9... | collective-permute-start | bytes 786440 | tf_op jit(solution)/shard_map/ppermute | solution.py:33
  96.7 10.7 %collective-permute-start.20 = (bf16[512,256]{1,0:T(8,128)(2,1)}, bf16[512,256]{1,0:T(8,128)(2,1)}, u32[]{:S(2)}, u32[]{:S(2)}) collective-permute-start(bf16[512,256]{1,0:T(8,128)(2,1)} %get-tuple-element.30), channel_id=1, source_target_pairs={{0,1},{1,2},{2,3},{3,0},{4,5},{5,6},{6,7},{7,4},{8,9},{9,10},{10,1... | collective-permute-start | bytes 786440 | tf_op jit(solution)/shard_map/ppermute | solution.py:33
  96.7 10.7 %collective-permute-start.21 = (bf16[512,256]{1,0:T(8,128)(2,1)}, bf16[512,256]{1,0:T(8,128)(2,1)}, u32[]{:S(2)}, u32[]{:S(2)}) collective-permute-start(bf16[512,256]{1,0:T(8,128)(2,1)} %get-tuple-element.31), channel_id=1, source_target_pairs={{0,2},{1,3},{2,0},{3,1},{4,6},{5,7},{6,4},{7,5},{8,10},{9,11},{10,... | collective-permute-start | bytes 786440 | tf_op jit(solution)/shard_map/ppermute | solution.py:33
  109.6 10.0 %collective-permute-start.22 = (bf16[512,256]{1,0:T(8,128)(2,1)S(1)}, bf16[512,256]{1,0:T(8,128)(2,1)S(1)}, u32[]{:S(2)}, u32[]{:S(2)}) collective-permute-start(bf16[512,256]{1,0:T(8,128)(2,1)S(1)} %get-tuple-element.25), channel_id=1, source_target_pairs={{0,1},{1,2},{2,3},{3,0},{4,5},{5,6},{6,7},{7,4},{8,9},{9,10},{10,1... | collective-permute-start | bytes 786440 | tf_op jit(solution)/shard_map/ppermute | solution.py:33
  109.6 11.3 %collective-permute-start.26 = (bf16[512,256]{1,0:T(8,128)(2,1)S(1)}, bf16[512,256]{1,0:T(8,128)(2,1)S(1)}, u32[]{:S(2)}, u32[]{:S(2)}) collective-permute-start(bf16[512,256]{1,0:T(8,128)(2,1)S(1)} %get-tuple-element.25), channel_id=1, source_target_pairs={{0,2},{1,3},{2,0},{3,1},{4,6},{5,7},{6,4},{7,5},{8,10},{9,11},{10,... | collective-permute-start | bytes 786440 | tf_op jit(solution)/shard_map/ppermute | solution.py:33
  111.8 10.7 %collective-permute-start.25 = (bf16[512,256]{1,0:T(8,128)(2,1)S(1)}, bf16[512,256]{1,0:T(8,128)(2,1)S(1)}, u32[]{:S(2)}, u32[]{:S(2)}) collective-permute-start(bf16[512,256]{1,0:T(8,128)(2,1)S(1)} %get-tuple-element.25), channel_id=1, source_target_pairs={{0,3},{1,0},{2,1},{3,2},{4,7},{5,4},{6,5},{7,6},{8,11},{9,8},{10,9... | collective-permute-start | bytes 786440 | tf_op jit(solution)/shard_map/ppermute | solution.py:33
  119.7 10.5 %collective-permute-start.23 = (bf16[2,512,256]{2,1,0:T(8,128)(2,1)S(1)}, bf16[2,512,256]{2,1,0:T(8,128)(2,1)S(1)}, u32[]{:S(2)}, u32[]{:S(2)}) collective-permute-start(bf16[2,512,256]{2,1,0:T(8,128)(2,1)S(1)} %pad_maximum_fusion.3.refs_0_), channel_id=1, source_target_pairs={{0,4},{1,5},{2,6},{3,7},{4,8},{5,9},{6,10},{7,11},{8,12},{9,13},{1... | collective-permute-start | bytes 1572872 | tf_op jit(solution)/shard_map/ppermute | solution.py:38
  122.6 10.1 %collective-permute-start.27 = (bf16[2,512,256]{2,1,0:T(8,128)(2,1)S(1)}, bf16[2,512,256]{2,1,0:T(8,128)(2,1)S(1)}, u32[]{:S(2)}, u32[]{:S(2)}) collective-permute-start(bf16[2,512,256]{2,1,0:T(8,128)(2,1)S(1)} %pad_maximum_fusion.4.refs_1_), channel_id=1, source_target_pairs={{0,12},{1,13},{2,14},{3,15},{4,0},{5,1},{6,2},{7,3},{8,4},{9,5},{1... | collective-permute-start | bytes 1572872 | tf_op jit(solution)/shard_map/ppermute | solution.py:38
  123.1 16.9 %collective-permute-start.30 = (bf16[2,512,256]{2,1,0:T(8,128)(2,1)S(1)}, bf16[2,512,256]{2,1,0:T(8,128)(2,1)S(1)}, u32[]{:S(2)}, u32[]{:S(2)}) collective-permute-start(bf16[2,512,256]{2,1,0:T(8,128)(2,1)S(1)} %pad_maximum_fusion.3.refs_0_), channel_id=1, source_target_pairs={{0,12},{1,13},{2,14},{3,15},{4,0},{5,1},{6,2},{7,3},{8,4},{9,5},{1... | collective-permute-start | bytes 1572872 | tf_op jit(solution)/shard_map/ppermute | solution.py:38
  126.1 14.0 %collective-permute-start.29 = (bf16[2,512,256]{2,1,0:T(8,128)(2,1)S(1)}, bf16[2,512,256]{2,1,0:T(8,128)(2,1)S(1)}, u32[]{:S(2)}, u32[]{:S(2)}) collective-permute-start(bf16[2,512,256]{2,1,0:T(8,128)(2,1)S(1)} %pad_maximum_fusion.4.refs_1_), channel_id=1, source_target_pairs={{0,4},{1,5},{2,6},{3,7},{4,8},{5,9},{6,10},{7,11},{8,12},{9,13},{1... | collective-permute-start | bytes 1572872 | tf_op jit(solution)/shard_map/ppermute | solution.py:38
  130.1 9.9 %copy-start.4 = (bf16[2,512,256]{2,1,0:T(8,128)(2,1)}, bf16[2,512,256]{2,1,0:T(8,128)(2,1)S(1)}, u32[]{:S(2)}) copy-start(bf16[2,512,256]{2,1,0:T(8,128)(2,1)S(1)} %collective-permute-done.23.refs_0_) | copy-start | bytes 1572868
  130.1 15.5 %collective-permute-start.24 = (bf16[2,512,256]{2,1,0:T(8,128)(2,1)S(1)}, bf16[2,512,256]{2,1,0:T(8,128)(2,1)S(1)}, u32[]{:S(2)}, u32[]{:S(2)}) collective-permute-start(bf16[2,512,256]{2,1,0:T(8,128)(2,1)S(1)} %collective-permute-done.23.refs_0_), channel_id=1, source_target_pairs={{0,4},{1,5},{2,6},{3,7},{4,8},{5,9},{6,10},{7,11},{8,12},{9,13},{1... | collective-permute-start | bytes 1572872 | tf_op jit(solution)/shard_map/ppermute | solution.py:38
  132.6 7.4 %copy-start.6 = (bf16[2,512,256]{2,1,0:T(8,128)(2,1)}, bf16[2,512,256]{2,1,0:T(8,128)(2,1)S(1)}, u32[]{:S(2)}) copy-start(bf16[2,512,256]{2,1,0:T(8,128)(2,1)S(1)} %collective-permute-done.27.refs_3_) | copy-start | bytes 1572868
  132.6 13.1 %collective-permute-start.28 = (bf16[2,512,256]{2,1,0:T(8,128)(2,1)S(1)}, bf16[2,512,256]{2,1,0:T(8,128)(2,1)S(1)}, u32[]{:S(2)}, u32[]{:S(2)}) collective-permute-start(bf16[2,512,256]{2,1,0:T(8,128)(2,1)S(1)} %collective-permute-done.27.refs_3_), channel_id=1, source_target_pairs={{0,12},{1,13},{2,14},{3,15},{4,0},{5,1},{6,2},{7,3},{8,4},{9,5},{1... | collective-permute-start | bytes 1572872 | tf_op jit(solution)/shard_map/ppermute | solution.py:38
  140.0 5.6 %copy-start.8 = (bf16[2,512,256]{2,1,0:T(8,128)(2,1)}, bf16[2,512,256]{2,1,0:T(8,128)(2,1)S(1)}, u32[]{:S(2)}) copy-start(bf16[2,512,256]{2,1,0:T(8,128)(2,1)S(1)} %collective-permute-done.30.refs_2_) | copy-start | bytes 1572868
  140.1 5.6 %copy-start.10 = (bf16[2,512,256]{2,1,0:T(8,128)(2,1)}, bf16[2,512,256]{2,1,0:T(8,128)(2,1)S(1)}, u32[]{:S(2)}) copy-start(bf16[2,512,256]{2,1,0:T(8,128)(2,1)S(1)} %collective-permute-done.29.refs_1_) | copy-start | bytes 1572868
  145.7 4.0 %copy-start.12 = (bf16[2,512,256]{2,1,0:T(8,128)(2,1)}, bf16[2,512,256]{2,1,0:T(8,128)(2,1)S(1)}, u32[]{:S(2)}) copy-start(bf16[2,512,256]{2,1,0:T(8,128)(2,1)S(1)} %collective-permute-done.24.refs_0_) | copy-start | bytes 1572868
  150.6 5.2 %collective-permute-start.31 = (bf16[4,512,128]{2,1,0:T(8,128)(2,1)}, bf16[4,512,128]{2,1,0:T(8,128)(2,1)}, u32[]{:S(2)}, u32[]{:S(2)}) collective-permute-start(bf16[4,512,128]{2,1,0:T(8,128)(2,1)} %get-tuple-element.18), channel_id=1, source_target_pairs={{0,16},{1,17},{2,18},{3,19},{4,20},{5,21},{6,22},{7,23},{8,24},{9,... | collective-permute-start | bytes 1572872 | tf_op jit(solution)/shard_map/ppermute | solution.py:46
  155.8 5.4 %copy-start.5 = (bf16[2,512,256]{2,1,0:T(8,128)(2,1)S(1)}, bf16[2,512,256]{2,1,0:T(8,128)(2,1)}, u32[]{:S(2)}) copy-start(bf16[2,512,256]{2,1,0:T(8,128)(2,1)} %copy-done.4) | copy-start | bytes 1572868
  155.8 5.4 %copy-start.7 = (bf16[2,512,256]{2,1,0:T(8,128)(2,1)S(1)}, bf16[2,512,256]{2,1,0:T(8,128)(2,1)}, u32[]{:S(2)}) copy-start(bf16[2,512,256]{2,1,0:T(8,128)(2,1)} %copy-done.6) | copy-start | bytes 1572868
  155.8 5.5 %copy-start.9 = (bf16[2,512,256]{2,1,0:T(8,128)(2,1)S(1)}, bf16[2,512,256]{2,1,0:T(8,128)(2,1)}, u32[]{:S(2)}) copy-start(bf16[2,512,256]{2,1,0:T(8,128)(2,1)} %copy-done.8) | copy-start | bytes 1572868
  155.8 5.5 %copy-start.11 = (bf16[2,512,256]{2,1,0:T(8,128)(2,1)S(1)}, bf16[2,512,256]{2,1,0:T(8,128)(2,1)}, u32[]{:S(2)}) copy-start(bf16[2,512,256]{2,1,0:T(8,128)(2,1)} %copy-done.10) | copy-start | bytes 1572868
  157.1 13.6 %collective-permute-start.32 = (bf16[512,128]{1,0:T(8,128)(2,1)S(1)}, bf16[512,128]{1,0:T(8,128)(2,1)S(1)}, u32[]{:S(2)}, u32[]{:S(2)}) collective-permute-start(bf16[512,128]{1,0:T(8,128)(2,1)S(1)} %get-tuple-element.27), channel_id=1, source_target_pairs={{32,0},{33,1},{34,2},{35,3},{36,4},{37,5},{38,6},{39,7},{40,8},{41... | collective-permute-start | bytes 393224 | tf_op jit(solution)/shard_map/ppermute | solution.py:42
  158.4 12.4 %collective-permute-start.34 = (bf16[512,128]{1,0:T(8,128)(2,1)S(1)}, bf16[512,128]{1,0:T(8,128)(2,1)S(1)}, u32[]{:S(2)}, u32[]{:S(2)}) collective-permute-start(bf16[512,128]{1,0:T(8,128)(2,1)S(1)} %get-tuple-element.28), channel_id=1, source_target_pairs={{96,0},{97,1},{98,2},{99,3},{100,4},{101,5},{102,6},{103,7},{104,8... | collective-permute-start | bytes 393224 | tf_op jit(solution)/shard_map/ppermute | solution.py:42
  159.7 7.5 %copy-start.13 = (bf16[2,512,256]{2,1,0:T(8,128)(2,1)S(1)}, bf16[2,512,256]{2,1,0:T(8,128)(2,1)}, u32[]{:S(2)}) copy-start(bf16[2,512,256]{2,1,0:T(8,128)(2,1)} %copy-done.12) | copy-start | bytes 1572868
  159.8 7.5 %copy-start.15 = (bf16[2,512,256]{2,1,0:T(8,128)(2,1)S(1)}, bf16[2,512,256]{2,1,0:T(8,128)(2,1)}, u32[]{:S(2)}) copy-start(bf16[2,512,256]{2,1,0:T(8,128)(2,1)} %copy-done.14) | copy-start | bytes 1572868
  159.8 11.1 %collective-permute-start.33 = (bf16[512,128]{1,0:T(8,128)(2,1)S(1)}, bf16[512,128]{1,0:T(8,128)(2,1)S(1)}, u32[]{:S(2)}, u32[]{:S(2)}) collective-permute-start(bf16[512,128]{1,0:T(8,128)(2,1)S(1)} %get-tuple-element.29), channel_id=1, source_target_pairs={{64,0},{65,1},{66,2},{67,3},{68,4},{69,5},{70,6},{71,7},{72,8},{73... | collective-permute-start | bytes 393224 | tf_op jit(solution)/shard_map/ppermute | solution.py:42
  (10 other events, 26.2 us)

commit v2 on v0

v2 whole, which is shorter than its diff:
```python
import jax
import numpy as np
import jax.numpy as jnp
from jax import lax
from jax.experimental import pallas as pl
from jax.experimental.pallas import tpu as pltpu
from jax.sharding import PartitionSpec as P

PICKS = 16
TOK = 512
AXES = ("layer", "feat")
LONG_STEPS = (0, -1, 1, 2)
SHORT_STEPS = (0, -1, 1, 2)
BF16 = jnp.bfloat16
F32 = jnp.float32
PARAMS = pltpu.CompilerParams(vmem_limit_bytes=14 * 1024 * 1024)


def pairs_of(move):
    out = []
    for y in range(4):
        for c in range(2):
            for z in range(4):
                for x in range(4):
                    y2, c2, z2, x2 = move(y, c, z, x)
                    if 0 <= y2 < 4:
                        out.append(((y * 2 + c) * 16 + z * 4 + x, (y2 * 2 + c2) * 16 + (z2 % 4) * 4 + x2 % 4))
    return out


def short(value, step):
    move = lambda y, c, z, x: (y, c, z, x + step) if c == 0 else (y, c, z + step, x)
    return lax.ppermute(value, AXES, pairs_of(move))


def long(value, step):
    move = lambda y, c, z, x: (y, c, z + step, x) if c == 0 else (y, c, z, x + step)
    return lax.ppermute(value, AXES, pairs_of(move))


def chips_y(value, step):
    return lax.ppermute(value, AXES, pairs_of(lambda y, c, z, x: (y + step, c, z, x)))


def other_core(value):
    return lax.ppermute(value, AXES, pairs_of(lambda y, c, z, x: (y, 1 - c, z, x)))


def dot(a, b):
    return jnp.dot(a, b, preferred_element_type=F32)


def call(kernel, scalars, args, out_shape, out_specs, grid=(), specs=None, flops=0, moved=0, name="", after=(), aliases=None, scratch=()):
    specs = [VMEM_SPEC] * len(args) if specs is None else list(specs)
    used = len(args)
    args = list(args) + list(after)
    specs += [pl.BlockSpec(memory_space=pl.ANY)] * len(after)

    def body(sc, *refs):
        kernel(sc, *refs[:used], *refs[used + len(after):])

    return pl.pallas_call(
        body,
        grid_spec=pltpu.PrefetchScalarGridSpec(
            num_scalar_prefetch=1, grid=grid, in_specs=specs, out_specs=out_specs, scratch_shapes=list(scratch),
        ),
        out_shape=out_shape,
        input_output_aliases=aliases or {},
        compiler_params=PARAMS,
        cost_estimate=pl.CostEstimate(flops=1, bytes_accessed=1, transcendentals=0),
        name=name,
    )(scalars, *args)


VMEM_SPEC = pl.BlockSpec(memory_space=pltpu.VMEM)
def shape(dims, dtype):
    return jax.ShapeDtypeStruct(dims, dtype)


def columns(sc, index):
    return pl.ds(pl.multiple_of(sc[index] * 256, 256), 256)


def encode(scalars, pairs, first, weight, total, finish):
    n = len(pairs)

    def kernel(sc, *refs):
        w, rest, out = refs[n], refs[n + 1:-1], refs[-1]
        left = jnp.concatenate([refs[i][k] for i in range(n) for k in range(2)], axis=1)
        right = jnp.concatenate([w[columns(sc, first * 2 + i), :] for i in range(2 * n)], axis=0)
        acc = dot(left, right)
        if total is not None:
            acc += rest[0][...]
        if finish is None:
            out[...] = acc
        else:
            out[...] = (rest[-2][...] * (acc + rest[-1][...])).astype(BF16)

    args = [*pairs, weight] + ([] if total is None else [total]) + ([] if finish is None else list(finish))
    return call(
        kernel, scalars, args, shape((TOK, 128), F32 if finish is None else BF16), VMEM_SPEC,
        flops=n * 4 * TOK * 256 * 128, moved=n * 524288, name="encode",
    )


def assemble(scalars, mine, other):
    def kernel(sc, *refs):
        acts, acts_t = refs[-2:]
        y, c = sc[16], sc[17]
        for o in range(4):
            a, b = refs[o][...], refs[4 + o][...]
            if o == 0:
                b = jnp.where(c == 1, b, jnp.zeros_like(b))
            both = jnp.concatenate([jnp.where(c == 0, a, b), jnp.where(c == 0, b, a)], axis=1)
            at = pl.ds(pl.multiple_of(((y - o) & 3) * 256, 256), 256)
            acts[:, at] = both
            acts_t[at, :] = both.T

    return call(
        kernel, scalars, [*mine, *other], (shape((TOK, 1024), BF16), shape((1024, TOK), BF16)), (VMEM_SPEC, VMEM_SPEC),
        moved=4 * 1048576, name="assemble",
    )


def decode(scalars, acts, dec, pairs, dtypes, after=()):
    def kernel(sc, a, w, *outs):
        for i, pair in enumerate(pairs):
            for k in range(2):
                outs[i][k] = dot(a[...], w[:, columns(sc, 2 * pair + k)]).astype(dtypes[i])

    return call(
        kernel, scalars, [acts, dec], tuple(shape((2, TOK, 256), d) for d in dtypes), (VMEM_SPEC,) * len(pairs),
        name="decode", after=after,
    )


def pass_on(scalars, u_next, v_next, u_prev, v_prev, from_left, from_right, after):
    def kernel(sc, un, vn, up, vp, fl, fr, right_most, right_own, left_most, left_own):
        right_own[...] = (un[0] + fl[0].astype(F32)).astype(BF16)
        right_most[0] = (un[1] + fl[1].astype(F32)).astype(BF16)
        left_own[...] = up[0]
        left_most[0] = up[1]
        for k in range(2):
            right_most[1 + k] = vn[k]
            left_most[1 + k] = (vp[k] + fr[k].astype(F32)).astype(BF16)

    return call(
        kernel, scalars, [u_next, v_next, u_prev, v_prev, from_left, from_right],
        (shape((3, TOK, 256), BF16), shape((TOK, 256), BF16)) * 2, (VMEM_SPEC,) * 4, name="pass_on", after=after,
    )


def write_columns(sc, acts_t, pair_refs, first, out, blocks, sems):
    copies = []
    for i, ref in enumerate(pair_refs):
        for k in range(2):
            j = 2 * i + k
            blocks[j] = dot(acts_t[...], ref[k]).astype(BF16)
            copies.append(pltpu.make_async_copy(blocks.at[j], out.at[:, columns(sc, 2 * first + j)], sems.at[j]))
            copies[-1].start()
    return copies


def block_scratch(n):
    return [pltpu.VMEM((n, 1024, 256), BF16), pltpu.SemaphoreType.DMA((n,))]


def decoder_grad(scalars, acts_t, pairs, first, out, after=()):
    n = len(pairs)

    def kernel(sc, a, *refs):
        for copy in write_columns(sc, a, refs[:n], first, *refs[-3:]):
            copy.wait()

    anywhere = pl.BlockSpec(memory_space=pl.ANY)
    return call(
        kernel, scalars, [acts_t, *pairs, out], shape((1024, 4096), BF16), anywhere, specs=[VMEM_SPEC] * (n + 1) + [anywhere],
        aliases={n + 2: 0}, name="decoder_grad", after=after, scratch=block_scratch(2 * n),
    )


def middle(scalars, pairs, first, dec, total, acts_t, early):
    n, m = len(pairs), len(early)

    def kernel(sc, *refs):
        w, before, a, rest = refs[n], refs[n + 1], refs[n + 2], refs[n + 3:]
        acc, out, blocks, sems = rest[m:]
        left = jnp.concatenate([refs[i][k] for i in range(n) for k in range(2)], axis=1)
        for k in range(4):
            rows = slice(k * 256, k * 256 + 256)
            right = jnp.concatenate([w[rows, columns(sc, 2 * first + i)] for i in range(2 * n)], axis=1)
            acc[k] = before[k] + lax.dot_general(left, right, (((1,), (1,)), ((), ())), preferred_element_type=F32)
        for copy in write_columns(sc, a, rest[:m], 0, out, blocks, sems):
            copy.wait()

    return call(
        kernel, scalars, [*pairs, dec, total, acts_t, *early], (shape((4, TOK, 256), F32), shape((1024, 4096), BF16)),
        (VMEM_SPEC, pl.BlockSpec(memory_space=pl.ANY)), name="middle", scratch=block_scratch(2 * m),
    )


def code_grad(scalars, pairs, first, dec, total, last, after=()):
    n = len(pairs)

    def kernel(sc, *refs):
        w, rest = refs[n], refs[n + 1:]
        left = jnp.concatenate([refs[i][k] for i in range(n) for k in range(2)], axis=1)
        y, c = sc[16], sc[17]
        for k in range(4):
            rows = slice(k * 256, k * 256 + 256)
            right = jnp.concatenate([w[rows, columns(sc, 2 * first + i)] for i in range(2 * n)], axis=1)
            acc = lax.dot_general(left, right, (((1,), (1,)), ((), ())), preferred_element_type=F32)
            if total is not None:
                acc += rest[0][k]
            if last:
                keep, send = rest[-2:]
                even, odd = acc[:, :128], acc[:, 128:]
                keep[k] = jnp.where(c == 0, even, odd)
                send[k] = jnp.where(c == 1, even, jnp.where(y == k, jnp.zeros_like(odd), odd)).astype(BF16)
            else:
                rest[-1][k] = acc

    args = [*pairs, dec] + ([] if total is None else [total])
    if last:
        outs = (shape((4, TOK, 128), F32), shape((4, TOK, 128), BF16))
    else:
        outs = (shape((4, TOK, 256), F32),)
    return call(
        kernel, scalars, args, outs, (VMEM_SPEC,) * len(outs),
        flops=n * 4 * TOK * 1024 * 256, moved=n * 524288, name="code_grad", after=after,
    )


def hold(scalars, value, after):
    def kernel(sc, source, out):
        pass

    spec = pl.BlockSpec(memory_space=pl.ANY)
    return call(kernel, scalars, [value], shape(value.shape, value.dtype), spec, specs=[spec], name="hold", after=after, aliases={1: 0})


def pair(scalars, a, b, after=()):
    def kernel(sc, first, second, out):
        out[0] = first[...]
        out[1] = second[...]

    return call(kernel, scalars, [a, b], shape((2, TOK, 256), BF16), VMEM_SPEC, name="pair", after=after)


def flip(scalars, pairs, after):
    def kernel(sc, *refs):
        n = len(pairs)
        for i in range(n):
            for k in range(2):
                refs[n + i][k] = refs[i][k].T

    return call(
        kernel, scalars, list(pairs), tuple(shape((2, 256, TOK), BF16) for _ in pairs), (VMEM_SPEC,) * len(pairs),
        moved=len(pairs) * 1048576, name="flip", after=after,
    )


def encoder_grad(scalars, flipped, gates, sums):
    n = len(flipped)

    def kernel(sc, *refs):
        g, parts, (out, rows, sems) = refs[n], refs[n + 1:-3], refs[-3:]
        total = parts[0][...] + parts[1][...].astype(F32) + parts[2][...].astype(F32) + parts[3][...].astype(F32)
        grad = (g[...] * total).astype(BF16)
        copies = []
        for i in range(n):
            for k in range(2):
                j = 2 * i + k
                rows[j] = dot(refs[i][k], grad)
                copies.append(pltpu.make_async_copy(rows.at[j], out.at[columns(sc, j), :], sems.at[j]))
                copies[-1].start()
        for copy in copies:
            copy.wait()

    return call(
        kernel, scalars, [*flipped, gates, *sums], shape((4096, 128), F32), pl.BlockSpec(memory_space=pl.ANY),
        name="encoder_grad", scratch=[pltpu.VMEM((2 * n, 256, 128), F32), pltpu.SemaphoreType.DMA((2 * n,))],
    )


def prepare(scalars, picks, after):
    def kernel(sc, act, gates):
        lanes = lax.broadcasted_iota(jnp.int32, (TOK, 128), 1)
        hit = act[:, 0:1] == lanes
        for j in range(1, PICKS):
            hit = jnp.logical_or(hit, act[:, j:j + 1] == lanes)
        gates[...] = jnp.where(hit, 1.0, 0.0)

    return call(kernel, scalars, [picks], shape((TOK, 128), F32), VMEM_SPEC, name="prepare", after=after)


def add_up(scalars, u_own, v_own, left, right):
    def kernel(sc, u, v, a, b, *outs):
        for k in range(3):
            own = u[1] if k == 0 else v[k - 1]
            outs[k][...] = (own + a[k].astype(F32) + b[k].astype(F32)).astype(BF16)

    return call(
        kernel, scalars, [u_own, v_own, left, right], (shape((TOK, 256), BF16),) * 3, (VMEM_SPEC,) * 3, name="add_up",
    )


def finish(scalars, own, own_left, own_right, parts, bias, target):
    def kernel(sc, a, *refs):
        b, t, rebuilt, signal = refs[-4:]
        value = a[0]
        for part in refs[:-4]:
            value += part[...].astype(F32)
        value += b[...]
        rebuilt[...] = value
        signal[...] = ((value - t[...].astype(F32)) * (TOK ** -0.5)).astype(BF16)

    return call(
        kernel, scalars, [own, own_left, own_right, *parts, bias, target], (shape((TOK, 256), F32), shape((TOK, 256), BF16)), (VMEM_SPEC,) * 2,
        name="finish",
    )


def split(scalars, keep, came):
    def kernel(sc, a, b, own, *outs):
        y = sc[16]
        for o in range(4):
            k = (y - o) & 3
            total = a[k] + b[k].astype(F32)
            if o == 0:
                own[...] = total
            else:
                outs[o - 1][...] = total.astype(BF16)

    return call(
        kernel, scalars, [keep, came], (shape((TOK, 128), F32),) + (shape((TOK, 128), BF16),) * 3, (VMEM_SPEC,) * 4,
        name="split",
    )


def device_table():
    rows = np.zeros((128, 128), np.int32)
    for layer in range(8):
        for feat in range(16):
            y, c, z, x = layer // 2, layer % 2, feat // 4, feat % 4
            row = []
            for ob in LONG_STEPS:
                for oa in SHORT_STEPS:
                    dz, dx = (ob, oa) if c == 0 else (oa, ob)
                    row.append((z + dz) % 4 * 4 + (x + dx) % 4)
            row += [y, c, feat, feat // 8, feat % 8 * 16]
            rows[layer * 16 + feat, :len(row)] = row
    return rows


def local(layer_input, enc_weight, enc_bias, active, dec_weight, dec_bias, target):
    place = lax.axis_index(AXES)
    scalars = lax.dynamic_slice_in_dim(jnp.asarray(device_table()), place, 1, 0)[0]
    dec = dec_weight.reshape(1024, 4096)
    block = layer_input[0]
    r1, r2, r3 = short(block, 1), short(block, -1), short(block, 2)
    feat = lax.axis_index("feat")
    wanted = lax.dynamic_slice_in_dim(target[0], feat * 256, 256, 1)
    bias = lax.dynamic_slice_in_dim(dec_bias, feat * 256, 256, 1)
    gates = prepare(scalars, lax.dynamic_slice_in_dim(active[0], feat * PICKS, PICKS, 1), (wanted, bias))
    u = pair(scalars, block, r1, after=(gates,))
    u1, u2 = long(u, 1), long(u, -1)
    v = pair(scalars, r2, r3)
    v1, v2 = long(v, 1), long(v, -1)
    inputs = (u, v, u1, v1, u2, v2, long(u1, 1), long(v2, -1))

    early = encode(scalars, inputs[:6], 0, enc_weight[0], None, None)
    act = encode(scalars, inputs[6:], 6, enc_weight[0], early, (gates, enc_bias))

    mine = [act] + [chips_y(act, o) for o in (1, 2, 3)]
    other = [other_core(m) for m in mine]
    acts, acts_t = assemble(scalars, mine, other)

    u_opp, v_opp = decode(scalars, acts, dec, (6, 7), (BF16, BF16))
    from_left, from_right = long(u_opp, 1), long(v_opp, -1)
    sums = decode(scalars, acts, dec, (4, 5, 2, 3, 0, 1), (F32, BF16, BF16, F32, F32, F32), after=(u_opp,))
    flipped = flip(scalars, inputs, after=(sums[0],))
    right_most, right_own, left_most, left_own = pass_on(scalars, *sums[:4], from_left, from_right, after=(flipped[0],))
    left, right = long(right_most, 1), long(left_most, -1)
    own_left, own_right = long(right_own, 1), long(left_own, -1)
    to_prev, to_next, to_opp = add_up(scalars, *sums[4:], left, right)
    parts = [short(to_opp, 2), short(to_next, 1), short(to_prev, -1)]
    rebuilt, signal = finish(scalars, sums[4], own_left, own_right, parts, bias, wanted)

    r1, r2, r3 = short(signal, 1), short(signal, -1), short(signal, 2)
    u = pair(scalars, signal, r1)
    u1, u2 = long(u, 1), long(u, -1)
    v = pair(scalars, r2, r3)
    v1, v2 = long(v, 1), long(v, -1)
    code, = code_grad(scalars, [u, v], 0, dec, None, False)
    held = hold(scalars, u1, (code, u2))
    u3 = long(held, 1)
    v3 = long(hold(scalars, v2, (v1, held)), -1)
    code, dec_out = middle(scalars, [u1, v1, u2, v2], 2, dec, code, acts_t, [u, v])
    keep, send = code_grad(scalars, [u3, v3], 6, dec, code, True)
    own, *down = split(scalars, keep, other_core(send))
    back = [chips_y(part, -o) for o, part in zip((1, 2, 3), down)]
    dec_out = decoder_grad(scalars, acts_t, [u1, v1, u2, v2, u3, v3], 2, dec_out, after=(down[0],))
    enc_out = encoder_grad(scalars, flipped, gates, [own, *back])
    return rebuilt[None], dec_out.reshape(8, 1, 128, 4096), enc_out[None]


def solution(mesh):
    return jax.shard_map(
        local,
        mesh=mesh,
        in_specs=(
            P("layer", None, "feat"),
            P("layer", None, "feat"),
            P("layer", "feat"),
            P("layer", None, None),
            P(None, "layer", "feat", None),
            P("layer", None),
            P("layer", None, None),
        ),
        out_specs=(
            P("layer", None, "feat"),
            P(None, "layer", "feat", None),
            P("layer", None, "feat"),
        ),
        check_vma=False,
    )
```

time: 311 us -> 151 us (0.49)
  waiting for transfers between devices: 224 us -> 50.3 us
  starting transfers between devices: 0.16 us -> 58.7 us
  matrix products: 36.8 us -> 0 us
  Pallas kernels: 0 us -> 36.8 us
  other arithmetic: 27.9 us -> 0 us
  between operations: 13.9 us -> 1.15 us
  local copies, waits for them, and re-layouts: 8.41 us -> 3.52 us
    psum x1 -> x0, waiting for transfers between devices: 142 us -> none  [local(): summed = lax.psum(partial_value, 'feat')]
    all_gather x2 -> x0, waiting for transfers between devices: 61.7 us -> none  [the longest x1 39 us: local(): inputs = lax.all_gather(layer_input, 'feat', axis=2, tiled=True)[0]]
    ppermute x0 -> x38, starting transfers between devices: none -> 58.7 us  [the longest x18 30.6 us: long(): return lax.ppermute(value, AXES, pairs_of(move))]
    ppermute x0 -> x38, waiting for transfers between devices: none -> 50.3 us  [the longest x18 30.9 us: long(): return lax.ppermute(value, AXES, pairs_of(move))]
    dot_general x5 -> x0, matrix products: 36.8 us -> none  [the longest x1 11.4 us: local(): jnp.einsum('stf,td->sfd', masked, signal, preferred_element_type=jnp.floa...]
    pallas_call x0 -> x22, Pallas kernels: none -> 36.8 us  [call(): pl.pallas_call(body, grid_spec=pltpu.PrefetchScalarGridSpec(num_scalar_pr...]
    reduce_or x1 -> x0, other arithmetic: 22.3 us -> none  [local(): jnp.any(feature_ids[:, :, None] == local_feats[None, None, :], axis=1)]
    reduce_scatter x1 -> x0, waiting for transfers between devices: 19.4 us -> none  [local(): lax.psum_scatter(term_rows * kept_rows.astype(jnp.float32)[:, None, None]...]
  transfers between devices with their start and end apart: 4 -> 38, of which waited for: 4 -> 24; matrix products, arithmetic and copies ran while one was open for 12% -> 2% of each run, Pallas kernels for 0% -> 17%
where the time goes in v2:
time: 151 us; the launch traced here: 150 us
  starting transfers between devices  58.7 us (39%)
  waiting for transfers between devices  50.3 us (33%)
  Pallas kernels  36.8 us (24%)
  local copies, waits for them, and re-layouts  3.52 us (2%)
    pallas_call x22, Pallas kernels, call(): pl.pallas_call(body, grid_spec=pltpu.PrefetchScalarGridSpec(num_scalar_pr...  36.8 us
    ppermute x18, waiting for transfers between devices, long(): return lax.ppermute(value, AXES, pairs_of(move))  30.9 us
    ppermute x18, starting transfers between devices, long(): return lax.ppermute(value, AXES, pairs_of(move))  30.6 us
    ppermute x9, starting transfers between devices, short(): return lax.ppermute(value, AXES, pairs_of(move))  14 us
    ppermute x6, starting transfers between devices, chips_y(): lax.ppermute(value, AXES, pairs_of(lambda y, c, z, x: (y + step, c, z, x)))  13.5 us
    ppermute x9, waiting for transfers between devices, short(): return lax.ppermute(value, AXES, pairs_of(move))  10.5 us
    ppermute x6, waiting for transfers between devices, chips_y(): lax.ppermute(value, AXES, pairs_of(lambda y, c, z, x: (y + step, c, z, x)))  5.72 us
    ppermute x5, waiting for transfers between devices, other_core(): lax.ppermute(value, AXES, pairs_of(lambda y, c, z, x: (y, 1 - c, z, x)))  3.24 us
  transfers between devices with their start and end apart: 38, of which 24 were waited for; matrix products, arithmetic and copies ran while one was open for 2% of the time, Pallas kernels for 17%

profile of v2, /device:TPU:0, one launch (start us, length us, event | category | flops | bytes accessed | tf_op | source)
XLA Modules:
  0.0 150.5 jit_solution(11425222149211816308)
XLA Ops:
  0.7 1.6 %collective-permute-start = (bf16[512,256]{1,0:T(8,128)(2,1)}, bf16[512,256]{1,0:T(8,128)(2,1)S(1)}, u32[]{:S(2)}, u32[]{:S(2)}) collective-permute-start(bf16[512,256]{1,0:T(8,128)(2,1)} %bitcast.21), channel_id=1, source_target_pairs={{0,1},{1,2},{2,3},{3,0},{4,5},{5,6},{6,7},{7,4},{8,9},{9,10},{10,1... | collective-permute-start | bytes 786440 | tf_op jit(solution)/shard_map/ppermute | solution.py:33
  2.3 1.7 %collective-permute-start.3 = (bf16[512,256]{1,0:T(8,128)(2,1)}, bf16[512,256]{1,0:T(8,128)(2,1)S(1)}, u32[]{:S(2)}, u32[]{:S(2)}) collective-permute-start(bf16[512,256]{1,0:T(8,128)(2,1)} %bitcast.22), channel_id=1, source_target_pairs={{0,3},{1,0},{2,1},{3,2},{4,7},{5,4},{6,5},{7,6},{8,11},{9,8},{10,9... | collective-permute-start | bytes 786440 | tf_op jit(solution)/shard_map/ppermute | solution.py:33
  4.0 1.9 %collective-permute-start.4 = (bf16[512,256]{1,0:T(8,128)(2,1)}, bf16[512,256]{1,0:T(8,128)(2,1)S(1)}, u32[]{:S(2)}, u32[]{:S(2)}) collective-permute-start(bf16[512,256]{1,0:T(8,128)(2,1)} %bitcast.23), channel_id=1, source_target_pairs={{0,2},{1,3},{2,0},{3,1},{4,6},{5,7},{6,4},{7,5},{8,10},{9,11},{10,... | collective-permute-start | bytes 786440 | tf_op jit(solution)/shard_map/ppermute | solution.py:33
  8.4 2.1 %prepare.1.refs_2_.refs_4_.refs_8_ = f32[512,128]{1,0:T(8,128)S(1)} custom-call(s32[128]{0:T(128)S(1)} %fusion.sc, s32[512,16]{1,0:T(8,128)S(1)} %dynamic-slice_bitcast_fusion.1.refs_0_, bf16[512,256]{1,0:T(8,128)(2,1)S(1)} %dynamic-slice_bitcast_fusion.refs_1_.refs_7_, f32[1,256]{1,0:T(1,128)S(1)} %constant_dynamic-slice_fusion.refs_2_.refs_6_), custom_call_target="tpu_custom_call" | custom-call | flops 1 | bytes 1 | tf_op jit(solution)/shard_map/prepare/pallas_call | solution.py:62
  12.0 2.0 %collective-permute-start.1 = (bf16[2,512,256]{2,1,0:T(8,128)(2,1)S(1)}, bf16[2,512,256]{2,1,0:T(8,128)(2,1)S(1)}, u32[]{:S(2)}, u32[]{:S(2)}) collective-permute-start(bf16[2,512,256]{2,1,0:T(8,128)(2,1)S(1)} %pair.4.refs_0_), channel_id=1, source_target_pairs={{0,4},{1,5},{2,6},{3,7},{4,8},{5,9},{6,10},{7,11},{8,12},{9,13},{1... | collective-permute-start | bytes 1572872 | tf_op jit(solution)/shard_map/ppermute | solution.py:38
  14.6 2.5 %collective-permute-start.5 = (bf16[2,512,256]{2,1,0:T(8,128)(2,1)S(1)}, bf16[2,512,256]{2,1,0:T(8,128)(2,1)S(1)}, u32[]{:S(2)}, u32[]{:S(2)}) collective-permute-start(bf16[2,512,256]{2,1,0:T(8,128)(2,1)S(1)} %pair.5.refs_1_), channel_id=1, source_target_pairs={{0,12},{1,13},{2,14},{3,15},{4,0},{5,1},{6,2},{7,3},{8,4},{9,5},{1... | collective-permute-start | bytes 1572872 | tf_op jit(solution)/shard_map/ppermute | solution.py:38
  17.1 1.7 %collective-permute-start.8 = (bf16[2,512,256]{2,1,0:T(8,128)(2,1)S(1)}, bf16[2,512,256]{2,1,0:T(8,128)(2,1)S(1)}, u32[]{:S(2)}, u32[]{:S(2)}) collective-permute-start(bf16[2,512,256]{2,1,0:T(8,128)(2,1)S(1)} %pair.4.refs_0_), channel_id=1, source_target_pairs={{0,12},{1,13},{2,14},{3,15},{4,0},{5,1},{6,2},{7,3},{8,4},{9,5},{1... | collective-permute-start | bytes 1572872 | tf_op jit(solution)/shard_map/ppermute | solution.py:38
  19.1 4.2 %collective-permute-done.1.refs_2_ = bf16[2,512,256]{2,1,0:T(8,128)(2,1)S(1)} collective-permute-done((bf16[2,512,256]{2,1,0:T(8,128)(2,1)S(1)}, bf16[2,512,256]{2,1,0:T(8,128)(2,1)S(1)}, u32[]{:S(2)}, u32[]{:S(2)}) %collective-permute-start.1) | collective-permute-done | bytes 524320 | tf_op jit(solution)/shard_map/ppermute | solution.py:38
  23.8 3.6 %collective-permute-start.6 = (bf16[2,512,256]{2,1,0:T(8,128)(2,1)S(1)}, bf16[2,512,256]{2,1,0:T(8,128)(2,1)S(1)}, u32[]{:S(2)}, u32[]{:S(2)}) collective-permute-start(bf16[2,512,256]{2,1,0:T(8,128)(2,1)S(1)} %collective-permute-done.5.refs_5_), channel_id=1, source_target_pairs={{0,12},{1,13},{2,14},{3,15},{4,0},{5,1},{6,2},{7,3},{8,4},{9,5},{1... | collective-permute-start | bytes 1572872 | tf_op jit(solution)/shard_map/ppermute | solution.py:38
  27.5 2.0 %collective-permute-done.8.refs_4_ = bf16[2,512,256]{2,1,0:T(8,128)(2,1)S(1)} collective-permute-done((bf16[2,512,256]{2,1,0:T(8,128)(2,1)S(1)}, bf16[2,512,256]{2,1,0:T(8,128)(2,1)S(1)}, u32[]{:S(2)}, u32[]{:S(2)}) %collective-permute-start.8) | collective-permute-done | bytes 524320 | tf_op jit(solution)/shard_map/ppermute | solution.py:38
  29.5 1.5 %encode.2.refs_3_ = f32[512,128]{1,0:T(8,128)S(1)} custom-call(s32[128]{0:T(128)S(1)} %fusion.sc, bf16[2,512,256]{2,1,0:T(8,128)(2,1)S(1)} %pair.4.refs_0_, bf16[2,512,256]{2,1,0:T(8,128)(2,1)S(1)} %pair.5.refs_1_, bf16[2,512,256]{2,1,0:T(8,128)(2,1)S(1)} %collective-permute-done.1.refs_2_, bf16[2,512,256]{2,1,0:T(8,128)(2,1)S(1)} %collective-permute-done.7.refs_3_, ...), custom_call_target="tpu_custom_call" | custom-call | flops 1 | bytes 1 | tf_op jit(solution)/shard_map/encode/pallas_call | solution.py:62
  31.0 3.8 %collective-permute-done.2.refs_0_.refs_6_ = bf16[2,512,256]{2,1,0:T(8,128)(2,1)S(1)} collective-permute-done((bf16[2,512,256]{2,1,0:T(8,128)(2,1)S(1)}, bf16[2,512,256]{2,1,0:T(8,128)(2,1)S(1)}, u32[]{:S(2)}, u32[]{:S(2)}) %collective-permute-start.2) | collective-permute-done | bytes 524320 | tf_op jit(solution)/shard_map/ppermute | solution.py:38
  36.1 3.5 %collective-permute-start.9 = (bf16[512,128]{1,0:T(8,128)(2,1)S(1)}, bf16[512,128]{1,0:T(8,128)(2,1)S(1)}, u32[]{:S(2)}, u32[]{:S(2)}) collective-permute-start(bf16[512,128]{1,0:T(8,128)(2,1)S(1)} %encode.3.refs_0_), channel_id=1, source_target_pairs={{0,32},{1,33},{2,34},{3,35},{4,36},{5,37},{6,38},{7,39},{8,40},{9,... | collective-permute-start | bytes 393224 | tf_op jit(solution)/shard_map/ppermute | solution.py:42
  39.6 4.8 %collective-permute-start.10 = (bf16[512,128]{1,0:T(8,128)(2,1)S(1)}, bf16[512,128]{1,0:T(8,128)(2,1)S(1)}, u32[]{:S(2)}, u32[]{:S(2)}) collective-permute-start(bf16[512,128]{1,0:T(8,128)(2,1)S(1)} %encode.3.refs_0_), channel_id=1, source_target_pairs={{0,64},{1,65},{2,66},{3,67},{4,68},{5,69},{6,70},{7,71},{8,72},{9,... | collective-permute-start | bytes 393224 | tf_op jit(solution)/shard_map/ppermute | solution.py:42
  44.4 1.3 collective-permute-start.11
  46.9 1.3 collective-permute-done.11.refs_3_
  48.2 1.3 collective-permute-done.15.refs_7_
  50.4 1.8 %decode.2 = (bf16[2,512,256]{2,1,0:T(8,128)(2,1)S(1)}, bf16[2,512,256]{2,1,0:T(8,128)(2,1)S(1)}) custom-call(s32[128]{0:T(128)S(1)} %fusion.sc, bf16[512,1024]{1,0:T(8,128)(2,1)S(1)} %get-tuple-element.38.refs_0_, bf16[1024,4096]{1,0:T(8,128)(2,1)S(1)} %bitcast.14), custom_call_target="tpu_custom_call" | custom-call | flops 1 | bytes 1 | tf_op jit(solution)/shard_map/decode/pallas_call | solution.py:62
  52.3 2.0 %collective-permute-start.16 = (bf16[2,512,256]{2,1,0:T(8,128)(2,1)S(1)}, bf16[2,512,256]{2,1,0:T(8,128)(2,1)S(1)}, u32[]{:S(2)}, u32[]{:S(2)}) collective-permute-start(bf16[2,512,256]{2,1,0:T(8,128)(2,1)S(1)} %get-tuple-element.39.refs_2_), channel_id=1, source_target_pairs={{0,4},{1,5},{2,6},{3,7},{4,8},{5,9},{6,10},{7,11},{8,12},{9,13},{1... | collective-permute-start | bytes 1572872 | tf_op jit(solution)/shard_map/ppermute | solution.py:38
  54.3 2.0 %collective-permute-start.17 = (bf16[2,512,256]{2,1,0:T(8,128)(2,1)S(1)}, bf16[2,512,256]{2,1,0:T(8,128)(2,1)S(1)}, u32[]{:S(2)}, u32[]{:S(2)}) collective-permute-start(bf16[2,512,256]{2,1,0:T(8,128)(2,1)S(1)} %get-tuple-element.45), channel_id=1, source_target_pairs={{0,12},{1,13},{2,14},{3,15},{4,0},{5,1},{6,2},{7,3},{8,4},{9,5},{1... | collective-permute-start | bytes 1572872 | tf_op jit(solution)/shard_map/ppermute | solution.py:38
  56.3 4.0 %decode.3 = (f32[2,512,256]{2,1,0:T(8,128)S(1)}, bf16[2,512,256]{2,1,0:T(8,128)(2,1)S(1)}, bf16[2,512,256]{2,1,0:T(8,128)(2,1)S(1)}, f32[2,512,256]{2,1,0:T(8,12...) custom-call(s32[128]{0:T(128)S(1)} %fusion.sc, bf16[512,1024]{1,0:T(8,128)(2,1)S(1)} %get-tuple-element.38.refs_0_, ...), custom_call_target="tpu_custom_call" | custom-call | flops 1 | bytes 1 | tf_op jit(solution)/shard_map/decode/pallas_call | solution.py:62
  60.3 1.7 %flip.1 = (bf16[2,256,512]{2,1,0:T(8,128)(2,1)S(1)}, bf16[2,256,512]{2,1,0:T(8,128)(2,1)S(1)}, bf16[2,256,512]{2,1,0:T(8,128)(2,1)S(1)}, bf16[2,256,512]{2,1,0:T...) custom-call(s32[128]{0:T(128)S(1)} %fusion.sc, ...), custom_call_target="tpu_custom_call" | custom-call | flops 1 | bytes 1 | tf_op jit(solution)/shard_map/flip/pallas_call | solution.py:62
  64.2 1.7 %collective-permute-start.20 = (bf16[3,512,256]{2,1,0:T(8,128)(2,1)S(1)}, bf16[3,512,256]{2,1,0:T(8,128)(2,1)S(1)}, u32[]{:S(2)}, u32[]{:S(2)}) collective-permute-start(bf16[3,512,256]{2,1,0:T(8,128)(2,1)S(1)} %get-tuple-element.50), channel_id=1, source_target_pairs={{0,4},{1,5},{2,6},{3,7},{4,8},{5,9},{6,10},{7,11},{8,12},{9,13},{1... | collective-permute-start | bytes 2359304 | tf_op jit(solution)/shard_map/ppermute | solution.py:38
  65.9 1.7 %collective-permute-start.21 = (bf16[3,512,256]{2,1,0:T(8,128)(2,1)S(1)}, bf16[3,512,256]{2,1,0:T(8,128)(2,1)S(1)}, u32[]{:S(2)}, u32[]{:S(2)}) collective-permute-start(bf16[3,512,256]{2,1,0:T(8,128)(2,1)S(1)} %get-tuple-element.51), channel_id=1, source_target_pairs={{0,12},{1,13},{2,14},{3,15},{4,0},{5,1},{6,2},{7,3},{8,4},{9,5},{1... | collective-permute-start | bytes 2359304 | tf_op jit(solution)/shard_map/ppermute | solution.py:38
  68.0 2.9 %collective-permute-start.19 = (bf16[512,256]{1,0:T(8,128)(2,1)S(1)}, bf16[512,256]{1,0:T(8,128)(2,1)S(1)}, u32[]{:S(2)}, u32[]{:S(2)}) collective-permute-start(bf16[512,256]{1,0:T(8,128)(2,1)S(1)} %get-tuple-element.48), channel_id=1, source_target_pairs={{0,12},{1,13},{2,14},{3,15},{4,0},{5,1},{6,2},{7,3},{8,4},{9,5},{1... | collective-permute-start | bytes 786440 | tf_op jit(solution)/shard_map/ppermute | solution.py:38
  70.8 6.7 %collective-permute-done.20.refs_2_ = bf16[3,512,256]{2,1,0:T(8,128)(2,1)S(1)} collective-permute-done((bf16[3,512,256]{2,1,0:T(8,128)(2,1)S(1)}, bf16[3,512,256]{2,1,0:T(8,128)(2,1)S(1)}, u32[]{:S(2)}, u32[]{:S(2)}) %collective-permute-start.20) | collective-permute-done | bytes 786464 | tf_op jit(solution)/shard_map/ppermute | solution.py:38
  78.7 1.8 %collective-permute-start.22 = (bf16[512,256]{1,0:T(8,128)(2,1)S(1)}, bf16[512,256]{1,0:T(8,128)(2,1)S(1)}, u32[]{:S(2)}, u32[]{:S(2)}) collective-permute-start(bf16[512,256]{1,0:T(8,128)(2,1)S(1)} %get-tuple-element.52), channel_id=1, source_target_pairs={{0,2},{1,3},{2,0},{3,1},{4,6},{5,7},{6,4},{7,5},{8,10},{9,11},{10,... | collective-permute-start | bytes 786440 | tf_op jit(solution)/shard_map/ppermute | solution.py:33
  81.5 2.3 %collective-permute-start.24 = (bf16[512,256]{1,0:T(8,128)(2,1)S(1)}, bf16[512,256]{1,0:T(8,128)(2,1)S(1)}, u32[]{:S(2)}, u32[]{:S(2)}) collective-permute-start(bf16[512,256]{1,0:T(8,128)(2,1)S(1)} %get-tuple-element.54), channel_id=1, source_target_pairs={{0,3},{1,0},{2,1},{3,2},{4,7},{5,4},{6,5},{7,6},{8,11},{9,8},{10,9... | collective-permute-start | bytes 786440 | tf_op jit(solution)/shard_map/ppermute | solution.py:33
  83.7 3.0 %collective-permute-done.22.refs_3_ = bf16[512,256]{1,0:T(8,128)(2,1)S(1)} collective-permute-done((bf16[512,256]{1,0:T(8,128)(2,1)S(1)}, bf16[512,256]{1,0:T(8,128)(2,1)S(1)}, u32[]{:S(2)}, u32[]{:S(2)}) %collective-permute-start.22) | collective-permute-done | bytes 262176 | tf_op jit(solution)/shard_map/ppermute | solution.py:33
  86.8 2.7 %collective-permute-done.23.refs_4_ = bf16[512,256]{1,0:T(8,128)(2,1)S(1)} collective-permute-done((bf16[512,256]{1,0:T(8,128)(2,1)S(1)}, bf16[512,256]{1,0:T(8,128)(2,1)S(1)}, u32[]{:S(2)}, u32[]{:S(2)}) %collective-permute-start.23) | collective-permute-done | bytes 262176 | tf_op jit(solution)/shard_map/ppermute | solution.py:33
  89.5 1.5 %finish.1 = (f32[512,256]{1,0:T(8,128)}, bf16[512,256]{1,0:T(8,128)(2,1)S(1)}) custom-call(s32[128]{0:T(128)S(1)} %fusion.sc, f32[2,512,256]{2,1,0:T(8,128)S(1)} %get-tuple-element.40.refs_0_, bf16[512,256]{1,0:T(8,128)(2,1)S(1)} %collective-permute-done.18.refs_1_, bf16[512,256]{1,0:T(8,128)(2,1)S(1)} %collective-permute-done.19.refs_2_, ...), custom_call_target="tpu_custom_call" | custom-call | flops 1 | bytes 1 | tf_op jit(solution)/shard_map/finish/pallas_call | solution.py:62
  92.0 2.3 %collective-permute-start.27 = (bf16[512,256]{1,0:T(8,128)(2,1)S(1)}, bf16[512,256]{1,0:T(8,128)(2,1)S(1)}, u32[]{:S(2)}, u32[]{:S(2)}) collective-permute-start(bf16[512,256]{1,0:T(8,128)(2,1)S(1)} %get-tuple-element.57.refs_0_), channel_id=1, source_target_pairs={{0,3},{1,0},{2,1},{3,2},{4,7},{5,4},{6,5},{7,6},{8,11},{9,8},{10,9... | collective-permute-start | bytes 786440 | tf_op jit(solution)/shard_map/ppermute | solution.py:33
  94.7 3.8 %collective-permute-done.25.refs_1_ = bf16[512,256]{1,0:T(8,128)(2,1)S(1)} collective-permute-done((bf16[512,256]{1,0:T(8,128)(2,1)S(1)}, bf16[512,256]{1,0:T(8,128)(2,1)S(1)}, u32[]{:S(2)}, u32[]{:S(2)}) %collective-permute-start.25) | collective-permute-done | bytes 262176 | tf_op jit(solution)/shard_map/ppermute | solution.py:33
  99.2 2.4 %collective-permute-start.26 = (bf16[2,512,256]{2,1,0:T(8,128)(2,1)S(1)}, bf16[2,512,256]{2,1,0:T(8,128)(2,1)S(1)}, u32[]{:S(2)}, u32[]{:S(2)}) collective-permute-start(bf16[2,512,256]{2,1,0:T(8,128)(2,1)S(1)} %pair.6.refs_0_.refs_7_), channel_id=1, source_target_pairs={{0,4},{1,5},{2,6},{3,7},{4,8},{5,9},{6,10},{7,11},{8,12},{9,13},{1... | collective-permute-start | bytes 1572872 | tf_op jit(solution)/shard_map/ppermute | solution.py:38
  104.2 4.3 %collective-permute-start.31 = (bf16[2,512,256]{2,1,0:T(8,128)(2,1)S(1)}, bf16[2,512,256]{2,1,0:T(8,128)(2,1)S(1)}, u32[]{:S(2)}, u32[]{:S(2)}) collective-permute-start(bf16[2,512,256]{2,1,0:T(8,128)(2,1)S(1)} %pair.7.refs_1_.refs_8_), channel_id=1, source_target_pairs={{0,12},{1,13},{2,14},{3,15},{4,0},{5,1},{6,2},{7,3},{8,4},{9,5},{1... | collective-permute-start | bytes 1572872 | tf_op jit(solution)/shard_map/ppermute | solution.py:38
  108.4 1.8 %code_grad.2.refs_1_.refs_5_ = f32[4,512,256]{2,1,0:T(8,128)S(1)} custom-call(s32[128]{0:T(128)S(1)} %fusion.sc, bf16[2,512,256]{2,1,0:T(8,128)(2,1)S(1)} %pair.6.refs_0_.refs_7_, bf16[2,512,256]{2,1,0:T(8,128)(2,1)S(1)} %pair.7.refs_1_.refs_8_, bf16[1024,4096]{1,0:T(8,128)(2,1)S(1)} %bitcast.16), custom_call_target="tpu_custom_call" | custom-call | flops 1 | bytes 1 | tf_op jit(solution)/shard_map/code_grad/pallas_call | solution.py:62
  111.3 5.1 %collective-permute-done.31.refs_3_.refs_4_ = bf16[2,512,256]{2,1,0:T(8,128)(2,1)S(1)} collective-permute-done((bf16[2,512,256]{2,1,0:T(8,128)(2,1)S(1)}, bf16[2,512,256]{2,1,0:T(8,128)(2,1)S(1)}, u32[]{:S(2)}, u32[]{:S(2)}) %collective-permute-start.31) | collective-permute-done | bytes 524320 | tf_op jit(solution)/shard_map/ppermute | solution.py:38
  116.4 2.5 %collective-permute-done.29.refs_1_.refs_2_ = bf16[2,512,256]{2,1,0:T(8,128)(2,1)S(1)} collective-permute-done((bf16[2,512,256]{2,1,0:T(8,128)(2,1)S(1)}, bf16[2,512,256]{2,1,0:T(8,128)(2,1)S(1)}, u32[]{:S(2)}, u32[]{:S(2)}) %collective-permute-start.29) | collective-permute-done | bytes 524320 | tf_op jit(solution)/shard_map/ppermute | solution.py:38
  119.5 2.0 %collective-permute-start.32 = (bf16[2,512,256]{2,1,0:T(8,128)(2,1)S(1)}, bf16[2,512,256]{2,1,0:T(8,128)(2,1)S(1)}, u32[]{:S(2)}, u32[]{:S(2)}) collective-permute-start(bf16[2,512,256]{2,1,0:T(8,128)(2,1)S(1)} %hold.2.refs_2_), channel_id=1, source_target_pairs={{0,4},{1,5},{2,6},{3,7},{4,8},{5,9},{6,10},{7,11},{8,12},{9,13},{1... | collective-permute-start | bytes 1572872 | tf_op jit(solution)/shard_map/ppermute | solution.py:38
  121.5 5.1 %middle.1 = (f32[4,512,256]{2,1,0:T(8,128)S(1)}, bf16[1024,4096]{1,0:T(8,128)(2,1)}) custom-call(s32[128]{0:T(128)S(1)} %fusion.sc, bf16[2,512,256]{2,1,0:T(8,128)(2,1)S(1)} %collective-permute-done.26.refs_0_.refs_1_, bf16[2,512,256]{2,1,0:T(8,128)(2,1)S(1)} %collective-permute-done.29.refs_1_.refs_2_, ...), custom_call_target="tpu_custom_call" | custom-call | flops 1 | bytes 1 | tf_op jit(solution)/shard_map/middle/pallas_call | solution.py:62
  126.6 2.1 %collective-permute-done.33.refs_1_.refs_6_ = bf16[2,512,256]{2,1,0:T(8,128)(2,1)S(1)} collective-permute-done((bf16[2,512,256]{2,1,0:T(8,128)(2,1)S(1)}, bf16[2,512,256]{2,1,0:T(8,128)(2,1)S(1)}, u32[]{:S(2)}, u32[]{:S(2)}) %collective-permute-start.33) | collective-permute-done | bytes 524320 | tf_op jit(solution)/shard_map/ppermute | solution.py:38
  128.6 1.5 %collective-permute-done.32.refs_0_.refs_5_ = bf16[2,512,256]{2,1,0:T(8,128)(2,1)S(1)} collective-permute-done((bf16[2,512,256]{2,1,0:T(8,128)(2,1)S(1)}, bf16[2,512,256]{2,1,0:T(8,128)(2,1)S(1)}, u32[]{:S(2)}, u32[]{:S(2)}) %collective-permute-start.32) | collective-permute-done | bytes 524320 | tf_op jit(solution)/shard_map/ppermute | solution.py:38
  130.1 1.8 %code_grad.3 = (f32[4,512,128]{2,1,0:T(8,128)S(1)}, bf16[4,512,128]{2,1,0:T(8,128)(2,1)S(1)}) custom-call(s32[128]{0:T(128)S(1)} %fusion.sc, bf16[2,512,256]{2,1,0:T(8,128)(2,1)S(1)} %collective-permute-done.32.refs_0_.refs_5_, bf16[2,512,256]{2,1,0:T(8,128)(2,1)S(1)} %collective-permute-done.33.refs_1_.refs_6_, bf16[1024,4096]{1,0:T(8,128)(2,1)S(1)} %bitcast.18, ...), custom_call_target="tpu_custom_call" | custom-call | flops 1 | bytes 1 | tf_op jit(solution)/shard_map/code_grad/pallas_call | solution.py:62
  132.1 1.9 %collective-permute-done.34.refs_1_ = bf16[4,512,128]{2,1,0:T(8,128)(2,1)S(1)} collective-permute-done((bf16[4,512,128]{2,1,0:T(8,128)(2,1)S(1)}, bf16[4,512,128]{2,1,0:T(8,128)(2,1)S(1)}, u32[]{:S(2)}, u32[]{:S(2)}) %collective-permute-start.34) | collective-permute-done | bytes 524320 | tf_op jit(solution)/shard_map/ppermute | solution.py:46
  134.6 1.3 collective-permute-start.35
  138.5 5.3 %decoder_grad.1 = bf16[1024,4096]{1,0:T(8,128)(2,1)} custom-call(s32[128]{0:T(128)S(1)} %fusion.sc, bf16[1024,512]{1,0:T(8,128)(2,1)S(1)} %get-tuple-element.56.refs_6_.refs_0_, bf16[2,512,256]{2,1,0:T(8,128)(2,1)S(1)} %collective-permute-done.26.refs_0_.refs_1_, ...), custom_call_target="tpu_custom_call", output_to_operand_aliasing={{}: (8, {})} | custom-call | flops 1 | bytes 1 | tf_op jit(solution)/shard_map/decoder_grad/pallas_call | solution.py:62
  144.9 2.8 %collective-permute-done.37.refs_12_ = bf16[512,128]{1,0:T(8,128)(2,1)S(1)} collective-permute-done((bf16[512,128]{1,0:T(8,128)(2,1)S(1)}, bf16[512,128]{1,0:T(8,128)(2,1)S(1)}, u32[]{:S(2)}, u32[]{:S(2)}) %collective-permute-start.37) | collective-permute-done | bytes 131104 | tf_op jit(solution)/shard_map/ppermute | solution.py:42
  147.7 2.6 %encoder_grad.1 = f32[4096,128]{1,0:T(8,128)} custom-call(s32[128]{0:T(128)S(1)} %fusion.sc, bf16[2,256,512]{2,1,0:T(8,128)(2,1)S(1)} %get-tuple-element.46.refs_6_.refs_0_, bf16[2,256,512]{2,1,0:T(8,128)(2,1)S(1)} %get-tuple-element.63.refs_1_, bf16[2,256,512]{2,1,0:T(8,128)(2,1)S(1)} %get-tuple-element.64.refs_2_, ...), custom_call_target="tpu_custom_call" | custom-call | flops 1 | bytes 1 | tf_op jit(solution)/shard_map/encoder_grad/pallas_call | solution.py:62
  (66 shorter events, 24.3 us)
Async XLA Ops:
  0.6 6.9 %copy-start = (s32[1,512,256]{2,1,0:T(8,128)S(1)}, s32[1,512,256]{2,1,0:T(8,128)}, u32[]{:S(2)}) copy-start(s32[1,512,256]{2,1,0:T(8,128)} %param.11) | copy-start | bytes 1572868
  0.6 28.8 %copy-start.2 = (bf16[1,4096,128]{2,1,0:T(8,128)(2,1)S(1)}, bf16[1,4096,128]{2,1,0:T(8,128)(2,1)}, u32[]{:S(2)}) copy-start(bf16[1,4096,128]{2,1,0:T(8,128)(2,1)} %param.9) | copy-start | bytes 3145732
  0.7 9.8 %collective-permute-start = (bf16[512,256]{1,0:T(8,128)(2,1)}, bf16[512,256]{1,0:T(8,128)(2,1)S(1)}, u32[]{:S(2)}, u32[]{:S(2)}) collective-permute-start(bf16[512,256]{1,0:T(8,128)(2,1)} %bitcast.21), channel_id=1, source_target_pairs={{0,1},{1,2},{2,3},{3,0},{4,5},{5,6},{6,7},{7,4},{8,9},{9,10},{10,1... | collective-permute-start | bytes 786440 | tf_op jit(solution)/shard_map/ppermute | solution.py:33
  2.3 11.7 %collective-permute-start.3 = (bf16[512,256]{1,0:T(8,128)(2,1)}, bf16[512,256]{1,0:T(8,128)(2,1)S(1)}, u32[]{:S(2)}, u32[]{:S(2)}) collective-permute-start(bf16[512,256]{1,0:T(8,128)(2,1)} %bitcast.22), channel_id=1, source_target_pairs={{0,3},{1,0},{2,1},{3,2},{4,7},{5,4},{6,5},{7,6},{8,11},{9,8},{10,9... | collective-permute-start | bytes 786440 | tf_op jit(solution)/shard_map/ppermute | solution.py:33
  4.0 10.0 %collective-permute-start.4 = (bf16[512,256]{1,0:T(8,128)(2,1)}, bf16[512,256]{1,0:T(8,128)(2,1)S(1)}, u32[]{:S(2)}, u32[]{:S(2)}) collective-permute-start(bf16[512,256]{1,0:T(8,128)(2,1)} %bitcast.23), channel_id=1, source_target_pairs={{0,2},{1,3},{2,0},{3,1},{4,6},{5,7},{6,4},{7,5},{8,10},{9,11},{10,... | collective-permute-start | bytes 786440 | tf_op jit(solution)/shard_map/ppermute | solution.py:33
  6.8 28.2 %copy-start.4 = (f32[1,128]{1,0:T(1,128)S(1)}, f32[1,128]{1,0:T(1,128)}, u32[]{:S(2)}) copy-start(f32[1,128]{1,0:T(1,128)} %refs_5_.1) | copy-start | bytes 1540
  10.5 1.0 copy-start.3
  12.0 11.3 %collective-permute-start.1 = (bf16[2,512,256]{2,1,0:T(8,128)(2,1)S(1)}, bf16[2,512,256]{2,1,0:T(8,128)(2,1)S(1)}, u32[]{:S(2)}, u32[]{:S(2)}) collective-permute-start(bf16[2,512,256]{2,1,0:T(8,128)(2,1)S(1)} %pair.4.refs_0_), channel_id=1, source_target_pairs={{0,4},{1,5},{2,6},{3,7},{4,8},{5,9},{6,10},{7,11},{8,12},{9,13},{1... | collective-permute-start | bytes 1572872 | tf_op jit(solution)/shard_map/ppermute | solution.py:38
  14.0 36.5 %copy-start.1 = (bf16[8,1,128,4096]{3,2,1,0:T(8,128)(2,1)S(1)}, bf16[8,1,128,4096]{3,2,1,0:T(8,128)(2,1)}, u32[]{:S(2)}) copy-start(bf16[8,1,128,4096]{3,2,1,0:T(8,128)(2,1)} %param.12) | copy-start | bytes 25165828
  14.6 9.3 %collective-permute-start.5 = (bf16[2,512,256]{2,1,0:T(8,128)(2,1)S(1)}, bf16[2,512,256]{2,1,0:T(8,128)(2,1)S(1)}, u32[]{:S(2)}, u32[]{:S(2)}) collective-permute-start(bf16[2,512,256]{2,1,0:T(8,128)(2,1)S(1)} %pair.5.refs_1_), channel_id=1, source_target_pairs={{0,12},{1,13},{2,14},{3,15},{4,0},{5,1},{6,2},{7,3},{8,4},{9,5},{1... | collective-permute-start | bytes 1572872 | tf_op jit(solution)/shard_map/ppermute | solution.py:38
  17.1 12.4 %collective-permute-start.8 = (bf16[2,512,256]{2,1,0:T(8,128)(2,1)S(1)}, bf16[2,512,256]{2,1,0:T(8,128)(2,1)S(1)}, u32[]{:S(2)}, u32[]{:S(2)}) collective-permute-start(bf16[2,512,256]{2,1,0:T(8,128)(2,1)S(1)} %pair.4.refs_0_), channel_id=1, source_target_pairs={{0,12},{1,13},{2,14},{3,15},{4,0},{5,1},{6,2},{7,3},{8,4},{9,5},{1... | collective-permute-start | bytes 1572872 | tf_op jit(solution)/shard_map/ppermute | solution.py:38
  18.8 10.7 %collective-permute-start.7 = (bf16[2,512,256]{2,1,0:T(8,128)(2,1)S(1)}, bf16[2,512,256]{2,1,0:T(8,128)(2,1)S(1)}, u32[]{:S(2)}, u32[]{:S(2)}) collective-permute-start(bf16[2,512,256]{2,1,0:T(8,128)(2,1)S(1)} %pair.5.refs_1_), channel_id=1, source_target_pairs={{0,4},{1,5},{2,6},{3,7},{4,8},{5,9},{6,10},{7,11},{8,12},{9,13},{1... | collective-permute-start | bytes 1572872 | tf_op jit(solution)/shard_map/ppermute | solution.py:38
  23.3 11.5 %collective-permute-start.2 = (bf16[2,512,256]{2,1,0:T(8,128)(2,1)S(1)}, bf16[2,512,256]{2,1,0:T(8,128)(2,1)S(1)}, u32[]{:S(2)}, u32[]{:S(2)}) collective-permute-start(bf16[2,512,256]{2,1,0:T(8,128)(2,1)S(1)} %collective-permute-done.1.refs_2_), channel_id=1, source_target_pairs={{0,4},{1,5},{2,6},{3,7},{4,8},{5,9},{6,10},{7,11},{8,12},{9,13},{1... | collective-permute-start | bytes 1572872 | tf_op jit(solution)/shard_map/ppermute | solution.py:38
  23.8 11.2 %collective-permute-start.6 = (bf16[2,512,256]{2,1,0:T(8,128)(2,1)S(1)}, bf16[2,512,256]{2,1,0:T(8,128)(2,1)S(1)}, u32[]{:S(2)}, u32[]{:S(2)}) collective-permute-start(bf16[2,512,256]{2,1,0:T(8,128)(2,1)S(1)} %collective-permute-done.5.refs_5_), channel_id=1, source_target_pairs={{0,12},{1,13},{2,14},{3,15},{4,0},{5,1},{6,2},{7,3},{8,4},{9,5},{1... | collective-permute-start | bytes 1572872 | tf_op jit(solution)/shard_map/ppermute | solution.py:38
  36.1 9.7 %collective-permute-start.9 = (bf16[512,128]{1,0:T(8,128)(2,1)S(1)}, bf16[512,128]{1,0:T(8,128)(2,1)S(1)}, u32[]{:S(2)}, u32[]{:S(2)}) collective-permute-start(bf16[512,128]{1,0:T(8,128)(2,1)S(1)} %encode.3.refs_0_), channel_id=1, source_target_pairs={{0,32},{1,33},{2,34},{3,35},{4,36},{5,37},{6,38},{7,39},{8,40},{9,... | collective-permute-start | bytes 393224 | tf_op jit(solution)/shard_map/ppermute | solution.py:42
  39.6 7.3 %collective-permute-start.10 = (bf16[512,128]{1,0:T(8,128)(2,1)S(1)}, bf16[512,128]{1,0:T(8,128)(2,1)S(1)}, u32[]{:S(2)}, u32[]{:S(2)}) collective-permute-start(bf16[512,128]{1,0:T(8,128)(2,1)S(1)} %encode.3.refs_0_), channel_id=1, source_target_pairs={{0,64},{1,65},{2,66},{3,67},{4,68},{5,69},{6,70},{7,71},{8,72},{9,... | collective-permute-start | bytes 393224 | tf_op jit(solution)/shard_map/ppermute | solution.py:42
  44.4 3.8 %collective-permute-start.11 = (bf16[512,128]{1,0:T(8,128)(2,1)S(1)}, bf16[512,128]{1,0:T(8,128)(2,1)S(1)}, u32[]{:S(2)}, u32[]{:S(2)}) collective-permute-start(bf16[512,128]{1,0:T(8,128)(2,1)S(1)} %encode.3.refs_0_), channel_id=1, source_target_pairs={{0,96},{1,97},{2,98},{3,99},{4,100},{5,101},{6,102},{7,103},{8,104... | collective-permute-start | bytes 393224 | tf_op jit(solution)/shard_map/ppermute | solution.py:42
  45.7 2.5 %collective-permute-start.12 = (bf16[512,128]{1,0:T(8,128)(2,1)S(1)}, bf16[512,128]{1,0:T(8,128)(2,1)S(1)}, u32[]{:S(2)}, u32[]{:S(2)}) collective-permute-start(bf16[512,128]{1,0:T(8,128)(2,1)S(1)} %encode.3.refs_0_), channel_id=1, source_target_pairs={{0,16},{1,17},{2,18},{3,19},{4,20},{5,21},{6,22},{7,23},{8,24},{9,... | collective-permute-start | bytes 393224 | tf_op jit(solution)/shard_map/ppermute | solution.py:46
  45.8 2.4 %collective-permute-start.13 = (bf16[512,128]{1,0:T(8,128)(2,1)S(1)}, bf16[512,128]{1,0:T(8,128)(2,1)S(1)}, u32[]{:S(2)}, u32[]{:S(2)}) collective-permute-start(bf16[512,128]{1,0:T(8,128)(2,1)S(1)} %collective-permute-done.9.refs_1_), channel_id=1, source_target_pairs={{0,16},{1,17},{2,18},{3,19},{4,20},{5,21},{6,22},{7,23},{8,24},{9,... | collective-permute-start | bytes 393224 | tf_op jit(solution)/shard_map/ppermute | solution.py:46
  46.9 1.3 collective-permute-start.14
  48.2 1.3 collective-permute-start.15
  52.3 10.9 %collective-permute-start.16 = (bf16[2,512,256]{2,1,0:T(8,128)(2,1)S(1)}, bf16[2,512,256]{2,1,0:T(8,128)(2,1)S(1)}, u32[]{:S(2)}, u32[]{:S(2)}) collective-permute-start(bf16[2,512,256]{2,1,0:T(8,128)(2,1)S(1)} %get-tuple-element.39.refs_2_), channel_id=1, source_target_pairs={{0,4},{1,5},{2,6},{3,7},{4,8},{5,9},{6,10},{7,11},{8,12},{9,13},{1... | collective-permute-start | bytes 1572872 | tf_op jit(solution)/shard_map/ppermute | solution.py:38
  54.3 9.2 %collective-permute-start.17 = (bf16[2,512,256]{2,1,0:T(8,128)(2,1)S(1)}, bf16[2,512,256]{2,1,0:T(8,128)(2,1)S(1)}, u32[]{:S(2)}, u32[]{:S(2)}) collective-permute-start(bf16[2,512,256]{2,1,0:T(8,128)(2,1)S(1)} %get-tuple-element.45), channel_id=1, source_target_pairs={{0,12},{1,13},{2,14},{3,15},{4,0},{5,1},{6,2},{7,3},{8,4},{9,5},{1... | collective-permute-start | bytes 1572872 | tf_op jit(solution)/shard_map/ppermute | solution.py:38
  64.2 13.3 %collective-permute-start.20 = (bf16[3,512,256]{2,1,0:T(8,128)(2,1)S(1)}, bf16[3,512,256]{2,1,0:T(8,128)(2,1)S(1)}, u32[]{:S(2)}, u32[]{:S(2)}) collective-permute-start(bf16[3,512,256]{2,1,0:T(8,128)(2,1)S(1)} %get-tuple-element.50), channel_id=1, source_target_pairs={{0,4},{1,5},{2,6},{3,7},{4,8},{5,9},{6,10},{7,11},{8,12},{9,13},{1... | collective-permute-start | bytes 2359304 | tf_op jit(solution)/shard_map/ppermute | solution.py:38
  65.9 12.0 %collective-permute-start.21 = (bf16[3,512,256]{2,1,0:T(8,128)(2,1)S(1)}, bf16[3,512,256]{2,1,0:T(8,128)(2,1)S(1)}, u32[]{:S(2)}, u32[]{:S(2)}) collective-permute-start(bf16[3,512,256]{2,1,0:T(8,128)(2,1)S(1)} %get-tuple-element.51), channel_id=1, source_target_pairs={{0,12},{1,13},{2,14},{3,15},{4,0},{5,1},{6,2},{7,3},{8,4},{9,5},{1... | collective-permute-start | bytes 2359304 | tf_op jit(solution)/shard_map/ppermute | solution.py:38
  67.6 16.1 %collective-permute-start.18 = (bf16[512,256]{1,0:T(8,128)(2,1)S(1)}, bf16[512,256]{1,0:T(8,128)(2,1)S(1)}, u32[]{:S(2)}, u32[]{:S(2)}) collective-permute-start(bf16[512,256]{1,0:T(8,128)(2,1)S(1)} %get-tuple-element.47), channel_id=1, source_target_pairs={{0,4},{1,5},{2,6},{3,7},{4,8},{5,9},{6,10},{7,11},{8,12},{9,13},{1... | collective-permute-start | bytes 786440 | tf_op jit(solution)/shard_map/ppermute | solution.py:38
  68.0 15.8 %collective-permute-start.19 = (bf16[512,256]{1,0:T(8,128)(2,1)S(1)}, bf16[512,256]{1,0:T(8,128)(2,1)S(1)}, u32[]{:S(2)}, u32[]{:S(2)}) collective-permute-start(bf16[512,256]{1,0:T(8,128)(2,1)S(1)} %get-tuple-element.48), channel_id=1, source_target_pairs={{0,12},{1,13},{2,14},{3,15},{4,0},{5,1},{6,2},{7,3},{8,4},{9,5},{1... | collective-permute-start | bytes 786440 | tf_op jit(solution)/shard_map/ppermute | solution.py:38
  78.7 8.1 %collective-permute-start.22 = (bf16[512,256]{1,0:T(8,128)(2,1)S(1)}, bf16[512,256]{1,0:T(8,128)(2,1)S(1)}, u32[]{:S(2)}, u32[]{:S(2)}) collective-permute-start(bf16[512,256]{1,0:T(8,128)(2,1)S(1)} %get-tuple-element.52), channel_id=1, source_target_pairs={{0,2},{1,3},{2,0},{3,1},{4,6},{5,7},{6,4},{7,5},{8,10},{9,11},{10,... | collective-permute-start | bytes 786440 | tf_op jit(solution)/shard_map/ppermute | solution.py:33
  80.5 9.0 %collective-permute-start.23 = (bf16[512,256]{1,0:T(8,128)(2,1)S(1)}, bf16[512,256]{1,0:T(8,128)(2,1)S(1)}, u32[]{:S(2)}, u32[]{:S(2)}) collective-permute-start(bf16[512,256]{1,0:T(8,128)(2,1)S(1)} %get-tuple-element.53), channel_id=1, source_target_pairs={{0,1},{1,2},{2,3},{3,0},{4,5},{5,6},{6,7},{7,4},{8,9},{9,10},{10,1... | collective-permute-start | bytes 786440 | tf_op jit(solution)/shard_map/ppermute | solution.py:33
  81.5 8.0 %collective-permute-start.24 = (bf16[512,256]{1,0:T(8,128)(2,1)S(1)}, bf16[512,256]{1,0:T(8,128)(2,1)S(1)}, u32[]{:S(2)}, u32[]{:S(2)}) collective-permute-start(bf16[512,256]{1,0:T(8,128)(2,1)S(1)} %get-tuple-element.54), channel_id=1, source_target_pairs={{0,3},{1,0},{2,1},{3,2},{4,7},{5,4},{6,5},{7,6},{8,11},{9,8},{10,9... | collective-permute-start | bytes 786440 | tf_op jit(solution)/shard_map/ppermute | solution.py:33
  91.0 7.6 %collective-permute-start.25 = (bf16[512,256]{1,0:T(8,128)(2,1)S(1)}, bf16[512,256]{1,0:T(8,128)(2,1)S(1)}, u32[]{:S(2)}, u32[]{:S(2)}) collective-permute-start(bf16[512,256]{1,0:T(8,128)(2,1)S(1)} %get-tuple-element.57.refs_0_), channel_id=1, source_target_pairs={{0,1},{1,2},{2,3},{3,0},{4,5},{5,6},{6,7},{7,4},{8,9},{9,10},{10,1... | collective-permute-start | bytes 786440 | tf_op jit(solution)/shard_map/ppermute | solution.py:33
  92.0 10.7 %collective-permute-start.27 = (bf16[512,256]{1,0:T(8,128)(2,1)S(1)}, bf16[512,256]{1,0:T(8,128)(2,1)S(1)}, u32[]{:S(2)}, u32[]{:S(2)}) collective-permute-start(bf16[512,256]{1,0:T(8,128)(2,1)S(1)} %get-tuple-element.57.refs_0_), channel_id=1, source_target_pairs={{0,3},{1,0},{2,1},{3,2},{4,7},{5,4},{6,5},{7,6},{8,11},{9,8},{10,9... | collective-permute-start | bytes 786440 | tf_op jit(solution)/shard_map/ppermute | solution.py:33
  94.2 9.4 %collective-permute-start.28 = (bf16[512,256]{1,0:T(8,128)(2,1)S(1)}, bf16[512,256]{1,0:T(8,128)(2,1)S(1)}, u32[]{:S(2)}, u32[]{:S(2)}) collective-permute-start(bf16[512,256]{1,0:T(8,128)(2,1)S(1)} %get-tuple-element.57.refs_0_), channel_id=1, source_target_pairs={{0,2},{1,3},{2,0},{3,1},{4,6},{5,7},{6,4},{7,5},{8,10},{9,11},{10,... | collective-permute-start | bytes 786440 | tf_op jit(solution)/shard_map/ppermute | solution.py:33
  99.2 11.1 %collective-permute-start.26 = (bf16[2,512,256]{2,1,0:T(8,128)(2,1)S(1)}, bf16[2,512,256]{2,1,0:T(8,128)(2,1)S(1)}, u32[]{:S(2)}, u32[]{:S(2)}) collective-permute-start(bf16[2,512,256]{2,1,0:T(8,128)(2,1)S(1)} %pair.6.refs_0_.refs_7_), channel_id=1, source_target_pairs={{0,4},{1,5},{2,6},{3,7},{4,8},{5,9},{6,10},{7,11},{8,12},{9,13},{1... | collective-permute-start | bytes 1572872 | tf_op jit(solution)/shard_map/ppermute | solution.py:38
  101.5 9.2 %collective-permute-start.30 = (bf16[2,512,256]{2,1,0:T(8,128)(2,1)S(1)}, bf16[2,512,256]{2,1,0:T(8,128)(2,1)S(1)}, u32[]{:S(2)}, u32[]{:S(2)}) collective-permute-start(bf16[2,512,256]{2,1,0:T(8,128)(2,1)S(1)} %pair.6.refs_0_.refs_7_), channel_id=1, source_target_pairs={{0,12},{1,13},{2,14},{3,15},{4,0},{5,1},{6,2},{7,3},{8,4},{9,5},{1... | collective-permute-start | bytes 1572872 | tf_op jit(solution)/shard_map/ppermute | solution.py:38
  104.2 12.2 %collective-permute-start.31 = (bf16[2,512,256]{2,1,0:T(8,128)(2,1)S(1)}, bf16[2,512,256]{2,1,0:T(8,128)(2,1)S(1)}, u32[]{:S(2)}, u32[]{:S(2)}) collective-permute-start(bf16[2,512,256]{2,1,0:T(8,128)(2,1)S(1)} %pair.7.refs_1_.refs_8_), channel_id=1, source_target_pairs={{0,12},{1,13},{2,14},{3,15},{4,0},{5,1},{6,2},{7,3},{8,4},{9,5},{1... | collective-permute-start | bytes 1572872 | tf_op jit(solution)/shard_map/ppermute | solution.py:38
  108.4 10.4 %collective-permute-start.29 = (bf16[2,512,256]{2,1,0:T(8,128)(2,1)S(1)}, bf16[2,512,256]{2,1,0:T(8,128)(2,1)S(1)}, u32[]{:S(2)}, u32[]{:S(2)}) collective-permute-start(bf16[2,512,256]{2,1,0:T(8,128)(2,1)S(1)} %pair.7.refs_1_.refs_8_), channel_id=1, source_target_pairs={{0,4},{1,5},{2,6},{3,7},{4,8},{5,9},{6,10},{7,11},{8,12},{9,13},{1... | collective-permute-start | bytes 1572872 | tf_op jit(solution)/shard_map/ppermute | solution.py:38
  119.4 9.3 %collective-permute-start.33 = (bf16[2,512,256]{2,1,0:T(8,128)(2,1)S(1)}, bf16[2,512,256]{2,1,0:T(8,128)(2,1)S(1)}, u32[]{:S(2)}, u32[]{:S(2)}) collective-permute-start(bf16[2,512,256]{2,1,0:T(8,128)(2,1)S(1)} %hold.3), channel_id=1, source_target_pairs={{0,12},{1,13},{2,14},{3,15},{4,0},{5,1},{6,2},{7,3},{8,4},{9,5},{1... | collective-permute-start | bytes 1572872 | tf_op jit(solution)/shard_map/ppermute | solution.py:38
  119.5 10.6 %collective-permute-start.32 = (bf16[2,512,256]{2,1,0:T(8,128)(2,1)S(1)}, bf16[2,512,256]{2,1,0:T(8,128)(2,1)S(1)}, u32[]{:S(2)}, u32[]{:S(2)}) collective-permute-start(bf16[2,512,256]{2,1,0:T(8,128)(2,1)S(1)} %hold.2.refs_2_), channel_id=1, source_target_pairs={{0,4},{1,5},{2,6},{3,7},{4,8},{5,9},{6,10},{7,11},{8,12},{9,13},{1... | collective-permute-start | bytes 1572872 | tf_op jit(solution)/shard_map/ppermute | solution.py:38
  132.0 2.0 %collective-permute-start.34 = (bf16[4,512,128]{2,1,0:T(8,128)(2,1)S(1)}, bf16[4,512,128]{2,1,0:T(8,128)(2,1)S(1)}, u32[]{:S(2)}, u32[]{:S(2)}) collective-permute-start(bf16[4,512,128]{2,1,0:T(8,128)(2,1)S(1)} %get-tuple-element.61), channel_id=1, source_target_pairs={{0,16},{1,17},{2,18},{3,19},{4,20},{5,21},{6,22},{7,23},{8,24},{9,... | collective-permute-start | bytes 1572872 | tf_op jit(solution)/shard_map/ppermute | solution.py:46
  134.6 9.2 %collective-permute-start.35 = (bf16[512,128]{1,0:T(8,128)(2,1)S(1)}, bf16[512,128]{1,0:T(8,128)(2,1)S(1)}, u32[]{:S(2)}, u32[]{:S(2)}) collective-permute-start(bf16[512,128]{1,0:T(8,128)(2,1)S(1)} %get-tuple-element.62.refs_8_), channel_id=1, source_target_pairs={{32,0},{33,1},{34,2},{35,3},{36,4},{37,5},{38,6},{39,7},{40,8},{41... | collective-permute-start | bytes 393224 | tf_op jit(solution)/shard_map/ppermute | solution.py:42
  135.9 8.9 %collective-permute-start.36 = (bf16[512,128]{1,0:T(8,128)(2,1)S(1)}, bf16[512,128]{1,0:T(8,128)(2,1)S(1)}, u32[]{:S(2)}, u32[]{:S(2)}) collective-permute-start(bf16[512,128]{1,0:T(8,128)(2,1)S(1)} %get-tuple-element.71), channel_id=1, source_target_pairs={{64,0},{65,1},{66,2},{67,3},{68,4},{69,5},{70,6},{71,7},{72,8},{73... | collective-permute-start | bytes 393224 | tf_op jit(solution)/shard_map/ppermute | solution.py:42
  137.2 10.4 %collective-permute-start.37 = (bf16[512,128]{1,0:T(8,128)(2,1)S(1)}, bf16[512,128]{1,0:T(8,128)(2,1)S(1)}, u32[]{:S(2)}, u32[]{:S(2)}) collective-permute-start(bf16[512,128]{1,0:T(8,128)(2,1)S(1)} %get-tuple-element.72), channel_id=1, source_target_pairs={{96,0},{97,1},{98,2},{99,3},{100,4},{101,5},{102,6},{103,7},{104,8... | collective-permute-start | bytes 393224 | tf_op jit(solution)/shard_map/ppermute | solution.py:42

commit v3 on v2

--- a/solution.py
+++ b/solution.py
@@ -56,20 +56,23 @@
     args = list(args) + list(after)
     specs += [pl.BlockSpec(memory_space=pl.ANY)] * len(after)
 
-    def body(sc, *refs):
+    lead = [] if scalars is None else [scalars]
+
+    def body(*refs):
+        sc, refs = (refs[0], refs[1:]) if lead else (None, refs)
         kernel(sc, *refs[:used], *refs[used + len(after):])
 
     return pl.pallas_call(
         body,
         grid_spec=pltpu.PrefetchScalarGridSpec(
-            num_scalar_prefetch=1, grid=grid, in_specs=specs, out_specs=out_specs, scratch_shapes=list(scratch),
+            num_scalar_prefetch=len(lead), grid=grid, in_specs=specs, out_specs=out_specs, scratch_shapes=list(scratch),
         ),
         out_shape=out_shape,
         input_output_aliases=aliases or {},
         compiler_params=PARAMS,
         cost_estimate=pl.CostEstimate(flops=1, bytes_accessed=1, transcendentals=0),
         name=name,
-    )(scalars, *args)
+    )(*lead, *args)
 
 
 VMEM_SPEC = pl.BlockSpec(memory_space=pltpu.VMEM)
@@ -145,8 +148,8 @@
             left_most[1 + k] = (vp[k] + fr[k].astype(F32)).astype(BF16)
 
     return call(
-        kernel, scalars, [u_next, v_next, u_prev, v_prev, from_left, from_right],
-        (shape((3, TOK, 256), BF16), shape((TOK, 256), BF16)) * 2, (VMEM_SPEC,) * 4, name="pass_on", after=after,
+        kernel, None, [u_next, v_next, u_prev, v_prev, from_left, from_right],
+        (shape((3, TOK, 256), BF16), shape((TOK, 256), BF16)) * 2, (VMEM_SPEC,) * 4, name="pass_on", after=(scalars, *after),
     )
 
 
@@ -179,23 +182,29 @@
     )
 
 
-def middle(scalars, pairs, first, dec, total, acts_t, early):
+def middle(scalars, pairs, first, dec, total, acts_t, early, value):
     n, m = len(pairs), len(early)
 
     def kernel(sc, *refs):
-        w, before, a, rest = refs[n], refs[n + 1], refs[n + 2], refs[n + 3:]
-        acc, out, blocks, sems = rest[m:]
+        w, before, a, val, rest = *refs[n:n + 4], refs[n + 4:]
+        acc, out, rebuilt, blocks, sems, sem = rest[m:]
+        copy = pltpu.make_async_copy(val, rebuilt, sem)
+        copy.start()
         left = jnp.concatenate([refs[i][k] for i in range(n) for k in range(2)], axis=1)
         for k in range(4):
             rows = slice(k * 256, k * 256 + 256)
             right = jnp.concatenate([w[rows, columns(sc, 2 * first + i)] for i in range(2 * n)], axis=1)
             acc[k] = before[k] + lax.dot_general(left, right, (((1,), (1,)), ((), ())), preferred_element_type=F32)
-        for copy in write_columns(sc, a, rest[:m], 0, out, blocks, sems):
-            copy.wait()
-
-    return call(
-        kernel, scalars, [*pairs, dec, total, acts_t, *early], (shape((4, TOK, 256), F32), shape((1024, 4096), BF16)),
-        (VMEM_SPEC, pl.BlockSpec(memory_space=pl.ANY)), name="middle", scratch=block_scratch(2 * m),
+        copies = write_columns(sc, a, rest[:m], 0, out, blocks, sems)
+        copy.wait()
+        for copy_out in copies:
+            copy_out.wait()
+
+    anywhere = pl.BlockSpec(memory_space=pl.ANY)
+    return call(
+        kernel, scalars, [*pairs, dec, total, acts_t, value, *early],
+        (shape((4, TOK, 256), F32), shape((1024, 4096), BF16), shape((TOK, 256), F32)),
+        (VMEM_SPEC, anywhere, anywhere), name="middle", scratch=block_scratch(2 * m) + [pltpu.SemaphoreType.DMA],
     )
 
 
@@ -231,20 +240,17 @@
     )
 
 
-def hold(scalars, value, after):
-    def kernel(sc, source, out):
-        pass
-
-    spec = pl.BlockSpec(memory_space=pl.ANY)
-    return call(kernel, scalars, [value], shape(value.shape, value.dtype), spec, specs=[spec], name="hold", after=after, aliases={1: 0})
-
-
 def pair(scalars, a, b, after=()):
-    def kernel(sc, first, second, out):
-        out[0] = first[...]
+    def kernel(sc, first, second, out, sem):
+        copy = pltpu.make_async_copy(first, out.at[0], sem)
+        copy.start()
         out[1] = second[...]
-
-    return call(kernel, scalars, [a, b], shape((2, TOK, 256), BF16), VMEM_SPEC, name="pair", after=after)
+        copy.wait()
+
+    return call(
+        kernel, None, [a, b], shape((2, TOK, 256), BF16), VMEM_SPEC, specs=[pl.BlockSpec(memory_space=pl.ANY), VMEM_SPEC],
+        name="pair", after=(scalars, *after), scratch=[pltpu.SemaphoreType.DMA],
+    )
 
 
 def flip(scalars, pairs, after):
@@ -255,8 +261,8 @@
                 refs[n + i][k] = refs[i][k].T
 
     return call(
-        kernel, scalars, list(pairs), tuple(shape((2, 256, TOK), BF16) for _ in pairs), (VMEM_SPEC,) * len(pairs),
-        moved=len(pairs) * 1048576, name="flip", after=after,
+        kernel, None, list(pairs), tuple(shape((2, 256, TOK), BF16) for _ in pairs), (VMEM_SPEC,) * len(pairs),
+        moved=len(pairs) * 1048576, name="flip", after=(scalars, *after),
     )
 
 
@@ -269,21 +275,21 @@
         grad = (g[...] * total).astype(BF16)
         copies = []
         for i in range(n):
+            rows[i] = dot(refs[i][...].reshape(512, TOK), grad)
             for k in range(2):
                 j = 2 * i + k
-                rows[j] = dot(refs[i][k], grad)
-                copies.append(pltpu.make_async_copy(rows.at[j], out.at[columns(sc, j), :], sems.at[j]))
+                copies.append(pltpu.make_async_copy(rows.at[i, k * 256:k * 256 + 256], out.at[columns(sc, j), :], sems.at[j]))
                 copies[-1].start()
         for copy in copies:
             copy.wait()
 
     return call(
         kernel, scalars, [*flipped, gates, *sums], shape((4096, 128), F32), pl.BlockSpec(memory_space=pl.ANY),
-        name="encoder_grad", scratch=[pltpu.VMEM((2 * n, 256, 128), F32), pltpu.SemaphoreType.DMA((2 * n,))],
-    )
-
-
-def prepare(scalars, picks, after):
+        name="encoder_grad", scratch=[pltpu.VMEM((n, 512, 128), F32), pltpu.SemaphoreType.DMA((2 * n,))],
+    )
+
+
+def prepare(scalars, picks):
     def kernel(sc, act, gates):
         lanes = lax.broadcasted_iota(jnp.int32, (TOK, 128), 1)
         hit = act[:, 0:1] == lanes
@@ -291,7 +297,7 @@
             hit = jnp.logical_or(hit, act[:, j:j + 1] == lanes)
         gates[...] = jnp.where(hit, 1.0, 0.0)
 
-    return call(kernel, scalars, [picks], shape((TOK, 128), F32), VMEM_SPEC, name="prepare", after=after)
+    return call(kernel, None, [picks], shape((TOK, 128), F32), VMEM_SPEC, name="prepare", after=(scalars,))
 
 
 def add_up(scalars, u_own, v_own, left, right):
@@ -301,7 +307,7 @@
             outs[k][...] = (own + a[k].astype(F32) + b[k].astype(F32)).astype(BF16)
 
     return call(
-        kernel, scalars, [u_own, v_own, left, right], (shape((TOK, 256), BF16),) * 3, (VMEM_SPEC,) * 3, name="add_up",
+        kernel, None, [u_own, v_own, left, right], (shape((TOK, 256), BF16),) * 3, (VMEM_SPEC,) * 3, name="add_up", after=(scalars,),
     )
 
 
@@ -316,8 +322,8 @@
         signal[...] = ((value - t[...].astype(F32)) * (TOK ** -0.5)).astype(BF16)
 
     return call(
-        kernel, scalars, [own, own_left, own_right, *parts, bias, target], (shape((TOK, 256), F32), shape((TOK, 256), BF16)), (VMEM_SPEC,) * 2,
-        name="finish",
+        kernel, None, [own, own_left, own_right, *parts, bias, target], (shape((TOK, 256), F32), shape((TOK, 256), BF16)), (VMEM_SPEC,) * 2,
+        name="finish", after=(scalars,),
     )
 
 
@@ -362,8 +368,9 @@
     feat = lax.axis_index("feat")
     wanted = lax.dynamic_slice_in_dim(target[0], feat * 256, 256, 1)
     bias = lax.dynamic_slice_in_dim(dec_bias, feat * 256, 256, 1)
-    gates = prepare(scalars, lax.dynamic_slice_in_dim(active[0], feat * PICKS, PICKS, 1), (wanted, bias))
-    u = pair(scalars, block, r1, after=(gates,))
+    picks = lax.dynamic_slice_in_dim(active[0], feat * PICKS, PICKS, 1)
+    u = pair(scalars, block, r1, after=(wanted, bias, picks))
+    gates = prepare(scalars, picks)
     u1, u2 = long(u, 1), long(u, -1)
     v = pair(scalars, r2, r3)
     v1, v2 = long(v, 1), long(v, -1)
@@ -385,18 +392,16 @@
     own_left, own_right = long(right_own, 1), long(left_own, -1)
     to_prev, to_next, to_opp = add_up(scalars, *sums[4:], left, right)
     parts = [short(to_opp, 2), short(to_next, 1), short(to_prev, -1)]
-    rebuilt, signal = finish(scalars, sums[4], own_left, own_right, parts, bias, wanted)
+    value, signal = finish(scalars, sums[4], own_left, own_right, parts, bias, wanted)
 
     r1, r2, r3 = short(signal, 1), short(signal, -1), short(signal, 2)
     u = pair(scalars, signal, r1)
     u1, u2 = long(u, 1), long(u, -1)
     v = pair(scalars, r2, r3)
     v1, v2 = long(v, 1), long(v, -1)
+    u3, v3 = long(u1, 1), long(v2, -1)
     code, = code_grad(scalars, [u, v], 0, dec, None, False)
-    held = hold(scalars, u1, (code, u2))
-    u3 = long(held, 1)
-    v3 = long(hold(scalars, v2, (v1, held)), -1)
-    code, dec_out = middle(scalars, [u1, v1, u2, v2], 2, dec, code, acts_t, [u, v])
+    code, dec_out, rebuilt = middle(scalars, [u1, v1, u2, v2], 2, dec, code, acts_t, [u, v], value)
     keep, send = code_grad(scalars, [u3, v3], 6, dec, code, True)
     own, *down = split(scalars, keep, other_core(send))
     back = [chips_y(part, -o) for o, part in zip((1, 2, 3), down)]

time: 151 us -> 144 us (0.954)
  Pallas kernels: 36.8 us -> 30.3 us
  starting transfers between devices: 58.7 us -> 63.6 us
  waiting for transfers between devices: 50.3 us -> 45.4 us
    ppermute x18, waiting for transfers between devices: 30.9 us -> 23.4 us  [long(): return lax.ppermute(value, AXES, pairs_of(move))]
    pallas_call x22 -> x20, Pallas kernels: 36.8 us -> 30.3 us  [call(): pl.pallas_call(body, grid_spec=pltpu.PrefetchScalarGridSpec(num_scalar_pr...]
    ppermute x18, starting transfers between devices: 30.6 us -> 35.2 us  [long(): return lax.ppermute(value, AXES, pairs_of(move))]
    ppermute x9, waiting for transfers between devices: 10.5 us -> 13.1 us  [short(): return lax.ppermute(value, AXES, pairs_of(move))]
  transfers between devices with their start and end apart: 38 -> 38, of which waited for: 24 -> 23; matrix products, arithmetic and copies ran while one was open for 2% -> 2% of each run, Pallas kernels for 17% -> 14%
where the time goes in v3:
time: 144 us
  starting transfers between devices  63.6 us (44%)
  waiting for transfers between devices  45.4 us (32%)
  Pallas kernels  30.3 us (21%)
  local copies, waits for them, and re-layouts  3.45 us (2%)
    ppermute x18, starting transfers between devices, long(): return lax.ppermute(value, AXES, pairs_of(move))  35.2 us
    pallas_call x20, Pallas kernels, call(): pl.pallas_call(body, grid_spec=pltpu.PrefetchScalarGridSpec(num_scalar_pr...  30.3 us
    ppermute x18, waiting for transfers between devices, long(): return lax.ppermute(value, AXES, pairs_of(move))  23.4 us
    ppermute x9, starting transfers between devices, short(): return lax.ppermute(value, AXES, pairs_of(move))  14.3 us
    ppermute x6, starting transfers between devices, chips_y(): lax.ppermute(value, AXES, pairs_of(lambda y, c, z, x: (y + step, c, z, x)))  13.5 us
    ppermute x9, waiting for transfers between devices, short(): return lax.ppermute(value, AXES, pairs_of(move))  13.1 us
    ppermute x6, waiting for transfers between devices, chips_y(): lax.ppermute(value, AXES, pairs_of(lambda y, c, z, x: (y + step, c, z, x)))  5.72 us
    ppermute x5, waiting for transfers between devices, other_core(): lax.ppermute(value, AXES, pairs_of(lambda y, c, z, x: (y, 1 - c, z, x)))  3.24 us
  transfers between devices with their start and end apart: 38, of which 23 were waited for; matrix products, arithmetic and copies ran while one was open for 2% of the time, Pallas kernels for 14%

profile of v3, /device:TPU:0, one launch (start us, length us, event | category | flops | bytes accessed | tf_op | source)
XLA Modules:
  0.0 143.9 jit_solution(18417804162689760910)
XLA Ops:
  0.7 1.6 %collective-permute-start = (bf16[512,256]{1,0:T(8,128)(2,1)}, bf16[512,256]{1,0:T(8,128)(2,1)S(1)}, u32[]{:S(2)}, u32[]{:S(2)}) collective-permute-start(bf16[512,256]{1,0:T(8,128)(2,1)} %bitcast.21), channel_id=1, source_target_pairs={{0,1},{1,2},{2,3},{3,0},{4,5},{5,6},{6,7},{7,4},{8,9},{9,10},{10,1... | collective-permute-start | bytes 786440 | tf_op jit(solution)/shard_map/ppermute | solution.py:33
  2.3 1.7 %collective-permute-start.3 = (bf16[512,256]{1,0:T(8,128)(2,1)}, bf16[512,256]{1,0:T(8,128)(2,1)S(1)}, u32[]{:S(2)}, u32[]{:S(2)}) collective-permute-start(bf16[512,256]{1,0:T(8,128)(2,1)} %bitcast.22), channel_id=1, source_target_pairs={{0,3},{1,0},{2,1},{3,2},{4,7},{5,4},{6,5},{7,6},{8,11},{9,8},{10,9... | collective-permute-start | bytes 786440 | tf_op jit(solution)/shard_map/ppermute | solution.py:33
  4.0 1.9 %collective-permute-start.4 = (bf16[512,256]{1,0:T(8,128)(2,1)}, bf16[512,256]{1,0:T(8,128)(2,1)S(1)}, u32[]{:S(2)}, u32[]{:S(2)}) collective-permute-start(bf16[512,256]{1,0:T(8,128)(2,1)} %bitcast.23), channel_id=1, source_target_pairs={{0,2},{1,3},{2,0},{3,1},{4,6},{5,7},{6,4},{7,5},{8,10},{9,11},{10,... | collective-permute-start | bytes 786440 | tf_op jit(solution)/shard_map/ppermute | solution.py:33
  9.5 2.1 %collective-permute-start.1 = (bf16[2,512,256]{2,1,0:T(8,128)(2,1)S(1)}, bf16[2,512,256]{2,1,0:T(8,128)(2,1)S(1)}, u32[]{:S(2)}, u32[]{:S(2)}) collective-permute-start(bf16[2,512,256]{2,1,0:T(8,128)(2,1)S(1)} %pair.4.refs_1_.refs_0_), channel_id=1, source_target_pairs={{0,4},{1,5},{2,6},{3,7},{4,8},{5,9},{6,10},{7,11},{8,12},{9,13},{1... | collective-permute-start | bytes 1572872 | tf_op jit(solution)/shard_map/ppermute | solution.py:38
  12.4 4.2 %collective-permute-start.5 = (bf16[2,512,256]{2,1,0:T(8,128)(2,1)S(1)}, bf16[2,512,256]{2,1,0:T(8,128)(2,1)S(1)}, u32[]{:S(2)}, u32[]{:S(2)}) collective-permute-start(bf16[2,512,256]{2,1,0:T(8,128)(2,1)S(1)} %pair.5.refs_2_.refs_1_), channel_id=1, source_target_pairs={{0,12},{1,13},{2,14},{3,15},{4,0},{5,1},{6,2},{7,3},{8,4},{9,5},{1... | collective-permute-start | bytes 1572872 | tf_op jit(solution)/shard_map/ppermute | solution.py:38
  17.1 1.6 %collective-permute-start.7 = (bf16[2,512,256]{2,1,0:T(8,128)(2,1)S(1)}, bf16[2,512,256]{2,1,0:T(8,128)(2,1)S(1)}, u32[]{:S(2)}, u32[]{:S(2)}) collective-permute-start(bf16[2,512,256]{2,1,0:T(8,128)(2,1)S(1)} %pair.5.refs_2_.refs_1_), channel_id=1, source_target_pairs={{0,4},{1,5},{2,6},{3,7},{4,8},{5,9},{6,10},{7,11},{8,12},{9,13},{1... | collective-permute-start | bytes 1572872 | tf_op jit(solution)/shard_map/ppermute | solution.py:38
  18.7 2.2 %collective-permute-done.1.refs_3_.refs_2_ = bf16[2,512,256]{2,1,0:T(8,128)(2,1)S(1)} collective-permute-done((bf16[2,512,256]{2,1,0:T(8,128)(2,1)S(1)}, bf16[2,512,256]{2,1,0:T(8,128)(2,1)S(1)}, u32[]{:S(2)}, u32[]{:S(2)}) %collective-permute-start.1) | collective-permute-done | bytes 524320 | tf_op jit(solution)/shard_map/ppermute | solution.py:38
  20.9 2.5 %collective-permute-done.5.refs_6_.refs_5_ = bf16[2,512,256]{2,1,0:T(8,128)(2,1)S(1)} collective-permute-done((bf16[2,512,256]{2,1,0:T(8,128)(2,1)S(1)}, bf16[2,512,256]{2,1,0:T(8,128)(2,1)S(1)}, u32[]{:S(2)}, u32[]{:S(2)}) %collective-permute-start.5) | collective-permute-done | bytes 524320 | tf_op jit(solution)/shard_map/ppermute | solution.py:38
  23.4 3.7 %collective-permute-start.6 = (bf16[2,512,256]{2,1,0:T(8,128)(2,1)S(1)}, bf16[2,512,256]{2,1,0:T(8,128)(2,1)S(1)}, u32[]{:S(2)}, u32[]{:S(2)}) collective-permute-start(bf16[2,512,256]{2,1,0:T(8,128)(2,1)S(1)} %collective-permute-done.5.refs_6_.refs_5_), channel_id=1, source_target_pairs={{0,12},{1,13},{2,14},{3,15},{4,0},{5,1},{6,2},{7,3},{8,4},{9,5},{1... | collective-permute-start | bytes 1572872 | tf_op jit(solution)/shard_map/ppermute | solution.py:38
  27.1 1.5 %prepare.1.refs_5_.refs_9_ = f32[512,128]{1,0:T(8,128)S(1)} custom-call(s32[512,16]{1,0:T(8,128)S(1)} %dynamic-slice_bitcast_fusion.refs_5_.refs_0_, s32[128]{0:T(128)S(1)} %fusion.refs_2_.refs_0_.refs_1_.refs_8_.refs_6_.refs_4_), custom_call_target="tpu_custom_call" | custom-call | flops 1 | bytes 1 | tf_op jit(solution)/shard_map/prepare/pallas_call | solution.py:65
  29.0 1.5 %encode.2.refs_4_ = f32[512,128]{1,0:T(8,128)S(1)} custom-call(s32[128]{0:T(128)S(1)} %fusion.refs_2_.refs_0_.refs_1_.refs_8_.refs_6_.refs_4_, bf16[2,512,256]{2,1,0:T(8,128)(2,1)S(1)} %pair.4.refs_1_.refs_0_, bf16[2,512,256]{2,1,0:T(8,128)(2,1)S(1)} %pair.5.refs_2_.refs_1_, bf16[2,512,256]{2,1,0:T(8,128)(2,1)S(1)} %collective-permute-done.1.refs_3_.refs_2_, ...), custom_call_target="tpu_custom_call" | custom-call | flops 1 | bytes 1 | tf_op jit(solution)/shard_map/encode/pallas_call | solution.py:65
  30.5 2.6 %collective-permute-done.2.refs_1_.refs_6_ = bf16[2,512,256]{2,1,0:T(8,128)(2,1)S(1)} collective-permute-done((bf16[2,512,256]{2,1,0:T(8,128)(2,1)S(1)}, bf16[2,512,256]{2,1,0:T(8,128)(2,1)S(1)}, u32[]{:S(2)}, u32[]{:S(2)}) %collective-permute-start.2) | collective-permute-done | bytes 524320 | tf_op jit(solution)/shard_map/ppermute | solution.py:38
  33.1 1.5 %collective-permute-done.6.refs_2_.refs_7_ = bf16[2,512,256]{2,1,0:T(8,128)(2,1)S(1)} collective-permute-done((bf16[2,512,256]{2,1,0:T(8,128)(2,1)S(1)}, bf16[2,512,256]{2,1,0:T(8,128)(2,1)S(1)}, u32[]{:S(2)}, u32[]{:S(2)}) %collective-permute-start.6) | collective-permute-done | bytes 524320 | tf_op jit(solution)/shard_map/ppermute | solution.py:38
  35.6 3.5 %collective-permute-start.9 = (bf16[512,128]{1,0:T(8,128)(2,1)S(1)}, bf16[512,128]{1,0:T(8,128)(2,1)S(1)}, u32[]{:S(2)}, u32[]{:S(2)}) collective-permute-start(bf16[512,128]{1,0:T(8,128)(2,1)S(1)} %encode.3.refs_1_), channel_id=1, source_target_pairs={{0,32},{1,33},{2,34},{3,35},{4,36},{5,37},{6,38},{7,39},{8,40},{9,... | collective-permute-start | bytes 393224 | tf_op jit(solution)/shard_map/ppermute | solution.py:42
  39.1 4.8 %collective-permute-start.10 = (bf16[512,128]{1,0:T(8,128)(2,1)S(1)}, bf16[512,128]{1,0:T(8,128)(2,1)S(1)}, u32[]{:S(2)}, u32[]{:S(2)}) collective-permute-start(bf16[512,128]{1,0:T(8,128)(2,1)S(1)} %encode.3.refs_1_), channel_id=1, source_target_pairs={{0,64},{1,65},{2,66},{3,67},{4,68},{5,69},{6,70},{7,71},{8,72},{9,... | collective-permute-start | bytes 393224 | tf_op jit(solution)/shard_map/ppermute | solution.py:42
  43.9 1.3 collective-permute-start.11
  46.4 1.3 collective-permute-done.11.refs_4_
  47.7 1.3 collective-permute-done.15.refs_8_
  50.0 1.8 %decode.2 = (bf16[2,512,256]{2,1,0:T(8,128)(2,1)S(1)}, bf16[2,512,256]{2,1,0:T(8,128)(2,1)S(1)}) custom-call(s32[128]{0:T(128)S(1)} %fusion.refs_2_.refs_0_.refs_1_.refs_8_.refs_6_.refs_4_, bf16[512,1024]{1,0:T(8,128)(2,1)S(1)} %get-tuple-element.39.refs_1_, bf16[1024,4096]{1,0:T(8,128)(2,1)S(1)} %bitcast.14), custom_call_target="tpu_custom_call" | custom-call | flops 1 | bytes 1 | tf_op jit(solution)/shard_map/decode/pallas_call | solution.py:65
  52.1 3.7 %collective-permute-start.17 = (bf16[2,512,256]{2,1,0:T(8,128)(2,1)S(1)}, bf16[2,512,256]{2,1,0:T(8,128)(2,1)S(1)}, u32[]{:S(2)}, u32[]{:S(2)}) collective-permute-start(bf16[2,512,256]{2,1,0:T(8,128)(2,1)S(1)} %get-tuple-element.46), channel_id=1, source_target_pairs={{0,12},{1,13},{2,14},{3,15},{4,0},{5,1},{6,2},{7,3},{8,4},{9,5},{1... | collective-permute-start | bytes 1572872 | tf_op jit(solution)/shard_map/ppermute | solution.py:38
  55.8 4.0 %decode.3 = (f32[2,512,256]{2,1,0:T(8,128)S(1)}, bf16[2,512,256]{2,1,0:T(8,128)(2,1)S(1)}, bf16[2,512,256]{2,1,0:T(8,128)(2,1)S(1)}, f32[2,512,256]{2,1,0:T(8,12...) custom-call(s32[128]{0:T(128)S(1)} %fusion.refs_2_.refs_0_.refs_1_.refs_8_.refs_6_.refs_4_, ...), custom_call_target="tpu_custom_call" | custom-call | flops 1 | bytes 1 | tf_op jit(solution)/shard_map/decode/pallas_call | solution.py:65
  61.0 1.7 %collective-permute-done.16.refs_4_ = bf16[2,512,256]{2,1,0:T(8,128)(2,1)S(1)} collective-permute-done((bf16[2,512,256]{2,1,0:T(8,128)(2,1)S(1)}, bf16[2,512,256]{2,1,0:T(8,128)(2,1)S(1)}, u32[]{:S(2)}, u32[]{:S(2)}) %collective-permute-start.16) | collective-permute-done | bytes 524320 | tf_op jit(solution)/shard_map/ppermute | solution.py:38
  63.0 1.5 %collective-permute-start.20 = (bf16[3,512,256]{2,1,0:T(8,128)(2,1)S(1)}, bf16[3,512,256]{2,1,0:T(8,128)(2,1)S(1)}, u32[]{:S(2)}, u32[]{:S(2)}) collective-permute-start(bf16[3,512,256]{2,1,0:T(8,128)(2,1)S(1)} %get-tuple-element.51), channel_id=1, source_target_pairs={{0,4},{1,5},{2,6},{3,7},{4,8},{5,9},{6,10},{7,11},{8,12},{9,13},{1... | collective-permute-start | bytes 2359304 | tf_op jit(solution)/shard_map/ppermute | solution.py:38
  64.4 2.2 %collective-permute-start.21 = (bf16[3,512,256]{2,1,0:T(8,128)(2,1)S(1)}, bf16[3,512,256]{2,1,0:T(8,128)(2,1)S(1)}, u32[]{:S(2)}, u32[]{:S(2)}) collective-permute-start(bf16[3,512,256]{2,1,0:T(8,128)(2,1)S(1)} %get-tuple-element.52), channel_id=1, source_target_pairs={{0,12},{1,13},{2,14},{3,15},{4,0},{5,1},{6,2},{7,3},{8,4},{9,5},{1... | collective-permute-start | bytes 2359304 | tf_op jit(solution)/shard_map/ppermute | solution.py:38
  66.6 3.2 %collective-permute-start.19 = (bf16[512,256]{1,0:T(8,128)(2,1)S(1)}, bf16[512,256]{1,0:T(8,128)(2,1)S(1)}, u32[]{:S(2)}, u32[]{:S(2)}) collective-permute-start(bf16[512,256]{1,0:T(8,128)(2,1)S(1)} %get-tuple-element.49), channel_id=1, source_target_pairs={{0,12},{1,13},{2,14},{3,15},{4,0},{5,1},{6,2},{7,3},{8,4},{9,5},{1... | collective-permute-start | bytes 786440 | tf_op jit(solution)/shard_map/ppermute | solution.py:38
  69.8 6.7 %collective-permute-done.20.refs_2_ = bf16[3,512,256]{2,1,0:T(8,128)(2,1)S(1)} collective-permute-done((bf16[3,512,256]{2,1,0:T(8,128)(2,1)S(1)}, bf16[3,512,256]{2,1,0:T(8,128)(2,1)S(1)}, u32[]{:S(2)}, u32[]{:S(2)}) %collective-permute-start.20) | collective-permute-done | bytes 786464 | tf_op jit(solution)/shard_map/ppermute | solution.py:38
  76.7 2.4 %collective-permute-start.22 = (bf16[512,256]{1,0:T(8,128)(2,1)S(1)}, bf16[512,256]{1,0:T(8,128)(2,1)S(1)}, u32[]{:S(2)}, u32[]{:S(2)}) collective-permute-start(bf16[512,256]{1,0:T(8,128)(2,1)S(1)} %get-tuple-element.53), channel_id=1, source_target_pairs={{0,2},{1,3},{2,0},{3,1},{4,6},{5,7},{6,4},{7,5},{8,10},{9,11},{10,... | collective-permute-start | bytes 786440 | tf_op jit(solution)/shard_map/ppermute | solution.py:33
  79.8 2.5 %collective-permute-start.24 = (bf16[512,256]{1,0:T(8,128)(2,1)S(1)}, bf16[512,256]{1,0:T(8,128)(2,1)S(1)}, u32[]{:S(2)}, u32[]{:S(2)}) collective-permute-start(bf16[512,256]{1,0:T(8,128)(2,1)S(1)} %get-tuple-element.55), channel_id=1, source_target_pairs={{0,3},{1,0},{2,1},{3,2},{4,7},{5,4},{6,5},{7,6},{8,11},{9,8},{10,9... | collective-permute-start | bytes 786440 | tf_op jit(solution)/shard_map/ppermute | solution.py:33
  82.3 2.4 %collective-permute-done.22.refs_3_ = bf16[512,256]{1,0:T(8,128)(2,1)S(1)} collective-permute-done((bf16[512,256]{1,0:T(8,128)(2,1)S(1)}, bf16[512,256]{1,0:T(8,128)(2,1)S(1)}, u32[]{:S(2)}, u32[]{:S(2)}) %collective-permute-start.22) | collective-permute-done | bytes 262176 | tf_op jit(solution)/shard_map/ppermute | solution.py:33
  84.8 2.7 %collective-permute-done.23.refs_4_ = bf16[512,256]{1,0:T(8,128)(2,1)S(1)} collective-permute-done((bf16[512,256]{1,0:T(8,128)(2,1)S(1)}, bf16[512,256]{1,0:T(8,128)(2,1)S(1)}, u32[]{:S(2)}, u32[]{:S(2)}) %collective-permute-start.23) | collective-permute-done | bytes 262176 | tf_op jit(solution)/shard_map/ppermute | solution.py:33
  87.8 2.5 %collective-permute-start.27 = (bf16[512,256]{1,0:T(8,128)(2,1)S(1)}, bf16[512,256]{1,0:T(8,128)(2,1)S(1)}, u32[]{:S(2)}, u32[]{:S(2)}) collective-permute-start(bf16[512,256]{1,0:T(8,128)(2,1)S(1)} %get-tuple-element.56.refs_0_), channel_id=1, source_target_pairs={{0,3},{1,0},{2,1},{3,2},{4,7},{5,4},{6,5},{7,6},{8,11},{9,8},{10,9... | collective-permute-start | bytes 786440 | tf_op jit(solution)/shard_map/ppermute | solution.py:33
  91.3 5.7 %collective-permute-done.27.refs_0_ = bf16[512,256]{1,0:T(8,128)(2,1)S(1)} collective-permute-done((bf16[512,256]{1,0:T(8,128)(2,1)S(1)}, bf16[512,256]{1,0:T(8,128)(2,1)S(1)}, u32[]{:S(2)}, u32[]{:S(2)}) %collective-permute-start.27) | collective-permute-done | bytes 262176 | tf_op jit(solution)/shard_map/ppermute | solution.py:33
  98.3 3.4 %collective-permute-start.31 = (bf16[2,512,256]{2,1,0:T(8,128)(2,1)S(1)}, bf16[2,512,256]{2,1,0:T(8,128)(2,1)S(1)}, u32[]{:S(2)}, u32[]{:S(2)}) collective-permute-start(bf16[2,512,256]{2,1,0:T(8,128)(2,1)S(1)} %pair.7.refs_2_.refs_10_), channel_id=1, source_target_pairs={{0,12},{1,13},{2,14},{3,15},{4,0},{5,1},{6,2},{7,3},{8,4},{9,5},{1... | collective-permute-start | bytes 1572872 | tf_op jit(solution)/shard_map/ppermute | solution.py:38
  101.7 1.5 %collective-permute-start.26 = (bf16[2,512,256]{2,1,0:T(8,128)(2,1)S(1)}, bf16[2,512,256]{2,1,0:T(8,128)(2,1)S(1)}, u32[]{:S(2)}, u32[]{:S(2)}) collective-permute-start(bf16[2,512,256]{2,1,0:T(8,128)(2,1)S(1)} %pair.6.refs_1_.refs_9_), channel_id=1, source_target_pairs={{0,4},{1,5},{2,6},{3,7},{4,8},{5,9},{6,10},{7,11},{8,12},{9,13},{1... | collective-permute-start | bytes 1572872 | tf_op jit(solution)/shard_map/ppermute | solution.py:38
  103.2 2.7 %collective-permute-start.29 = (bf16[2,512,256]{2,1,0:T(8,128)(2,1)S(1)}, bf16[2,512,256]{2,1,0:T(8,128)(2,1)S(1)}, u32[]{:S(2)}, u32[]{:S(2)}) collective-permute-start(bf16[2,512,256]{2,1,0:T(8,128)(2,1)S(1)} %pair.7.refs_2_.refs_10_), channel_id=1, source_target_pairs={{0,4},{1,5},{2,6},{3,7},{4,8},{5,9},{6,10},{7,11},{8,12},{9,13},{1... | collective-permute-start | bytes 1572872 | tf_op jit(solution)/shard_map/ppermute | solution.py:38
  106.5 1.9 %collective-permute-done.31.refs_4_.refs_5_ = bf16[2,512,256]{2,1,0:T(8,128)(2,1)S(1)} collective-permute-done((bf16[2,512,256]{2,1,0:T(8,128)(2,1)S(1)}, bf16[2,512,256]{2,1,0:T(8,128)(2,1)S(1)}, u32[]{:S(2)}, u32[]{:S(2)}) %collective-permute-start.31) | collective-permute-done | bytes 524320 | tf_op jit(solution)/shard_map/ppermute | solution.py:38
  108.4 3.7 %collective-permute-start.33 = (bf16[2,512,256]{2,1,0:T(8,128)(2,1)S(1)}, bf16[2,512,256]{2,1,0:T(8,128)(2,1)S(1)}, u32[]{:S(2)}, u32[]{:S(2)}) collective-permute-start(bf16[2,512,256]{2,1,0:T(8,128)(2,1)S(1)} %collective-permute-done.31.refs_4_.refs_5_), channel_id=1, source_target_pairs={{0,12},{1,13},{2,14},{3,15},{4,0},{5,1},{6,2},{7,3},{8,4},{9,5},{1... | collective-permute-start | bytes 1572872 | tf_op jit(solution)/shard_map/ppermute | solution.py:38
  112.7 1.8 %code_grad.2.refs_6_ = f32[4,512,256]{2,1,0:T(8,128)S(1)} custom-call(s32[128]{0:T(128)S(1)} %fusion.refs_2_.refs_0_.refs_1_.refs_8_.refs_6_.refs_4_, bf16[2,512,256]{2,1,0:T(8,128)(2,1)S(1)} %pair.6.refs_1_.refs_9_, bf16[2,512,256]{2,1,0:T(8,128)(2,1)S(1)} %pair.7.refs_2_.refs_10_, bf16[1024,4096]{1,0:T(8,128)(2,1)S(1)} %bitcast.16), custom_call_target="tpu_custom_call" | custom-call | flops 1 | bytes 1 | tf_op jit(solution)/shard_map/code_grad/pallas_call | solution.py:65
  114.5 3.3 %collective-permute-done.29.refs_2_.refs_3_ = bf16[2,512,256]{2,1,0:T(8,128)(2,1)S(1)} collective-permute-done((bf16[2,512,256]{2,1,0:T(8,128)(2,1)S(1)}, bf16[2,512,256]{2,1,0:T(8,128)(2,1)S(1)}, u32[]{:S(2)}, u32[]{:S(2)}) %collective-permute-start.29) | collective-permute-done | bytes 524320 | tf_op jit(solution)/shard_map/ppermute | solution.py:38
  117.8 5.1 %middle.1 = (f32[4,512,256]{2,1,0:T(8,128)S(1)}, bf16[1024,4096]{1,0:T(8,128)(2,1)}, f32[512,256]{1,0:T(8,128)}) custom-call(s32[128]{0:T(128)S(1)} %fusion.refs_2_.refs_0_.refs_1_.refs_8_.refs_6_.refs_4_, bf16[2,512,256]{2,1,0:T(8,128)(2,1)S(1)} %collective-permute-done.26.refs_1_.refs_2_, bf16[2,512,256]{2,1,0:T(8,128)(2,1)S(1)} %collective-permute-done.29.refs_2_.refs_3_, ...), custom_call_target="tpu_custom_call" | custom-call | flops 1 | bytes 1 | tf_op jit(solution)/shard_map/middle/pallas_call | solution.py:65
  123.4 1.9 %code_grad.3 = (f32[4,512,128]{2,1,0:T(8,128)S(1)}, bf16[4,512,128]{2,1,0:T(8,128)(2,1)S(1)}) custom-call(s32[128]{0:T(128)S(1)} %fusion.refs_2_.refs_0_.refs_1_.refs_8_.refs_6_.refs_4_, bf16[2,512,256]{2,1,0:T(8,128)(2,1)S(1)} %collective-permute-done.32.refs_1_.refs_6_, bf16[2,512,256]{2,1,0:T(8,128)(2,1)S(1)} %collective-permute-done.33.refs_2_.refs_7_, ...), custom_call_target="tpu_custom_call" | custom-call | flops 1 | bytes 1 | tf_op jit(solution)/shard_map/code_grad/pallas_call | solution.py:65
  125.4 1.9 %collective-permute-done.34.refs_2_ = bf16[4,512,128]{2,1,0:T(8,128)(2,1)S(1)} collective-permute-done((bf16[4,512,128]{2,1,0:T(8,128)(2,1)S(1)}, bf16[4,512,128]{2,1,0:T(8,128)(2,1)S(1)}, u32[]{:S(2)}, u32[]{:S(2)}) %collective-permute-start.34) | collective-permute-done | bytes 524320 | tf_op jit(solution)/shard_map/ppermute | solution.py:46
  127.9 1.3 collective-permute-start.35
  129.2 1.3 collective-permute-start.36
  130.5 1.3 collective-permute-start.37
  131.8 5.3 %decoder_grad.1 = bf16[1024,4096]{1,0:T(8,128)(2,1)} custom-call(s32[128]{0:T(128)S(1)} %fusion.refs_2_.refs_0_.refs_1_.refs_8_.refs_6_.refs_4_, bf16[1024,512]{1,0:T(8,128)(2,1)S(1)} %get-tuple-element.57.refs_7_.refs_1_, bf16[2,512,256]{2,1,0:T(8,128)(2,1)S(1)} %collective-permute-done.26.refs_1_.refs_2_, ...), custom_call_target="tpu_custom_call", output_to_operand_aliasing={{}: (8, {})} | custom-call | flops 1 | bytes 1 | tf_op jit(solution)/shard_map/decoder_grad/pallas_call | solution.py:65
  138.2 2.8 %collective-permute-done.37.refs_13_ = bf16[512,128]{1,0:T(8,128)(2,1)S(1)} collective-permute-done((bf16[512,128]{1,0:T(8,128)(2,1)S(1)}, bf16[512,128]{1,0:T(8,128)(2,1)S(1)}, u32[]{:S(2)}, u32[]{:S(2)}) %collective-permute-start.37) | collective-permute-done | bytes 131104 | tf_op jit(solution)/shard_map/ppermute | solution.py:42
  141.0 2.7 %encoder_grad.1 = f32[4096,128]{1,0:T(8,128)} custom-call(s32[128]{0:T(128)S(1)} %fusion.refs_2_.refs_0_.refs_1_.refs_8_.refs_6_.refs_4_, bf16[2,256,512]{2,1,0:T(8,128)(2,1)S(1)} %get-tuple-element.47.refs_7_.refs_1_, bf16[2,256,512]{2,1,0:T(8,128)(2,1)S(1)} %get-tuple-element.65.refs_2_, bf16[2,256,512]{2,1,0:T(8,128)(2,1)S(1)} %get-tuple-element.66.refs_3_, ...), custom_call_target="tpu_custom_call" | custom-call | flops 1 | bytes 1 | tf_op jit(solution)/shard_map/encoder_grad/pallas_call | solution.py:65
  (62 shorter events, 17.0 us)
Async XLA Ops:
  0.6 7.6 %copy-start = (s32[1,512,256]{2,1,0:T(8,128)S(1)}, s32[1,512,256]{2,1,0:T(8,128)}, u32[]{:S(2)}) copy-start(s32[1,512,256]{2,1,0:T(8,128)} %param.11) | copy-start | bytes 1572868
  0.6 28.3 %copy-start.2 = (bf16[1,4096,128]{2,1,0:T(8,128)(2,1)S(1)}, bf16[1,4096,128]{2,1,0:T(8,128)(2,1)}, u32[]{:S(2)}) copy-start(bf16[1,4096,128]{2,1,0:T(8,128)(2,1)} %param.9) | copy-start | bytes 3145732
  0.7 7.9 %collective-permute-start = (bf16[512,256]{1,0:T(8,128)(2,1)}, bf16[512,256]{1,0:T(8,128)(2,1)S(1)}, u32[]{:S(2)}, u32[]{:S(2)}) collective-permute-start(bf16[512,256]{1,0:T(8,128)(2,1)} %bitcast.21), channel_id=1, source_target_pairs={{0,1},{1,2},{2,3},{3,0},{4,5},{5,6},{6,7},{7,4},{8,9},{9,10},{10,1... | collective-permute-start | bytes 786440 | tf_op jit(solution)/shard_map/ppermute | solution.py:33
  2.3 9.3 %collective-permute-start.3 = (bf16[512,256]{1,0:T(8,128)(2,1)}, bf16[512,256]{1,0:T(8,128)(2,1)S(1)}, u32[]{:S(2)}, u32[]{:S(2)}) collective-permute-start(bf16[512,256]{1,0:T(8,128)(2,1)} %bitcast.22), channel_id=1, source_target_pairs={{0,3},{1,0},{2,1},{3,2},{4,7},{5,4},{6,5},{7,6},{8,11},{9,8},{10,9... | collective-permute-start | bytes 786440 | tf_op jit(solution)/shard_map/ppermute | solution.py:33
  4.0 8.4 %collective-permute-start.4 = (bf16[512,256]{1,0:T(8,128)(2,1)}, bf16[512,256]{1,0:T(8,128)(2,1)S(1)}, u32[]{:S(2)}, u32[]{:S(2)}) collective-permute-start(bf16[512,256]{1,0:T(8,128)(2,1)} %bitcast.23), channel_id=1, source_target_pairs={{0,2},{1,3},{2,0},{3,1},{4,6},{5,7},{6,4},{7,5},{8,10},{9,11},{10,... | collective-permute-start | bytes 786440 | tf_op jit(solution)/shard_map/ppermute | solution.py:33
  8.2 26.4 %copy-start.4 = (f32[1,128]{1,0:T(1,128)S(1)}, f32[1,128]{1,0:T(1,128)}, u32[]{:S(2)}) copy-start(f32[1,128]{1,0:T(1,128)} %refs_6_.1) | copy-start | bytes 1540
  8.5 1.0 copy-start.3
  9.5 11.3 %collective-permute-start.1 = (bf16[2,512,256]{2,1,0:T(8,128)(2,1)S(1)}, bf16[2,512,256]{2,1,0:T(8,128)(2,1)S(1)}, u32[]{:S(2)}, u32[]{:S(2)}) collective-permute-start(bf16[2,512,256]{2,1,0:T(8,128)(2,1)S(1)} %pair.4.refs_1_.refs_0_), channel_id=1, source_target_pairs={{0,4},{1,5},{2,6},{3,7},{4,8},{5,9},{6,10},{7,11},{8,12},{9,13},{1... | collective-permute-start | bytes 1572872 | tf_op jit(solution)/shard_map/ppermute | solution.py:38
  12.4 10.9 %collective-permute-start.5 = (bf16[2,512,256]{2,1,0:T(8,128)(2,1)S(1)}, bf16[2,512,256]{2,1,0:T(8,128)(2,1)S(1)}, u32[]{:S(2)}, u32[]{:S(2)}) collective-permute-start(bf16[2,512,256]{2,1,0:T(8,128)(2,1)S(1)} %pair.5.refs_2_.refs_1_), channel_id=1, source_target_pairs={{0,12},{1,13},{2,14},{3,15},{4,0},{5,1},{6,2},{7,3},{8,4},{9,5},{1... | collective-permute-start | bytes 1572872 | tf_op jit(solution)/shard_map/ppermute | solution.py:38
  16.7 12.3 %collective-permute-start.8 = (bf16[2,512,256]{2,1,0:T(8,128)(2,1)S(1)}, bf16[2,512,256]{2,1,0:T(8,128)(2,1)S(1)}, u32[]{:S(2)}, u32[]{:S(2)}) collective-permute-start(bf16[2,512,256]{2,1,0:T(8,128)(2,1)S(1)} %pair.4.refs_1_.refs_0_), channel_id=1, source_target_pairs={{0,12},{1,13},{2,14},{3,15},{4,0},{5,1},{6,2},{7,3},{8,4},{9,5},{1... | collective-permute-start | bytes 1572872 | tf_op jit(solution)/shard_map/ppermute | solution.py:38
  17.1 11.9 %collective-permute-start.7 = (bf16[2,512,256]{2,1,0:T(8,128)(2,1)S(1)}, bf16[2,512,256]{2,1,0:T(8,128)(2,1)S(1)}, u32[]{:S(2)}, u32[]{:S(2)}) collective-permute-start(bf16[2,512,256]{2,1,0:T(8,128)(2,1)S(1)} %pair.5.refs_2_.refs_1_), channel_id=1, source_target_pairs={{0,4},{1,5},{2,6},{3,7},{4,8},{5,9},{6,10},{7,11},{8,12},{9,13},{1... | collective-permute-start | bytes 1572872 | tf_op jit(solution)/shard_map/ppermute | solution.py:38
  20.9 12.2 %collective-permute-start.2 = (bf16[2,512,256]{2,1,0:T(8,128)(2,1)S(1)}, bf16[2,512,256]{2,1,0:T(8,128)(2,1)S(1)}, u32[]{:S(2)}, u32[]{:S(2)}) collective-permute-start(bf16[2,512,256]{2,1,0:T(8,128)(2,1)S(1)} %collective-permute-done.1.refs_3_.refs_2_), channel_id=1, source_target_pairs={{0,4},{1,5},{2,6},{3,7},{4,8},{5,9},{6,10},{7,11},{8,12},{9,13},{1... | collective-permute-start | bytes 1572872 | tf_op jit(solution)/shard_map/ppermute | solution.py:38
  23.4 11.2 %collective-permute-start.6 = (bf16[2,512,256]{2,1,0:T(8,128)(2,1)S(1)}, bf16[2,512,256]{2,1,0:T(8,128)(2,1)S(1)}, u32[]{:S(2)}, u32[]{:S(2)}) collective-permute-start(bf16[2,512,256]{2,1,0:T(8,128)(2,1)S(1)} %collective-permute-done.5.refs_6_.refs_5_), channel_id=1, source_target_pairs={{0,12},{1,13},{2,14},{3,15},{4,0},{5,1},{6,2},{7,3},{8,4},{9,5},{1... | collective-permute-start | bytes 1572872 | tf_op jit(solution)/shard_map/ppermute | solution.py:38
  27.1 22.9 %copy-start.1 = (bf16[8,1,128,4096]{3,2,1,0:T(8,128)(2,1)S(1)}, bf16[8,1,128,4096]{3,2,1,0:T(8,128)(2,1)}, u32[]{:S(2)}) copy-start(bf16[8,1,128,4096]{3,2,1,0:T(8,128)(2,1)} %param.12) | copy-start | bytes 25165828
  35.6 9.7 %collective-permute-start.9 = (bf16[512,128]{1,0:T(8,128)(2,1)S(1)}, bf16[512,128]{1,0:T(8,128)(2,1)S(1)}, u32[]{:S(2)}, u32[]{:S(2)}) collective-permute-start(bf16[512,128]{1,0:T(8,128)(2,1)S(1)} %encode.3.refs_1_), channel_id=1, source_target_pairs={{0,32},{1,33},{2,34},{3,35},{4,36},{5,37},{6,38},{7,39},{8,40},{9,... | collective-permute-start | bytes 393224 | tf_op jit(solution)/shard_map/ppermute | solution.py:42
  39.1 7.3 %collective-permute-start.10 = (bf16[512,128]{1,0:T(8,128)(2,1)S(1)}, bf16[512,128]{1,0:T(8,128)(2,1)S(1)}, u32[]{:S(2)}, u32[]{:S(2)}) collective-permute-start(bf16[512,128]{1,0:T(8,128)(2,1)S(1)} %encode.3.refs_1_), channel_id=1, source_target_pairs={{0,64},{1,65},{2,66},{3,67},{4,68},{5,69},{6,70},{7,71},{8,72},{9,... | collective-permute-start | bytes 393224 | tf_op jit(solution)/shard_map/ppermute | solution.py:42
  43.9 3.8 %collective-permute-start.11 = (bf16[512,128]{1,0:T(8,128)(2,1)S(1)}, bf16[512,128]{1,0:T(8,128)(2,1)S(1)}, u32[]{:S(2)}, u32[]{:S(2)}) collective-permute-start(bf16[512,128]{1,0:T(8,128)(2,1)S(1)} %encode.3.refs_1_), channel_id=1, source_target_pairs={{0,96},{1,97},{2,98},{3,99},{4,100},{5,101},{6,102},{7,103},{8,104... | collective-permute-start | bytes 393224 | tf_op jit(solution)/shard_map/ppermute | solution.py:42
  45.2 2.5 %collective-permute-start.12 = (bf16[512,128]{1,0:T(8,128)(2,1)S(1)}, bf16[512,128]{1,0:T(8,128)(2,1)S(1)}, u32[]{:S(2)}, u32[]{:S(2)}) collective-permute-start(bf16[512,128]{1,0:T(8,128)(2,1)S(1)} %encode.3.refs_1_), channel_id=1, source_target_pairs={{0,16},{1,17},{2,18},{3,19},{4,20},{5,21},{6,22},{7,23},{8,24},{9,... | collective-permute-start | bytes 393224 | tf_op jit(solution)/shard_map/ppermute | solution.py:46
  45.3 2.4 %collective-permute-start.13 = (bf16[512,128]{1,0:T(8,128)(2,1)S(1)}, bf16[512,128]{1,0:T(8,128)(2,1)S(1)}, u32[]{:S(2)}, u32[]{:S(2)}) collective-permute-start(bf16[512,128]{1,0:T(8,128)(2,1)S(1)} %collective-permute-done.9.refs_2_), channel_id=1, source_target_pairs={{0,16},{1,17},{2,18},{3,19},{4,20},{5,21},{6,22},{7,23},{8,24},{9,... | collective-permute-start | bytes 393224 | tf_op jit(solution)/shard_map/ppermute | solution.py:46
  46.4 1.3 collective-permute-start.14
  47.7 1.3 collective-permute-start.15
  51.8 10.9 %collective-permute-start.16 = (bf16[2,512,256]{2,1,0:T(8,128)(2,1)S(1)}, bf16[2,512,256]{2,1,0:T(8,128)(2,1)S(1)}, u32[]{:S(2)}, u32[]{:S(2)}) collective-permute-start(bf16[2,512,256]{2,1,0:T(8,128)(2,1)S(1)} %get-tuple-element.40.refs_3_), channel_id=1, source_target_pairs={{0,4},{1,5},{2,6},{3,7},{4,8},{5,9},{6,10},{7,11},{8,12},{9,13},{1... | collective-permute-start | bytes 1572872 | tf_op jit(solution)/shard_map/ppermute | solution.py:38
  52.1 10.6 %collective-permute-start.17 = (bf16[2,512,256]{2,1,0:T(8,128)(2,1)S(1)}, bf16[2,512,256]{2,1,0:T(8,128)(2,1)S(1)}, u32[]{:S(2)}, u32[]{:S(2)}) collective-permute-start(bf16[2,512,256]{2,1,0:T(8,128)(2,1)S(1)} %get-tuple-element.46), channel_id=1, source_target_pairs={{0,12},{1,13},{2,14},{3,15},{4,0},{5,1},{6,2},{7,3},{8,4},{9,5},{1... | collective-permute-start | bytes 1572872 | tf_op jit(solution)/shard_map/ppermute | solution.py:38
  63.0 13.5 %collective-permute-start.20 = (bf16[3,512,256]{2,1,0:T(8,128)(2,1)S(1)}, bf16[3,512,256]{2,1,0:T(8,128)(2,1)S(1)}, u32[]{:S(2)}, u32[]{:S(2)}) collective-permute-start(bf16[3,512,256]{2,1,0:T(8,128)(2,1)S(1)} %get-tuple-element.51), channel_id=1, source_target_pairs={{0,4},{1,5},{2,6},{3,7},{4,8},{5,9},{6,10},{7,11},{8,12},{9,13},{1... | collective-permute-start | bytes 2359304 | tf_op jit(solution)/shard_map/ppermute | solution.py:38
  64.4 12.0 %collective-permute-start.21 = (bf16[3,512,256]{2,1,0:T(8,128)(2,1)S(1)}, bf16[3,512,256]{2,1,0:T(8,128)(2,1)S(1)}, u32[]{:S(2)}, u32[]{:S(2)}) collective-permute-start(bf16[3,512,256]{2,1,0:T(8,128)(2,1)S(1)} %get-tuple-element.52), channel_id=1, source_target_pairs={{0,12},{1,13},{2,14},{3,15},{4,0},{5,1},{6,2},{7,3},{8,4},{9,5},{1... | collective-permute-start | bytes 2359304 | tf_op jit(solution)/shard_map/ppermute | solution.py:38
  66.6 15.7 %collective-permute-start.18 = (bf16[512,256]{1,0:T(8,128)(2,1)S(1)}, bf16[512,256]{1,0:T(8,128)(2,1)S(1)}, u32[]{:S(2)}, u32[]{:S(2)}) collective-permute-start(bf16[512,256]{1,0:T(8,128)(2,1)S(1)} %get-tuple-element.48), channel_id=1, source_target_pairs={{0,4},{1,5},{2,6},{3,7},{4,8},{5,9},{6,10},{7,11},{8,12},{9,13},{1... | collective-permute-start | bytes 786440 | tf_op jit(solution)/shard_map/ppermute | solution.py:38
  66.6 15.7 %collective-permute-start.19 = (bf16[512,256]{1,0:T(8,128)(2,1)S(1)}, bf16[512,256]{1,0:T(8,128)(2,1)S(1)}, u32[]{:S(2)}, u32[]{:S(2)}) collective-permute-start(bf16[512,256]{1,0:T(8,128)(2,1)S(1)} %get-tuple-element.49), channel_id=1, source_target_pairs={{0,12},{1,13},{2,14},{3,15},{4,0},{5,1},{6,2},{7,3},{8,4},{9,5},{1... | collective-permute-start | bytes 786440 | tf_op jit(solution)/shard_map/ppermute | solution.py:38
  76.7 8.0 %collective-permute-start.22 = (bf16[512,256]{1,0:T(8,128)(2,1)S(1)}, bf16[512,256]{1,0:T(8,128)(2,1)S(1)}, u32[]{:S(2)}, u32[]{:S(2)}) collective-permute-start(bf16[512,256]{1,0:T(8,128)(2,1)S(1)} %get-tuple-element.53), channel_id=1, source_target_pairs={{0,2},{1,3},{2,0},{3,1},{4,6},{5,7},{6,4},{7,5},{8,10},{9,11},{10,... | collective-permute-start | bytes 786440 | tf_op jit(solution)/shard_map/ppermute | solution.py:33
  79.1 8.4 %collective-permute-start.23 = (bf16[512,256]{1,0:T(8,128)(2,1)S(1)}, bf16[512,256]{1,0:T(8,128)(2,1)S(1)}, u32[]{:S(2)}, u32[]{:S(2)}) collective-permute-start(bf16[512,256]{1,0:T(8,128)(2,1)S(1)} %get-tuple-element.54), channel_id=1, source_target_pairs={{0,1},{1,2},{2,3},{3,0},{4,5},{5,6},{6,7},{7,4},{8,9},{9,10},{10,1... | collective-permute-start | bytes 786440 | tf_op jit(solution)/shard_map/ppermute | solution.py:33
  79.8 7.7 %collective-permute-start.24 = (bf16[512,256]{1,0:T(8,128)(2,1)S(1)}, bf16[512,256]{1,0:T(8,128)(2,1)S(1)}, u32[]{:S(2)}, u32[]{:S(2)}) collective-permute-start(bf16[512,256]{1,0:T(8,128)(2,1)S(1)} %get-tuple-element.55), channel_id=1, source_target_pairs={{0,3},{1,0},{2,1},{3,2},{4,7},{5,4},{6,5},{7,6},{8,11},{9,8},{10,9... | collective-permute-start | bytes 786440 | tf_op jit(solution)/shard_map/ppermute | solution.py:33
  87.8 9.2 %collective-permute-start.27 = (bf16[512,256]{1,0:T(8,128)(2,1)S(1)}, bf16[512,256]{1,0:T(8,128)(2,1)S(1)}, u32[]{:S(2)}, u32[]{:S(2)}) collective-permute-start(bf16[512,256]{1,0:T(8,128)(2,1)S(1)} %get-tuple-element.56.refs_0_), channel_id=1, source_target_pairs={{0,3},{1,0},{2,1},{3,2},{4,7},{5,4},{6,5},{7,6},{8,11},{9,8},{10,9... | collective-permute-start | bytes 786440 | tf_op jit(solution)/shard_map/ppermute | solution.py:33
  90.3 8.0 %collective-permute-start.28 = (bf16[512,256]{1,0:T(8,128)(2,1)S(1)}, bf16[512,256]{1,0:T(8,128)(2,1)S(1)}, u32[]{:S(2)}, u32[]{:S(2)}) collective-permute-start(bf16[512,256]{1,0:T(8,128)(2,1)S(1)} %get-tuple-element.56.refs_0_), channel_id=1, source_target_pairs={{0,2},{1,3},{2,0},{3,1},{4,6},{5,7},{6,4},{7,5},{8,10},{9,11},{10,... | collective-permute-start | bytes 786440 | tf_op jit(solution)/shard_map/ppermute | solution.py:33
  91.2 10.5 %collective-permute-start.25 = (bf16[512,256]{1,0:T(8,128)(2,1)S(1)}, bf16[512,256]{1,0:T(8,128)(2,1)S(1)}, u32[]{:S(2)}, u32[]{:S(2)}) collective-permute-start(bf16[512,256]{1,0:T(8,128)(2,1)S(1)} %get-tuple-element.56.refs_0_), channel_id=1, source_target_pairs={{0,1},{1,2},{2,3},{3,0},{4,5},{5,6},{6,7},{7,4},{8,9},{9,10},{10,1... | collective-permute-start | bytes 786440 | tf_op jit(solution)/shard_map/ppermute | solution.py:33
  98.3 10.1 %collective-permute-start.31 = (bf16[2,512,256]{2,1,0:T(8,128)(2,1)S(1)}, bf16[2,512,256]{2,1,0:T(8,128)(2,1)S(1)}, u32[]{:S(2)}, u32[]{:S(2)}) collective-permute-start(bf16[2,512,256]{2,1,0:T(8,128)(2,1)S(1)} %pair.7.refs_2_.refs_10_), channel_id=1, source_target_pairs={{0,12},{1,13},{2,14},{3,15},{4,0},{5,1},{6,2},{7,3},{8,4},{9,5},{1... | collective-permute-start | bytes 1572872 | tf_op jit(solution)/shard_map/ppermute | solution.py:38
  101.7 10.5 %collective-permute-start.26 = (bf16[2,512,256]{2,1,0:T(8,128)(2,1)S(1)}, bf16[2,512,256]{2,1,0:T(8,128)(2,1)S(1)}, u32[]{:S(2)}, u32[]{:S(2)}) collective-permute-start(bf16[2,512,256]{2,1,0:T(8,128)(2,1)S(1)} %pair.6.refs_1_.refs_9_), channel_id=1, source_target_pairs={{0,4},{1,5},{2,6},{3,7},{4,8},{5,9},{6,10},{7,11},{8,12},{9,13},{1... | collective-permute-start | bytes 1572872 | tf_op jit(solution)/shard_map/ppermute | solution.py:38
  103.2 14.6 %collective-permute-start.29 = (bf16[2,512,256]{2,1,0:T(8,128)(2,1)S(1)}, bf16[2,512,256]{2,1,0:T(8,128)(2,1)S(1)}, u32[]{:S(2)}, u32[]{:S(2)}) collective-permute-start(bf16[2,512,256]{2,1,0:T(8,128)(2,1)S(1)} %pair.7.refs_2_.refs_10_), channel_id=1, source_target_pairs={{0,4},{1,5},{2,6},{3,7},{4,8},{5,9},{6,10},{7,11},{8,12},{9,13},{1... | collective-permute-start | bytes 1572872 | tf_op jit(solution)/shard_map/ppermute | solution.py:38
  106.0 11.8 %collective-permute-start.30 = (bf16[2,512,256]{2,1,0:T(8,128)(2,1)S(1)}, bf16[2,512,256]{2,1,0:T(8,128)(2,1)S(1)}, u32[]{:S(2)}, u32[]{:S(2)}) collective-permute-start(bf16[2,512,256]{2,1,0:T(8,128)(2,1)S(1)} %pair.6.refs_1_.refs_9_), channel_id=1, source_target_pairs={{0,12},{1,13},{2,14},{3,15},{4,0},{5,1},{6,2},{7,3},{8,4},{9,5},{1... | collective-permute-start | bytes 1572872 | tf_op jit(solution)/shard_map/ppermute | solution.py:38
  108.4 14.5 %collective-permute-start.33 = (bf16[2,512,256]{2,1,0:T(8,128)(2,1)S(1)}, bf16[2,512,256]{2,1,0:T(8,128)(2,1)S(1)}, u32[]{:S(2)}, u32[]{:S(2)}) collective-permute-start(bf16[2,512,256]{2,1,0:T(8,128)(2,1)S(1)} %collective-permute-done.31.refs_4_.refs_5_), channel_id=1, source_target_pairs={{0,12},{1,13},{2,14},{3,15},{4,0},{5,1},{6,2},{7,3},{8,4},{9,5},{1... | collective-permute-start | bytes 1572872 | tf_op jit(solution)/shard_map/ppermute | solution.py:38
  112.2 11.2 %collective-permute-start.32 = (bf16[2,512,256]{2,1,0:T(8,128)(2,1)S(1)}, bf16[2,512,256]{2,1,0:T(8,128)(2,1)S(1)}, u32[]{:S(2)}, u32[]{:S(2)}) collective-permute-start(bf16[2,512,256]{2,1,0:T(8,128)(2,1)S(1)} %collective-permute-done.26.refs_1_.refs_2_), channel_id=1, source_target_pairs={{0,4},{1,5},{2,6},{3,7},{4,8},{5,9},{6,10},{7,11},{8,12},{9,13},{1... | collective-permute-start | bytes 1572872 | tf_op jit(solution)/shard_map/ppermute | solution.py:38
  125.3 2.0 %collective-permute-start.34 = (bf16[4,512,128]{2,1,0:T(8,128)(2,1)S(1)}, bf16[4,512,128]{2,1,0:T(8,128)(2,1)S(1)}, u32[]{:S(2)}, u32[]{:S(2)}) collective-permute-start(bf16[4,512,128]{2,1,0:T(8,128)(2,1)S(1)} %get-tuple-element.63), channel_id=1, source_target_pairs={{0,16},{1,17},{2,18},{3,19},{4,20},{5,21},{6,22},{7,23},{8,24},{9,... | collective-permute-start | bytes 1572872 | tf_op jit(solution)/shard_map/ppermute | solution.py:46
  127.9 9.2 %collective-permute-start.35 = (bf16[512,128]{1,0:T(8,128)(2,1)S(1)}, bf16[512,128]{1,0:T(8,128)(2,1)S(1)}, u32[]{:S(2)}, u32[]{:S(2)}) collective-permute-start(bf16[512,128]{1,0:T(8,128)(2,1)S(1)} %get-tuple-element.64.refs_9_), channel_id=1, source_target_pairs={{32,0},{33,1},{34,2},{35,3},{36,4},{37,5},{38,6},{39,7},{40,8},{41... | collective-permute-start | bytes 393224 | tf_op jit(solution)/shard_map/ppermute | solution.py:42
  129.2 8.9 %collective-permute-start.36 = (bf16[512,128]{1,0:T(8,128)(2,1)S(1)}, bf16[512,128]{1,0:T(8,128)(2,1)S(1)}, u32[]{:S(2)}, u32[]{:S(2)}) collective-permute-start(bf16[512,128]{1,0:T(8,128)(2,1)S(1)} %get-tuple-element.73), channel_id=1, source_target_pairs={{64,0},{65,1},{66,2},{67,3},{68,4},{69,5},{70,6},{71,7},{72,8},{73... | collective-permute-start | bytes 393224 | tf_op jit(solution)/shard_map/ppermute | solution.py:42
  130.5 10.4 %collective-permute-start.37 = (bf16[512,128]{1,0:T(8,128)(2,1)S(1)}, bf16[512,128]{1,0:T(8,128)(2,1)S(1)}, u32[]{:S(2)}, u32[]{:S(2)}) collective-permute-start(bf16[512,128]{1,0:T(8,128)(2,1)S(1)} %get-tuple-element.74), channel_id=1, source_target_pairs={{96,0},{97,1},{98,2},{99,3},{100,4},{101,5},{102,6},{103,7},{104,8... | collective-permute-start | bytes 393224 | tf_op jit(solution)/shard_map/ppermute | solution.py:42

commit v4 on v3

--- a/solution.py
+++ b/solution.py
@@ -84,25 +84,36 @@
     return pl.ds(pl.multiple_of(sc[index] * 256, 256), 256)
 
 
-def encode(scalars, pairs, first, weight, total, finish):
+def encode(scalars, pairs, weight, dec):
     n = len(pairs)
 
     def kernel(sc, *refs):
-        w, rest, out = refs[n], refs[n + 1:-1], refs[-1]
+        w, d, out, rows, far = refs[n:]
+        for i in range(4):
+            far[i] = d[:, columns(sc, 12 + i)]
         left = jnp.concatenate([refs[i][k] for i in range(n) for k in range(2)], axis=1)
-        right = jnp.concatenate([w[columns(sc, first * 2 + i), :] for i in range(2 * n)], axis=0)
-        acc = dot(left, right)
-        if total is not None:
-            acc += rest[0][...]
-        if finish is None:
-            out[...] = acc
-        else:
-            out[...] = (rest[-2][...] * (acc + rest[-1][...])).astype(BF16)
-
-    args = [*pairs, weight] + ([] if total is None else [total]) + ([] if finish is None else list(finish))
-    return call(
-        kernel, scalars, args, shape((TOK, 128), F32 if finish is None else BF16), VMEM_SPEC,
-        flops=n * 4 * TOK * 256 * 128, moved=n * 524288, name="encode",
+        right = jnp.concatenate([w[columns(sc, i), :] for i in range(2 * n)], axis=0)
+        out[...] = dot(left, right)
+        for i in range(2 * n, 16):
+            rows[(i - 2 * n) * 256:(i - 2 * n) * 256 + 256, :] = w[columns(sc, i), :]
+
+    rest = 4096 - n * 512
+    return call(
+        kernel, scalars, [*pairs, weight, dec], (shape((TOK, 128), F32), shape((rest, 128), BF16), shape((4, 1024, 256), BF16)),
+        (VMEM_SPEC,) * 3, name="encode",
+    )
+
+
+def activate(scalars, pairs, rows, total, gates, bias):
+    n = len(pairs)
+
+    def kernel(sc, *refs):
+        w, before, g, b, out = refs[n:]
+        left = jnp.concatenate([refs[i][k] for i in range(n) for k in range(2)], axis=1)
+        out[...] = (g[...] * (before[...] + dot(left, w[...]) + b[...])).astype(BF16)
+
+    return call(
+        kernel, None, [*pairs, rows, total, gates, bias], shape((TOK, 128), BF16), VMEM_SPEC, name="activate", after=(scalars,),
     )
 
 
@@ -122,6 +133,17 @@
     return call(
         kernel, scalars, [*mine, *other], (shape((TOK, 1024), BF16), shape((1024, TOK), BF16)), (VMEM_SPEC, VMEM_SPEC),
         moved=4 * 1048576, name="assemble",
+    )
+
+
+def decode_far(scalars, acts, far):
+    def kernel(sc, a, w, *outs):
+        for i in range(2):
+            for k in range(2):
+                outs[i][k] = dot(a[...], w[2 * i + k]).astype(BF16)
+
+    return call(
+        kernel, None, [acts, far], (shape((2, TOK, 256), BF16),) * 2, (VMEM_SPEC,) * 2, name="decode_far", after=(scalars,),
     )
 
 
@@ -224,8 +246,9 @@
             if last:
                 keep, send = rest[-2:]
                 even, odd = acc[:, :128], acc[:, 128:]
-                keep[k] = jnp.where(c == 0, even, odd)
-                send[k] = jnp.where(c == 1, even, jnp.where(y == k, jnp.zeros_like(odd), odd)).astype(BF16)
+                slot = (y - k) & 3
+                keep[slot] = jnp.where(c == 0, even, odd)
+                send[slot] = jnp.where(c == 1, even, jnp.where(y == k, jnp.zeros_like(odd), odd)).astype(BF16)
             else:
                 rest[-1][k] = acc
 
@@ -254,38 +277,32 @@
 
 
 def flip(scalars, pairs, after):
-    def kernel(sc, *refs):
-        n = len(pairs)
+    n = len(pairs)
+
+    def kernel(sc, *refs):
         for i in range(n):
             for k in range(2):
-                refs[n + i][k] = refs[i][k].T
-
-    return call(
-        kernel, None, list(pairs), tuple(shape((2, 256, TOK), BF16) for _ in pairs), (VMEM_SPEC,) * len(pairs),
-        moved=len(pairs) * 1048576, name="flip", after=(scalars, *after),
-    )
+                refs[n][columns(sc, 2 * i + k), :] = refs[i][k].T
+
+    return call(kernel, scalars, list(pairs), shape((4096, TOK), BF16), VMEM_SPEC, name="flip", after=after)
 
 
 def encoder_grad(scalars, flipped, gates, sums):
-    n = len(flipped)
-
-    def kernel(sc, *refs):
-        g, parts, (out, rows, sems) = refs[n], refs[n + 1:-3], refs[-3:]
+    def kernel(sc, f, g, *refs):
+        parts, (out, rows, sems) = refs[:-3], refs[-3:]
         total = parts[0][...] + parts[1][...].astype(F32) + parts[2][...].astype(F32) + parts[3][...].astype(F32)
         grad = (g[...] * total).astype(BF16)
         copies = []
-        for i in range(n):
-            rows[i] = dot(refs[i][...].reshape(512, TOK), grad)
-            for k in range(2):
-                j = 2 * i + k
-                copies.append(pltpu.make_async_copy(rows.at[i, k * 256:k * 256 + 256], out.at[columns(sc, j), :], sems.at[j]))
-                copies[-1].start()
+        for i in range(8):
+            rows[i] = dot(f[i * 512:i * 512 + 512, :], grad)
+            copies.append(pltpu.make_async_copy(rows.at[i], out.at[i * 512:i * 512 + 512, :], sems.at[i]))
+            copies[-1].start()
         for copy in copies:
             copy.wait()
 
     return call(
-        kernel, scalars, [*flipped, gates, *sums], shape((4096, 128), F32), pl.BlockSpec(memory_space=pl.ANY),
-        name="encoder_grad", scratch=[pltpu.VMEM((n, 512, 128), F32), pltpu.SemaphoreType.DMA((2 * n,))],
+        kernel, None, [flipped, gates, *sums], shape((4096, 128), F32), pl.BlockSpec(memory_space=pl.ANY),
+        name="encoder_grad", after=(scalars,), scratch=[pltpu.VMEM((8, 512, 128), F32), pltpu.SemaphoreType.DMA((8,))],
     )
 
 
@@ -329,18 +346,13 @@
 
 def split(scalars, keep, came):
     def kernel(sc, a, b, own, *outs):
-        y = sc[16]
-        for o in range(4):
-            k = (y - o) & 3
-            total = a[k] + b[k].astype(F32)
-            if o == 0:
-                own[...] = total
-            else:
-                outs[o - 1][...] = total.astype(BF16)
-
-    return call(
-        kernel, scalars, [keep, came], (shape((TOK, 128), F32),) + (shape((TOK, 128), BF16),) * 3, (VMEM_SPEC,) * 4,
-        name="split",
+        own[...] = a[0] + b[0].astype(F32)
+        for o in (1, 2, 3):
+            outs[o - 1][...] = (a[o] + b[o].astype(F32)).astype(BF16)
+
+    return call(
+        kernel, None, [keep, came], (shape((TOK, 128), F32),) + (shape((TOK, 128), BF16),) * 3, (VMEM_SPEC,) * 4,
+        name="split", after=(scalars,),
     )
 
 
@@ -376,18 +388,18 @@
     v1, v2 = long(v, 1), long(v, -1)
     inputs = (u, v, u1, v1, u2, v2, long(u1, 1), long(v2, -1))
 
-    early = encode(scalars, inputs[:6], 0, enc_weight[0], None, None)
-    act = encode(scalars, inputs[6:], 6, enc_weight[0], early, (gates, enc_bias))
+    early, rows, far = encode(scalars, inputs[:6], enc_weight[0], dec)
+    act = activate(scalars, inputs[6:], rows, early, gates, enc_bias)
 
     mine = [act] + [chips_y(act, o) for o in (1, 2, 3)]
     other = [other_core(m) for m in mine]
     acts, acts_t = assemble(scalars, mine, other)
 
-    u_opp, v_opp = decode(scalars, acts, dec, (6, 7), (BF16, BF16))
+    u_opp, v_opp = decode_far(scalars, acts, far)
     from_left, from_right = long(u_opp, 1), long(v_opp, -1)
     sums = decode(scalars, acts, dec, (4, 5, 2, 3, 0, 1), (F32, BF16, BF16, F32, F32, F32), after=(u_opp,))
     flipped = flip(scalars, inputs, after=(sums[0],))
-    right_most, right_own, left_most, left_own = pass_on(scalars, *sums[:4], from_left, from_right, after=(flipped[0],))
+    right_most, right_own, left_most, left_own = pass_on(scalars, *sums[:4], from_left, from_right, after=(flipped,))
     left, right = long(right_most, 1), long(left_most, -1)
     own_left, own_right = long(right_own, 1), long(left_own, -1)
     to_prev, to_next, to_opp = add_up(scalars, *sums[4:], left, right)

time: 144 us -> 142 us (0.986)
  waiting for transfers between devices: 45.4 us -> 41.1 us
  local copies, waits for them, and re-layouts: 3.45 us -> 6.84 us
    ppermute x18, waiting for transfers between devices: 23.4 us -> 19.1 us  [long(): return lax.ppermute(value, AXES, pairs_of(move))]
    unnamed x10 -> x14, local copies, waits for them, and re-layouts: 0.97 us -> 4.36 us
  transfers between devices with their start and end apart: 38 -> 38, of which waited for: 23 -> 22; matrix products, arithmetic and copies ran while one was open for 2% -> 2% of each run, Pallas kernels for 14% -> 15%
where the time goes in v4:
time: 142 us
  starting transfers between devices  63.7 us (45%)
  waiting for transfers between devices  41.1 us (29%)
  Pallas kernels  28.9 us (20%)
  local copies, waits for them, and re-layouts  6.84 us (5%)
    ppermute x18, starting transfers between devices, long(): return lax.ppermute(value, AXES, pairs_of(move))  35.2 us
    pallas_call x20, Pallas kernels, call(): pl.pallas_call(body, grid_spec=pltpu.PrefetchScalarGridSpec(num_scalar_pr...  28.9 us
    ppermute x18, waiting for transfers between devices, long(): return lax.ppermute(value, AXES, pairs_of(move))  19.1 us
    ppermute x9, starting transfers between devices, short(): return lax.ppermute(value, AXES, pairs_of(move))  14.3 us
    ppermute x6, starting transfers between devices, chips_y(): lax.ppermute(value, AXES, pairs_of(lambda y, c, z, x: (y + step, c, z, x)))  13.5 us
    ppermute x9, waiting for transfers between devices, short(): return lax.ppermute(value, AXES, pairs_of(move))  13.1 us
    ppermute x6, waiting for transfers between devices, chips_y(): lax.ppermute(value, AXES, pairs_of(lambda y, c, z, x: (y + step, c, z, x)))  5.71 us
    unnamed x14, local copies, waits for them, and re-layouts  4.36 us
  transfers between devices with their start and end apart: 38, of which 22 were waited for; matrix products, arithmetic and copies ran while one was open for 2% of the time, Pallas kernels for 15%

profile of v4, /device:TPU:0, one launch (start us, length us, event | category | flops | bytes accessed | tf_op | source)
XLA Modules:
  0.0 141.6 jit_solution(7214256232587485432)
XLA Ops:
  0.7 1.6 %collective-permute-start = (bf16[512,256]{1,0:T(8,128)(2,1)}, bf16[512,256]{1,0:T(8,128)(2,1)S(1)}, u32[]{:S(2)}, u32[]{:S(2)}) collective-permute-start(bf16[512,256]{1,0:T(8,128)(2,1)} %bitcast.20), channel_id=1, source_target_pairs={{0,1},{1,2},{2,3},{3,0},{4,5},{5,6},{6,7},{7,4},{8,9},{9,10},{10,1... | collective-permute-start | bytes 786440 | tf_op jit(solution)/shard_map/ppermute | solution.py:33
  2.3 1.7 %collective-permute-start.3 = (bf16[512,256]{1,0:T(8,128)(2,1)}, bf16[512,256]{1,0:T(8,128)(2,1)S(1)}, u32[]{:S(2)}, u32[]{:S(2)}) collective-permute-start(bf16[512,256]{1,0:T(8,128)(2,1)} %bitcast.21), channel_id=1, source_target_pairs={{0,3},{1,0},{2,1},{3,2},{4,7},{5,4},{6,5},{7,6},{8,11},{9,8},{10,9... | collective-permute-start | bytes 786440 | tf_op jit(solution)/shard_map/ppermute | solution.py:33
  4.0 1.9 %collective-permute-start.4 = (bf16[512,256]{1,0:T(8,128)(2,1)}, bf16[512,256]{1,0:T(8,128)(2,1)S(1)}, u32[]{:S(2)}, u32[]{:S(2)}) collective-permute-start(bf16[512,256]{1,0:T(8,128)(2,1)} %bitcast.22), channel_id=1, source_target_pairs={{0,2},{1,3},{2,0},{3,1},{4,6},{5,7},{6,4},{7,5},{8,10},{9,11},{10,... | collective-permute-start | bytes 786440 | tf_op jit(solution)/shard_map/ppermute | solution.py:33
  9.5 2.1 %collective-permute-start.1 = (bf16[2,512,256]{2,1,0:T(8,128)(2,1)S(1)}, bf16[2,512,256]{2,1,0:T(8,128)(2,1)S(1)}, u32[]{:S(2)}, u32[]{:S(2)}) collective-permute-start(bf16[2,512,256]{2,1,0:T(8,128)(2,1)S(1)} %pair.4.refs_1_), channel_id=1, source_target_pairs={{0,4},{1,5},{2,6},{3,7},{4,8},{5,9},{6,10},{7,11},{8,12},{9,13},{1... | collective-permute-start | bytes 1572872 | tf_op jit(solution)/shard_map/ppermute | solution.py:38
  12.5 4.2 %collective-permute-start.5 = (bf16[2,512,256]{2,1,0:T(8,128)(2,1)S(1)}, bf16[2,512,256]{2,1,0:T(8,128)(2,1)S(1)}, u32[]{:S(2)}, u32[]{:S(2)}) collective-permute-start(bf16[2,512,256]{2,1,0:T(8,128)(2,1)S(1)} %pair.5.refs_2_), channel_id=1, source_target_pairs={{0,12},{1,13},{2,14},{3,15},{4,0},{5,1},{6,2},{7,3},{8,4},{9,5},{1... | collective-permute-start | bytes 1572872 | tf_op jit(solution)/shard_map/ppermute | solution.py:38
  17.1 1.6 %collective-permute-start.7 = (bf16[2,512,256]{2,1,0:T(8,128)(2,1)S(1)}, bf16[2,512,256]{2,1,0:T(8,128)(2,1)S(1)}, u32[]{:S(2)}, u32[]{:S(2)}) collective-permute-start(bf16[2,512,256]{2,1,0:T(8,128)(2,1)S(1)} %pair.5.refs_2_), channel_id=1, source_target_pairs={{0,4},{1,5},{2,6},{3,7},{4,8},{5,9},{6,10},{7,11},{8,12},{9,13},{1... | collective-permute-start | bytes 1572872 | tf_op jit(solution)/shard_map/ppermute | solution.py:38
  18.7 2.2 %collective-permute-done.1.refs_3_ = bf16[2,512,256]{2,1,0:T(8,128)(2,1)S(1)} collective-permute-done((bf16[2,512,256]{2,1,0:T(8,128)(2,1)S(1)}, bf16[2,512,256]{2,1,0:T(8,128)(2,1)S(1)}, u32[]{:S(2)}, u32[]{:S(2)}) %collective-permute-start.1) | collective-permute-done | bytes 524320 | tf_op jit(solution)/shard_map/ppermute | solution.py:38
  20.9 2.5 %collective-permute-done.5.refs_6_ = bf16[2,512,256]{2,1,0:T(8,128)(2,1)S(1)} collective-permute-done((bf16[2,512,256]{2,1,0:T(8,128)(2,1)S(1)}, bf16[2,512,256]{2,1,0:T(8,128)(2,1)S(1)}, u32[]{:S(2)}, u32[]{:S(2)}) %collective-permute-start.5) | collective-permute-done | bytes 524320 | tf_op jit(solution)/shard_map/ppermute | solution.py:38
  23.4 3.7 %collective-permute-start.6 = (bf16[2,512,256]{2,1,0:T(8,128)(2,1)S(1)}, bf16[2,512,256]{2,1,0:T(8,128)(2,1)S(1)}, u32[]{:S(2)}, u32[]{:S(2)}) collective-permute-start(bf16[2,512,256]{2,1,0:T(8,128)(2,1)S(1)} %collective-permute-done.5.refs_6_), channel_id=1, source_target_pairs={{0,12},{1,13},{2,14},{3,15},{4,0},{5,1},{6,2},{7,3},{8,4},{9,5},{1... | collective-permute-start | bytes 1572872 | tf_op jit(solution)/shard_map/ppermute | solution.py:38
  27.1 1.5 %prepare.1.refs_4_.refs_1_ = f32[512,128]{1,0:T(8,128)S(1)} custom-call(s32[512,16]{1,0:T(8,128)S(1)} %dynamic-slice_bitcast_fusion.refs_5_.refs_0_, s32[128]{0:T(128)S(1)} %fusion.refs_2_.refs_0_.refs_1_.refs_6_.refs_4_.refs_8_), custom_call_target="tpu_custom_call" | custom-call | flops 1 | bytes 1 | tf_op jit(solution)/shard_map/prepare/pallas_call | solution.py:65
  29.0 3.4 %copy-done.2 = bf16[8,1,128,4096]{3,2,1,0:T(8,128)(2,1)S(1)} copy-done((bf16[8,1,128,4096]{3,2,1,0:T(8,128)(2,1)S(1)}, bf16[8,1,128,4096]{3,2,1,0:T(8,128)(2,1)}, u32[]{:S(2)}) %copy-start.2) | copy-done | bytes 8388632
  32.4 1.8 %encode.1 = (f32[512,128]{1,0:T(8,128)S(1)}, bf16[1024,128]{1,0:T(8,128)(2,1)S(1)}, bf16[4,1024,256]{2,1,0:T(8,128)(2,1)S(1)}) custom-call(s32[128]{0:T(128)S(1)} %fusion.refs_2_.refs_0_.refs_1_.refs_6_.refs_4_.refs_8_, bf16[2,512,256]{2,1,0:T(8,128)(2,1)S(1)} %pair.4.refs_1_, bf16[2,512,256]{2,1,0:T(8,128)(2,1)S(1)} %pair.5.refs_2_, ...), custom_call_target="tpu_custom_call" | custom-call | flops 1 | bytes 1 | tf_op jit(solution)/shard_map/encode/pallas_call | solution.py:65
  35.1 3.5 %collective-permute-start.9 = (bf16[512,128]{1,0:T(8,128)(2,1)S(1)}, bf16[512,128]{1,0:T(8,128)(2,1)S(1)}, u32[]{:S(2)}, u32[]{:S(2)}) collective-permute-start(bf16[512,128]{1,0:T(8,128)(2,1)S(1)} %activate.1.refs_1_), channel_id=1, source_target_pairs={{0,32},{1,33},{2,34},{3,35},{4,36},{5,37},{6,38},{7,39},{8,40},{9,... | collective-permute-start | bytes 393224 | tf_op jit(solution)/shard_map/ppermute | solution.py:42
  38.5 4.8 %collective-permute-start.10 = (bf16[512,128]{1,0:T(8,128)(2,1)S(1)}, bf16[512,128]{1,0:T(8,128)(2,1)S(1)}, u32[]{:S(2)}, u32[]{:S(2)}) collective-permute-start(bf16[512,128]{1,0:T(8,128)(2,1)S(1)} %activate.1.refs_1_), channel_id=1, source_target_pairs={{0,64},{1,65},{2,66},{3,67},{4,68},{5,69},{6,70},{7,71},{8,72},{9,... | collective-permute-start | bytes 393224 | tf_op jit(solution)/shard_map/ppermute | solution.py:42
  43.4 1.3 collective-permute-start.11
  45.9 1.3 collective-permute-done.11.refs_4_
  47.2 1.3 collective-permute-done.15.refs_8_
  49.4 1.3 decode_far.1
  51.0 3.7 %collective-permute-start.17 = (bf16[2,512,256]{2,1,0:T(8,128)(2,1)S(1)}, bf16[2,512,256]{2,1,0:T(8,128)(2,1)S(1)}, u32[]{:S(2)}, u32[]{:S(2)}) collective-permute-start(bf16[2,512,256]{2,1,0:T(8,128)(2,1)S(1)} %get-tuple-element.44), channel_id=1, source_target_pairs={{0,12},{1,13},{2,14},{3,15},{4,0},{5,1},{6,2},{7,3},{8,4},{9,5},{1... | collective-permute-start | bytes 1572872 | tf_op jit(solution)/shard_map/ppermute | solution.py:38
  54.7 4.0 %decode.1 = (f32[2,512,256]{2,1,0:T(8,128)S(1)}, bf16[2,512,256]{2,1,0:T(8,128)(2,1)S(1)}, bf16[2,512,256]{2,1,0:T(8,128)(2,1)S(1)}, f32[2,512,256]{2,1,0:T(8,12...) custom-call(s32[128]{0:T(128)S(1)} %fusion.refs_2_.refs_0_.refs_1_.refs_6_.refs_4_.refs_8_, ...), custom_call_target="tpu_custom_call" | custom-call | flops 1 | bytes 1 | tf_op jit(solution)/shard_map/decode/pallas_call | solution.py:65
  58.7 1.7 %flip.1.refs_7_.refs_0_ = bf16[4096,512]{1,0:T(8,128)(2,1)S(1)} custom-call(s32[128]{0:T(128)S(1)} %fusion.refs_2_.refs_0_.refs_1_.refs_6_.refs_4_.refs_8_, bf16[2,512,256]{2,1,0:T(8,128)(2,1)S(1)} %pair.4.refs_1_, bf16[2,512,256]{2,1,0:T(8,128)(2,1)S(1)} %pair.5.refs_2_, bf16[2,512,256]{2,1,0:T(8,128)(2,1)S(1)} %collective-permute-done.1.refs_3_, ...), custom_call_target="tpu_custom_call" | custom-call | flops 1 | bytes 1 | tf_op jit(solution)/shard_map/flip/pallas_call | solution.py:65
  61.8 1.5 %collective-permute-start.20 = (bf16[3,512,256]{2,1,0:T(8,128)(2,1)S(1)}, bf16[3,512,256]{2,1,0:T(8,128)(2,1)S(1)}, u32[]{:S(2)}, u32[]{:S(2)}) collective-permute-start(bf16[3,512,256]{2,1,0:T(8,128)(2,1)S(1)} %get-tuple-element.48), channel_id=1, source_target_pairs={{0,4},{1,5},{2,6},{3,7},{4,8},{5,9},{6,10},{7,11},{8,12},{9,13},{1... | collective-permute-start | bytes 2359304 | tf_op jit(solution)/shard_map/ppermute | solution.py:38
  63.3 2.2 %collective-permute-start.21 = (bf16[3,512,256]{2,1,0:T(8,128)(2,1)S(1)}, bf16[3,512,256]{2,1,0:T(8,128)(2,1)S(1)}, u32[]{:S(2)}, u32[]{:S(2)}) collective-permute-start(bf16[3,512,256]{2,1,0:T(8,128)(2,1)S(1)} %get-tuple-element.49), channel_id=1, source_target_pairs={{0,12},{1,13},{2,14},{3,15},{4,0},{5,1},{6,2},{7,3},{8,4},{9,5},{1... | collective-permute-start | bytes 2359304 | tf_op jit(solution)/shard_map/ppermute | solution.py:38
  65.5 3.2 %collective-permute-start.19 = (bf16[512,256]{1,0:T(8,128)(2,1)S(1)}, bf16[512,256]{1,0:T(8,128)(2,1)S(1)}, u32[]{:S(2)}, u32[]{:S(2)}) collective-permute-start(bf16[512,256]{1,0:T(8,128)(2,1)S(1)} %get-tuple-element.46), channel_id=1, source_target_pairs={{0,12},{1,13},{2,14},{3,15},{4,0},{5,1},{6,2},{7,3},{8,4},{9,5},{1... | collective-permute-start | bytes 786440 | tf_op jit(solution)/shard_map/ppermute | solution.py:38
  68.7 6.7 %collective-permute-done.20.refs_2_ = bf16[3,512,256]{2,1,0:T(8,128)(2,1)S(1)} collective-permute-done((bf16[3,512,256]{2,1,0:T(8,128)(2,1)S(1)}, bf16[3,512,256]{2,1,0:T(8,128)(2,1)S(1)}, u32[]{:S(2)}, u32[]{:S(2)}) %collective-permute-start.20) | collective-permute-done | bytes 786464 | tf_op jit(solution)/shard_map/ppermute | solution.py:38
  75.6 2.4 %collective-permute-start.22 = (bf16[512,256]{1,0:T(8,128)(2,1)S(1)}, bf16[512,256]{1,0:T(8,128)(2,1)S(1)}, u32[]{:S(2)}, u32[]{:S(2)}) collective-permute-start(bf16[512,256]{1,0:T(8,128)(2,1)S(1)} %get-tuple-element.50), channel_id=1, source_target_pairs={{0,2},{1,3},{2,0},{3,1},{4,6},{5,7},{6,4},{7,5},{8,10},{9,11},{10,... | collective-permute-start | bytes 786440 | tf_op jit(solution)/shard_map/ppermute | solution.py:33
  78.7 2.5 %collective-permute-start.24 = (bf16[512,256]{1,0:T(8,128)(2,1)S(1)}, bf16[512,256]{1,0:T(8,128)(2,1)S(1)}, u32[]{:S(2)}, u32[]{:S(2)}) collective-permute-start(bf16[512,256]{1,0:T(8,128)(2,1)S(1)} %get-tuple-element.52), channel_id=1, source_target_pairs={{0,3},{1,0},{2,1},{3,2},{4,7},{5,4},{6,5},{7,6},{8,11},{9,8},{10,9... | collective-permute-start | bytes 786440 | tf_op jit(solution)/shard_map/ppermute | solution.py:33
  81.2 2.4 %collective-permute-done.22.refs_3_ = bf16[512,256]{1,0:T(8,128)(2,1)S(1)} collective-permute-done((bf16[512,256]{1,0:T(8,128)(2,1)S(1)}, bf16[512,256]{1,0:T(8,128)(2,1)S(1)}, u32[]{:S(2)}, u32[]{:S(2)}) %collective-permute-start.22) | collective-permute-done | bytes 262176 | tf_op jit(solution)/shard_map/ppermute | solution.py:33
  83.7 2.7 %collective-permute-done.23.refs_4_ = bf16[512,256]{1,0:T(8,128)(2,1)S(1)} collective-permute-done((bf16[512,256]{1,0:T(8,128)(2,1)S(1)}, bf16[512,256]{1,0:T(8,128)(2,1)S(1)}, u32[]{:S(2)}, u32[]{:S(2)}) %collective-permute-start.23) | collective-permute-done | bytes 262176 | tf_op jit(solution)/shard_map/ppermute | solution.py:33
  86.7 2.5 %collective-permute-start.27 = (bf16[512,256]{1,0:T(8,128)(2,1)S(1)}, bf16[512,256]{1,0:T(8,128)(2,1)S(1)}, u32[]{:S(2)}, u32[]{:S(2)}) collective-permute-start(bf16[512,256]{1,0:T(8,128)(2,1)S(1)} %get-tuple-element.53.refs_0_), channel_id=1, source_target_pairs={{0,3},{1,0},{2,1},{3,2},{4,7},{5,4},{6,5},{7,6},{8,11},{9,8},{10,9... | collective-permute-start | bytes 786440 | tf_op jit(solution)/shard_map/ppermute | solution.py:33
  90.2 5.7 %collective-permute-done.27.refs_0_ = bf16[512,256]{1,0:T(8,128)(2,1)S(1)} collective-permute-done((bf16[512,256]{1,0:T(8,128)(2,1)S(1)}, bf16[512,256]{1,0:T(8,128)(2,1)S(1)}, u32[]{:S(2)}, u32[]{:S(2)}) %collective-permute-start.27) | collective-permute-done | bytes 262176 | tf_op jit(solution)/shard_map/ppermute | solution.py:33
  95.9 1.2 collective-permute-done.28.refs_1_
  97.2 3.4 %collective-permute-start.31 = (bf16[2,512,256]{2,1,0:T(8,128)(2,1)S(1)}, bf16[2,512,256]{2,1,0:T(8,128)(2,1)S(1)}, u32[]{:S(2)}, u32[]{:S(2)}) collective-permute-start(bf16[2,512,256]{2,1,0:T(8,128)(2,1)S(1)} %pair.7.refs_2_.refs_10_), channel_id=1, source_target_pairs={{0,12},{1,13},{2,14},{3,15},{4,0},{5,1},{6,2},{7,3},{8,4},{9,5},{1... | collective-permute-start | bytes 1572872 | tf_op jit(solution)/shard_map/ppermute | solution.py:38
  100.6 1.5 %collective-permute-start.26 = (bf16[2,512,256]{2,1,0:T(8,128)(2,1)S(1)}, bf16[2,512,256]{2,1,0:T(8,128)(2,1)S(1)}, u32[]{:S(2)}, u32[]{:S(2)}) collective-permute-start(bf16[2,512,256]{2,1,0:T(8,128)(2,1)S(1)} %pair.6.refs_1_.refs_9_), channel_id=1, source_target_pairs={{0,4},{1,5},{2,6},{3,7},{4,8},{5,9},{6,10},{7,11},{8,12},{9,13},{1... | collective-permute-start | bytes 1572872 | tf_op jit(solution)/shard_map/ppermute | solution.py:38
  102.1 2.7 %collective-permute-start.29 = (bf16[2,512,256]{2,1,0:T(8,128)(2,1)S(1)}, bf16[2,512,256]{2,1,0:T(8,128)(2,1)S(1)}, u32[]{:S(2)}, u32[]{:S(2)}) collective-permute-start(bf16[2,512,256]{2,1,0:T(8,128)(2,1)S(1)} %pair.7.refs_2_.refs_10_), channel_id=1, source_target_pairs={{0,4},{1,5},{2,6},{3,7},{4,8},{5,9},{6,10},{7,11},{8,12},{9,13},{1... | collective-permute-start | bytes 1572872 | tf_op jit(solution)/shard_map/ppermute | solution.py:38
  105.4 1.9 %collective-permute-done.31.refs_4_.refs_5_ = bf16[2,512,256]{2,1,0:T(8,128)(2,1)S(1)} collective-permute-done((bf16[2,512,256]{2,1,0:T(8,128)(2,1)S(1)}, bf16[2,512,256]{2,1,0:T(8,128)(2,1)S(1)}, u32[]{:S(2)}, u32[]{:S(2)}) %collective-permute-start.31) | collective-permute-done | bytes 524320 | tf_op jit(solution)/shard_map/ppermute | solution.py:38
  107.2 3.7 %collective-permute-start.33 = (bf16[2,512,256]{2,1,0:T(8,128)(2,1)S(1)}, bf16[2,512,256]{2,1,0:T(8,128)(2,1)S(1)}, u32[]{:S(2)}, u32[]{:S(2)}) collective-permute-start(bf16[2,512,256]{2,1,0:T(8,128)(2,1)S(1)} %collective-permute-done.31.refs_4_.refs_5_), channel_id=1, source_target_pairs={{0,12},{1,13},{2,14},{3,15},{4,0},{5,1},{6,2},{7,3},{8,4},{9,5},{1... | collective-permute-start | bytes 1572872 | tf_op jit(solution)/shard_map/ppermute | solution.py:38
  111.6 1.8 %code_grad.2.refs_6_ = f32[4,512,256]{2,1,0:T(8,128)S(1)} custom-call(s32[128]{0:T(128)S(1)} %fusion.refs_2_.refs_0_.refs_1_.refs_6_.refs_4_.refs_8_, bf16[2,512,256]{2,1,0:T(8,128)(2,1)S(1)} %pair.6.refs_1_.refs_9_, bf16[2,512,256]{2,1,0:T(8,128)(2,1)S(1)} %pair.7.refs_2_.refs_10_, bf16[1024,4096]{1,0:T(8,128)(2,1)S(1)} %bitcast.16), custom_call_target="tpu_custom_call" | custom-call | flops 1 | bytes 1 | tf_op jit(solution)/shard_map/code_grad/pallas_call | solution.py:65
  113.4 3.3 %collective-permute-done.29.refs_2_.refs_3_ = bf16[2,512,256]{2,1,0:T(8,128)(2,1)S(1)} collective-permute-done((bf16[2,512,256]{2,1,0:T(8,128)(2,1)S(1)}, bf16[2,512,256]{2,1,0:T(8,128)(2,1)S(1)}, u32[]{:S(2)}, u32[]{:S(2)}) %collective-permute-start.29) | collective-permute-done | bytes 524320 | tf_op jit(solution)/shard_map/ppermute | solution.py:38
  116.7 5.1 %middle.1 = (f32[4,512,256]{2,1,0:T(8,128)S(1)}, bf16[1024,4096]{1,0:T(8,128)(2,1)}, f32[512,256]{1,0:T(8,128)}) custom-call(s32[128]{0:T(128)S(1)} %fusion.refs_2_.refs_0_.refs_1_.refs_6_.refs_4_.refs_8_, bf16[2,512,256]{2,1,0:T(8,128)(2,1)S(1)} %collective-permute-done.26.refs_1_.refs_2_, bf16[2,512,256]{2,1,0:T(8,128)(2,1)S(1)} %collective-permute-done.29.refs_2_.refs_3_, ...), custom_call_target="tpu_custom_call" | custom-call | flops 1 | bytes 1 | tf_op jit(solution)/shard_map/middle/pallas_call | solution.py:65
  122.3 1.8 %code_grad.3 = (f32[4,512,128]{2,1,0:T(8,128)S(1)}, bf16[4,512,128]{2,1,0:T(8,128)(2,1)S(1)}) custom-call(s32[128]{0:T(128)S(1)} %fusion.refs_2_.refs_0_.refs_1_.refs_6_.refs_4_.refs_8_, bf16[2,512,256]{2,1,0:T(8,128)(2,1)S(1)} %collective-permute-done.32.refs_1_.refs_6_, bf16[2,512,256]{2,1,0:T(8,128)(2,1)S(1)} %collective-permute-done.33.refs_2_.refs_7_, ...), custom_call_target="tpu_custom_call" | custom-call | flops 1 | bytes 1 | tf_op jit(solution)/shard_map/code_grad/pallas_call | solution.py:65
  124.3 1.9 %collective-permute-done.34.refs_1_ = bf16[4,512,128]{2,1,0:T(8,128)(2,1)S(1)} collective-permute-done((bf16[4,512,128]{2,1,0:T(8,128)(2,1)S(1)}, bf16[4,512,128]{2,1,0:T(8,128)(2,1)S(1)}, u32[]{:S(2)}, u32[]{:S(2)}) %collective-permute-start.34) | collective-permute-done | bytes 524320 | tf_op jit(solution)/shard_map/ppermute | solution.py:46
  126.2 1.3 collective-permute-start.35
  127.5 1.3 collective-permute-start.36
  128.8 1.3 collective-permute-start.37
  130.2 5.3 %decoder_grad.1 = bf16[1024,4096]{1,0:T(8,128)(2,1)} custom-call(s32[128]{0:T(128)S(1)} %fusion.refs_2_.refs_0_.refs_1_.refs_6_.refs_4_.refs_8_, bf16[1024,512]{1,0:T(8,128)(2,1)S(1)} %get-tuple-element.54.refs_7_.refs_1_, bf16[2,512,256]{2,1,0:T(8,128)(2,1)S(1)} %collective-permute-done.26.refs_1_.refs_2_, ...), custom_call_target="tpu_custom_call", output_to_operand_aliasing={{}: (8, {})} | custom-call | flops 1 | bytes 1 | tf_op jit(solution)/shard_map/decoder_grad/pallas_call | solution.py:65
  136.5 2.8 %collective-permute-done.37.refs_5_ = bf16[512,128]{1,0:T(8,128)(2,1)S(1)} collective-permute-done((bf16[512,128]{1,0:T(8,128)(2,1)S(1)}, bf16[512,128]{1,0:T(8,128)(2,1)S(1)}, u32[]{:S(2)}, u32[]{:S(2)}) %collective-permute-start.37) | collective-permute-done | bytes 131104 | tf_op jit(solution)/shard_map/ppermute | solution.py:42
  139.3 2.1 %encoder_grad.1 = f32[4096,128]{1,0:T(8,128)} custom-call(bf16[4096,512]{1,0:T(8,128)(2,1)S(1)} %flip.1.refs_7_.refs_0_, f32[512,128]{1,0:T(8,128)S(1)} %prepare.1.refs_4_.refs_1_, f32[512,128]{1,0:T(8,128)S(1)} %get-tuple-element.62.refs_2_, bf16[512,128]{1,0:T(8,128)(2,1)S(1)} %collective-permute-done.35.refs_3_, ...), custom_call_target="tpu_custom_call" | custom-call | flops 1 | bytes 1 | tf_op jit(solution)/shard_map/encoder_grad/pallas_call | solution.py:65
  (66 shorter events, 15.2 us)
Async XLA Ops:
  0.6 7.6 %copy-start = (s32[1,512,256]{2,1,0:T(8,128)S(1)}, s32[1,512,256]{2,1,0:T(8,128)}, u32[]{:S(2)}) copy-start(s32[1,512,256]{2,1,0:T(8,128)} %param.11) | copy-start | bytes 1572868
  0.6 28.3 %copy-start.4 = (bf16[1,4096,128]{2,1,0:T(8,128)(2,1)S(1)}, bf16[1,4096,128]{2,1,0:T(8,128)(2,1)}, u32[]{:S(2)}) copy-start(bf16[1,4096,128]{2,1,0:T(8,128)(2,1)} %param.9) | copy-start | bytes 3145732
  0.7 7.9 %collective-permute-start = (bf16[512,256]{1,0:T(8,128)(2,1)}, bf16[512,256]{1,0:T(8,128)(2,1)S(1)}, u32[]{:S(2)}, u32[]{:S(2)}) collective-permute-start(bf16[512,256]{1,0:T(8,128)(2,1)} %bitcast.20), channel_id=1, source_target_pairs={{0,1},{1,2},{2,3},{3,0},{4,5},{5,6},{6,7},{7,4},{8,9},{9,10},{10,1... | collective-permute-start | bytes 786440 | tf_op jit(solution)/shard_map/ppermute | solution.py:33
  2.3 9.3 %collective-permute-start.3 = (bf16[512,256]{1,0:T(8,128)(2,1)}, bf16[512,256]{1,0:T(8,128)(2,1)S(1)}, u32[]{:S(2)}, u32[]{:S(2)}) collective-permute-start(bf16[512,256]{1,0:T(8,128)(2,1)} %bitcast.21), channel_id=1, source_target_pairs={{0,3},{1,0},{2,1},{3,2},{4,7},{5,4},{6,5},{7,6},{8,11},{9,8},{10,9... | collective-permute-start | bytes 786440 | tf_op jit(solution)/shard_map/ppermute | solution.py:33
  4.0 8.4 %collective-permute-start.4 = (bf16[512,256]{1,0:T(8,128)(2,1)}, bf16[512,256]{1,0:T(8,128)(2,1)S(1)}, u32[]{:S(2)}, u32[]{:S(2)}) collective-permute-start(bf16[512,256]{1,0:T(8,128)(2,1)} %bitcast.22), channel_id=1, source_target_pairs={{0,2},{1,3},{2,0},{3,1},{4,6},{5,7},{6,4},{7,5},{8,10},{9,11},{10,... | collective-permute-start | bytes 786440 | tf_op jit(solution)/shard_map/ppermute | solution.py:33
  8.5 1.0 copy-start.5
  9.5 11.3 %collective-permute-start.1 = (bf16[2,512,256]{2,1,0:T(8,128)(2,1)S(1)}, bf16[2,512,256]{2,1,0:T(8,128)(2,1)S(1)}, u32[]{:S(2)}, u32[]{:S(2)}) collective-permute-start(bf16[2,512,256]{2,1,0:T(8,128)(2,1)S(1)} %pair.4.refs_1_), channel_id=1, source_target_pairs={{0,4},{1,5},{2,6},{3,7},{4,8},{5,9},{6,10},{7,11},{8,12},{9,13},{1... | collective-permute-start | bytes 1572872 | tf_op jit(solution)/shard_map/ppermute | solution.py:38
  12.5 10.9 %collective-permute-start.5 = (bf16[2,512,256]{2,1,0:T(8,128)(2,1)S(1)}, bf16[2,512,256]{2,1,0:T(8,128)(2,1)S(1)}, u32[]{:S(2)}, u32[]{:S(2)}) collective-permute-start(bf16[2,512,256]{2,1,0:T(8,128)(2,1)S(1)} %pair.5.refs_2_), channel_id=1, source_target_pairs={{0,12},{1,13},{2,14},{3,15},{4,0},{5,1},{6,2},{7,3},{8,4},{9,5},{1... | collective-permute-start | bytes 1572872 | tf_op jit(solution)/shard_map/ppermute | solution.py:38
  16.7 12.3 %collective-permute-start.8 = (bf16[2,512,256]{2,1,0:T(8,128)(2,1)S(1)}, bf16[2,512,256]{2,1,0:T(8,128)(2,1)S(1)}, u32[]{:S(2)}, u32[]{:S(2)}) collective-permute-start(bf16[2,512,256]{2,1,0:T(8,128)(2,1)S(1)} %pair.4.refs_1_), channel_id=1, source_target_pairs={{0,12},{1,13},{2,14},{3,15},{4,0},{5,1},{6,2},{7,3},{8,4},{9,5},{1... | collective-permute-start | bytes 1572872 | tf_op jit(solution)/shard_map/ppermute | solution.py:38
  17.1 11.9 %collective-permute-start.7 = (bf16[2,512,256]{2,1,0:T(8,128)(2,1)S(1)}, bf16[2,512,256]{2,1,0:T(8,128)(2,1)S(1)}, u32[]{:S(2)}, u32[]{:S(2)}) collective-permute-start(bf16[2,512,256]{2,1,0:T(8,128)(2,1)S(1)} %pair.5.refs_2_), channel_id=1, source_target_pairs={{0,4},{1,5},{2,6},{3,7},{4,8},{5,9},{6,10},{7,11},{8,12},{9,13},{1... | collective-permute-start | bytes 1572872 | tf_op jit(solution)/shard_map/ppermute | solution.py:38
  20.9 13.3 %collective-permute-start.2 = (bf16[2,512,256]{2,1,0:T(8,128)(2,1)S(1)}, bf16[2,512,256]{2,1,0:T(8,128)(2,1)S(1)}, u32[]{:S(2)}, u32[]{:S(2)}) collective-permute-start(bf16[2,512,256]{2,1,0:T(8,128)(2,1)S(1)} %collective-permute-done.1.refs_3_), channel_id=1, source_target_pairs={{0,4},{1,5},{2,6},{3,7},{4,8},{5,9},{6,10},{7,11},{8,12},{9,13},{1... | collective-permute-start | bytes 1572872 | tf_op jit(solution)/shard_map/ppermute | solution.py:38
  23.4 11.2 %collective-permute-start.6 = (bf16[2,512,256]{2,1,0:T(8,128)(2,1)S(1)}, bf16[2,512,256]{2,1,0:T(8,128)(2,1)S(1)}, u32[]{:S(2)}, u32[]{:S(2)}) collective-permute-start(bf16[2,512,256]{2,1,0:T(8,128)(2,1)S(1)} %collective-permute-done.5.refs_6_), channel_id=1, source_target_pairs={{0,12},{1,13},{2,14},{3,15},{4,0},{5,1},{6,2},{7,3},{8,4},{9,5},{1... | collective-permute-start | bytes 1572872 | tf_op jit(solution)/shard_map/ppermute | solution.py:38
  29.0 3.4 %copy-start.2 = (bf16[8,1,128,4096]{3,2,1,0:T(8,128)(2,1)S(1)}, bf16[8,1,128,4096]{3,2,1,0:T(8,128)(2,1)}, u32[]{:S(2)}) copy-start(bf16[8,1,128,4096]{3,2,1,0:T(8,128)(2,1)} %param.12) | copy-start | bytes 25165828
  32.4 2.2 %copy-start.6 = (f32[1,128]{1,0:T(1,128)S(1)}, f32[1,128]{1,0:T(1,128)}, u32[]{:S(2)}) copy-start(f32[1,128]{1,0:T(1,128)} %refs_5_.1) | copy-start | bytes 1540
  32.4 22.3 %copy-start.3 = (bf16[8,1,128,4096]{3,2,1,0:T(8,128)(2,1)S(1)}, bf16[8,1,128,4096]{3,2,1,0:T(8,128)(2,1)}, u32[]{:S(2)}) copy-start(bf16[8,1,128,4096]{3,2,1,0:T(8,128)(2,1)} %param.12) | copy-start | bytes 25165828
  35.1 9.7 %collective-permute-start.9 = (bf16[512,128]{1,0:T(8,128)(2,1)S(1)}, bf16[512,128]{1,0:T(8,128)(2,1)S(1)}, u32[]{:S(2)}, u32[]{:S(2)}) collective-permute-start(bf16[512,128]{1,0:T(8,128)(2,1)S(1)} %activate.1.refs_1_), channel_id=1, source_target_pairs={{0,32},{1,33},{2,34},{3,35},{4,36},{5,37},{6,38},{7,39},{8,40},{9,... | collective-permute-start | bytes 393224 | tf_op jit(solution)/shard_map/ppermute | solution.py:42
  38.5 7.3 %collective-permute-start.10 = (bf16[512,128]{1,0:T(8,128)(2,1)S(1)}, bf16[512,128]{1,0:T(8,128)(2,1)S(1)}, u32[]{:S(2)}, u32[]{:S(2)}) collective-permute-start(bf16[512,128]{1,0:T(8,128)(2,1)S(1)} %activate.1.refs_1_), channel_id=1, source_target_pairs={{0,64},{1,65},{2,66},{3,67},{4,68},{5,69},{6,70},{7,71},{8,72},{9,... | collective-permute-start | bytes 393224 | tf_op jit(solution)/shard_map/ppermute | solution.py:42
  43.4 3.8 %collective-permute-start.11 = (bf16[512,128]{1,0:T(8,128)(2,1)S(1)}, bf16[512,128]{1,0:T(8,128)(2,1)S(1)}, u32[]{:S(2)}, u32[]{:S(2)}) collective-permute-start(bf16[512,128]{1,0:T(8,128)(2,1)S(1)} %activate.1.refs_1_), channel_id=1, source_target_pairs={{0,96},{1,97},{2,98},{3,99},{4,100},{5,101},{6,102},{7,103},{8,104... | collective-permute-start | bytes 393224 | tf_op jit(solution)/shard_map/ppermute | solution.py:42
  44.7 2.5 %collective-permute-start.12 = (bf16[512,128]{1,0:T(8,128)(2,1)S(1)}, bf16[512,128]{1,0:T(8,128)(2,1)S(1)}, u32[]{:S(2)}, u32[]{:S(2)}) collective-permute-start(bf16[512,128]{1,0:T(8,128)(2,1)S(1)} %activate.1.refs_1_), channel_id=1, source_target_pairs={{0,16},{1,17},{2,18},{3,19},{4,20},{5,21},{6,22},{7,23},{8,24},{9,... | collective-permute-start | bytes 393224 | tf_op jit(solution)/shard_map/ppermute | solution.py:46
  44.8 2.4 %collective-permute-start.13 = (bf16[512,128]{1,0:T(8,128)(2,1)S(1)}, bf16[512,128]{1,0:T(8,128)(2,1)S(1)}, u32[]{:S(2)}, u32[]{:S(2)}) collective-permute-start(bf16[512,128]{1,0:T(8,128)(2,1)S(1)} %collective-permute-done.9.refs_2_), channel_id=1, source_target_pairs={{0,16},{1,17},{2,18},{3,19},{4,20},{5,21},{6,22},{7,23},{8,24},{9,... | collective-permute-start | bytes 393224 | tf_op jit(solution)/shard_map/ppermute | solution.py:46
  45.9 1.3 collective-permute-start.14
  47.2 1.3 collective-permute-start.15
  50.7 10.9 %collective-permute-start.16 = (bf16[2,512,256]{2,1,0:T(8,128)(2,1)S(1)}, bf16[2,512,256]{2,1,0:T(8,128)(2,1)S(1)}, u32[]{:S(2)}, u32[]{:S(2)}) collective-permute-start(bf16[2,512,256]{2,1,0:T(8,128)(2,1)S(1)} %get-tuple-element.38.refs_3_), channel_id=1, source_target_pairs={{0,4},{1,5},{2,6},{3,7},{4,8},{5,9},{6,10},{7,11},{8,12},{9,13},{1... | collective-permute-start | bytes 1572872 | tf_op jit(solution)/shard_map/ppermute | solution.py:38
  51.0 10.6 %collective-permute-start.17 = (bf16[2,512,256]{2,1,0:T(8,128)(2,1)S(1)}, bf16[2,512,256]{2,1,0:T(8,128)(2,1)S(1)}, u32[]{:S(2)}, u32[]{:S(2)}) collective-permute-start(bf16[2,512,256]{2,1,0:T(8,128)(2,1)S(1)} %get-tuple-element.44), channel_id=1, source_target_pairs={{0,12},{1,13},{2,14},{3,15},{4,0},{5,1},{6,2},{7,3},{8,4},{9,5},{1... | collective-permute-start | bytes 1572872 | tf_op jit(solution)/shard_map/ppermute | solution.py:38
  61.8 13.5 %collective-permute-start.20 = (bf16[3,512,256]{2,1,0:T(8,128)(2,1)S(1)}, bf16[3,512,256]{2,1,0:T(8,128)(2,1)S(1)}, u32[]{:S(2)}, u32[]{:S(2)}) collective-permute-start(bf16[3,512,256]{2,1,0:T(8,128)(2,1)S(1)} %get-tuple-element.48), channel_id=1, source_target_pairs={{0,4},{1,5},{2,6},{3,7},{4,8},{5,9},{6,10},{7,11},{8,12},{9,13},{1... | collective-permute-start | bytes 2359304 | tf_op jit(solution)/shard_map/ppermute | solution.py:38
  63.3 12.0 %collective-permute-start.21 = (bf16[3,512,256]{2,1,0:T(8,128)(2,1)S(1)}, bf16[3,512,256]{2,1,0:T(8,128)(2,1)S(1)}, u32[]{:S(2)}, u32[]{:S(2)}) collective-permute-start(bf16[3,512,256]{2,1,0:T(8,128)(2,1)S(1)} %get-tuple-element.49), channel_id=1, source_target_pairs={{0,12},{1,13},{2,14},{3,15},{4,0},{5,1},{6,2},{7,3},{8,4},{9,5},{1... | collective-permute-start | bytes 2359304 | tf_op jit(solution)/shard_map/ppermute | solution.py:38
  65.5 15.7 %collective-permute-start.18 = (bf16[512,256]{1,0:T(8,128)(2,1)S(1)}, bf16[512,256]{1,0:T(8,128)(2,1)S(1)}, u32[]{:S(2)}, u32[]{:S(2)}) collective-permute-start(bf16[512,256]{1,0:T(8,128)(2,1)S(1)} %get-tuple-element.45), channel_id=1, source_target_pairs={{0,4},{1,5},{2,6},{3,7},{4,8},{5,9},{6,10},{7,11},{8,12},{9,13},{1... | collective-permute-start | bytes 786440 | tf_op jit(solution)/shard_map/ppermute | solution.py:38
  65.5 15.7 %collective-permute-start.19 = (bf16[512,256]{1,0:T(8,128)(2,1)S(1)}, bf16[512,256]{1,0:T(8,128)(2,1)S(1)}, u32[]{:S(2)}, u32[]{:S(2)}) collective-permute-start(bf16[512,256]{1,0:T(8,128)(2,1)S(1)} %get-tuple-element.46), channel_id=1, source_target_pairs={{0,12},{1,13},{2,14},{3,15},{4,0},{5,1},{6,2},{7,3},{8,4},{9,5},{1... | collective-permute-start | bytes 786440 | tf_op jit(solution)/shard_map/ppermute | solution.py:38
  75.6 8.0 %collective-permute-start.22 = (bf16[512,256]{1,0:T(8,128)(2,1)S(1)}, bf16[512,256]{1,0:T(8,128)(2,1)S(1)}, u32[]{:S(2)}, u32[]{:S(2)}) collective-permute-start(bf16[512,256]{1,0:T(8,128)(2,1)S(1)} %get-tuple-element.50), channel_id=1, source_target_pairs={{0,2},{1,3},{2,0},{3,1},{4,6},{5,7},{6,4},{7,5},{8,10},{9,11},{10,... | collective-permute-start | bytes 786440 | tf_op jit(solution)/shard_map/ppermute | solution.py:33
  78.0 8.4 %collective-permute-start.23 = (bf16[512,256]{1,0:T(8,128)(2,1)S(1)}, bf16[512,256]{1,0:T(8,128)(2,1)S(1)}, u32[]{:S(2)}, u32[]{:S(2)}) collective-permute-start(bf16[512,256]{1,0:T(8,128)(2,1)S(1)} %get-tuple-element.51), channel_id=1, source_target_pairs={{0,1},{1,2},{2,3},{3,0},{4,5},{5,6},{6,7},{7,4},{8,9},{9,10},{10,1... | collective-permute-start | bytes 786440 | tf_op jit(solution)/shard_map/ppermute | solution.py:33
  78.7 7.7 %collective-permute-start.24 = (bf16[512,256]{1,0:T(8,128)(2,1)S(1)}, bf16[512,256]{1,0:T(8,128)(2,1)S(1)}, u32[]{:S(2)}, u32[]{:S(2)}) collective-permute-start(bf16[512,256]{1,0:T(8,128)(2,1)S(1)} %get-tuple-element.52), channel_id=1, source_target_pairs={{0,3},{1,0},{2,1},{3,2},{4,7},{5,4},{6,5},{7,6},{8,11},{9,8},{10,9... | collective-permute-start | bytes 786440 | tf_op jit(solution)/shard_map/ppermute | solution.py:33
  86.7 9.2 %collective-permute-start.27 = (bf16[512,256]{1,0:T(8,128)(2,1)S(1)}, bf16[512,256]{1,0:T(8,128)(2,1)S(1)}, u32[]{:S(2)}, u32[]{:S(2)}) collective-permute-start(bf16[512,256]{1,0:T(8,128)(2,1)S(1)} %get-tuple-element.53.refs_0_), channel_id=1, source_target_pairs={{0,3},{1,0},{2,1},{3,2},{4,7},{5,4},{6,5},{7,6},{8,11},{9,8},{10,9... | collective-permute-start | bytes 786440 | tf_op jit(solution)/shard_map/ppermute | solution.py:33
  89.1 8.0 %collective-permute-start.28 = (bf16[512,256]{1,0:T(8,128)(2,1)S(1)}, bf16[512,256]{1,0:T(8,128)(2,1)S(1)}, u32[]{:S(2)}, u32[]{:S(2)}) collective-permute-start(bf16[512,256]{1,0:T(8,128)(2,1)S(1)} %get-tuple-element.53.refs_0_), channel_id=1, source_target_pairs={{0,2},{1,3},{2,0},{3,1},{4,6},{5,7},{6,4},{7,5},{8,10},{9,11},{10,... | collective-permute-start | bytes 786440 | tf_op jit(solution)/shard_map/ppermute | solution.py:33
  90.1 10.5 %collective-permute-start.25 = (bf16[512,256]{1,0:T(8,128)(2,1)S(1)}, bf16[512,256]{1,0:T(8,128)(2,1)S(1)}, u32[]{:S(2)}, u32[]{:S(2)}) collective-permute-start(bf16[512,256]{1,0:T(8,128)(2,1)S(1)} %get-tuple-element.53.refs_0_), channel_id=1, source_target_pairs={{0,1},{1,2},{2,3},{3,0},{4,5},{5,6},{6,7},{7,4},{8,9},{9,10},{10,1... | collective-permute-start | bytes 786440 | tf_op jit(solution)/shard_map/ppermute | solution.py:33
  97.2 10.1 %collective-permute-start.31 = (bf16[2,512,256]{2,1,0:T(8,128)(2,1)S(1)}, bf16[2,512,256]{2,1,0:T(8,128)(2,1)S(1)}, u32[]{:S(2)}, u32[]{:S(2)}) collective-permute-start(bf16[2,512,256]{2,1,0:T(8,128)(2,1)S(1)} %pair.7.refs_2_.refs_10_), channel_id=1, source_target_pairs={{0,12},{1,13},{2,14},{3,15},{4,0},{5,1},{6,2},{7,3},{8,4},{9,5},{1... | collective-permute-start | bytes 1572872 | tf_op jit(solution)/shard_map/ppermute | solution.py:38
  100.6 10.5 %collective-permute-start.26 = (bf16[2,512,256]{2,1,0:T(8,128)(2,1)S(1)}, bf16[2,512,256]{2,1,0:T(8,128)(2,1)S(1)}, u32[]{:S(2)}, u32[]{:S(2)}) collective-permute-start(bf16[2,512,256]{2,1,0:T(8,128)(2,1)S(1)} %pair.6.refs_1_.refs_9_), channel_id=1, source_target_pairs={{0,4},{1,5},{2,6},{3,7},{4,8},{5,9},{6,10},{7,11},{8,12},{9,13},{1... | collective-permute-start | bytes 1572872 | tf_op jit(solution)/shard_map/ppermute | solution.py:38
  102.1 14.6 %collective-permute-start.29 = (bf16[2,512,256]{2,1,0:T(8,128)(2,1)S(1)}, bf16[2,512,256]{2,1,0:T(8,128)(2,1)S(1)}, u32[]{:S(2)}, u32[]{:S(2)}) collective-permute-start(bf16[2,512,256]{2,1,0:T(8,128)(2,1)S(1)} %pair.7.refs_2_.refs_10_), channel_id=1, source_target_pairs={{0,4},{1,5},{2,6},{3,7},{4,8},{5,9},{6,10},{7,11},{8,12},{9,13},{1... | collective-permute-start | bytes 1572872 | tf_op jit(solution)/shard_map/ppermute | solution.py:38
  104.9 11.8 %collective-permute-start.30 = (bf16[2,512,256]{2,1,0:T(8,128)(2,1)S(1)}, bf16[2,512,256]{2,1,0:T(8,128)(2,1)S(1)}, u32[]{:S(2)}, u32[]{:S(2)}) collective-permute-start(bf16[2,512,256]{2,1,0:T(8,128)(2,1)S(1)} %pair.6.refs_1_.refs_9_), channel_id=1, source_target_pairs={{0,12},{1,13},{2,14},{3,15},{4,0},{5,1},{6,2},{7,3},{8,4},{9,5},{1... | collective-permute-start | bytes 1572872 | tf_op jit(solution)/shard_map/ppermute | solution.py:38
  107.2 14.5 %collective-permute-start.33 = (bf16[2,512,256]{2,1,0:T(8,128)(2,1)S(1)}, bf16[2,512,256]{2,1,0:T(8,128)(2,1)S(1)}, u32[]{:S(2)}, u32[]{:S(2)}) collective-permute-start(bf16[2,512,256]{2,1,0:T(8,128)(2,1)S(1)} %collective-permute-done.31.refs_4_.refs_5_), channel_id=1, source_target_pairs={{0,12},{1,13},{2,14},{3,15},{4,0},{5,1},{6,2},{7,3},{8,4},{9,5},{1... | collective-permute-start | bytes 1572872 | tf_op jit(solution)/shard_map/ppermute | solution.py:38
  111.1 11.2 %collective-permute-start.32 = (bf16[2,512,256]{2,1,0:T(8,128)(2,1)S(1)}, bf16[2,512,256]{2,1,0:T(8,128)(2,1)S(1)}, u32[]{:S(2)}, u32[]{:S(2)}) collective-permute-start(bf16[2,512,256]{2,1,0:T(8,128)(2,1)S(1)} %collective-permute-done.26.refs_1_.refs_2_), channel_id=1, source_target_pairs={{0,4},{1,5},{2,6},{3,7},{4,8},{5,9},{6,10},{7,11},{8,12},{9,13},{1... | collective-permute-start | bytes 1572872 | tf_op jit(solution)/shard_map/ppermute | solution.py:38
  124.2 2.0 %collective-permute-start.34 = (bf16[4,512,128]{2,1,0:T(8,128)(2,1)S(1)}, bf16[4,512,128]{2,1,0:T(8,128)(2,1)S(1)}, u32[]{:S(2)}, u32[]{:S(2)}) collective-permute-start(bf16[4,512,128]{2,1,0:T(8,128)(2,1)S(1)} %get-tuple-element.60), channel_id=1, source_target_pairs={{0,16},{1,17},{2,18},{3,19},{4,20},{5,21},{6,22},{7,23},{8,24},{9,... | collective-permute-start | bytes 1572872 | tf_op jit(solution)/shard_map/ppermute | solution.py:46
  126.2 9.2 %collective-permute-start.35 = (bf16[512,128]{1,0:T(8,128)(2,1)S(1)}, bf16[512,128]{1,0:T(8,128)(2,1)S(1)}, u32[]{:S(2)}, u32[]{:S(2)}) collective-permute-start(bf16[512,128]{1,0:T(8,128)(2,1)S(1)} %get-tuple-element.61.refs_9_), channel_id=1, source_target_pairs={{32,0},{33,1},{34,2},{35,3},{36,4},{37,5},{38,6},{39,7},{40,8},{41... | collective-permute-start | bytes 393224 | tf_op jit(solution)/shard_map/ppermute | solution.py:42
  127.5 8.9 %collective-permute-start.36 = (bf16[512,128]{1,0:T(8,128)(2,1)S(1)}, bf16[512,128]{1,0:T(8,128)(2,1)S(1)}, u32[]{:S(2)}, u32[]{:S(2)}) collective-permute-start(bf16[512,128]{1,0:T(8,128)(2,1)S(1)} %get-tuple-element.63), channel_id=1, source_target_pairs={{64,0},{65,1},{66,2},{67,3},{68,4},{69,5},{70,6},{71,7},{72,8},{73... | collective-permute-start | bytes 393224 | tf_op jit(solution)/shard_map/ppermute | solution.py:42
  128.8 10.4 %collective-permute-start.37 = (bf16[512,128]{1,0:T(8,128)(2,1)S(1)}, bf16[512,128]{1,0:T(8,128)(2,1)S(1)}, u32[]{:S(2)}, u32[]{:S(2)}) collective-permute-start(bf16[512,128]{1,0:T(8,128)(2,1)S(1)} %get-tuple-element.64), channel_id=1, source_target_pairs={{96,0},{97,1},{98,2},{99,3},{100,4},{101,5},{102,6},{103,7},{104,8... | collective-permute-start | bytes 393224 | tf_op jit(solution)/shard_map/ppermute | solution.py:42
  130.1 11.3 %copy-start.1 = (s32[1,512,256]{2,1,0:T(8,128)S(1)}, s32[1,512,256]{2,1,0:T(8,128)}, u32[]{:S(2)}) copy-start(s32[1,512,256]{2,1,0:T(8,128)} %param.11) | copy-start | bytes 1572868

commit v5 on v4

--- a/solution.py
+++ b/solution.py
@@ -88,9 +88,15 @@
     n = len(pairs)
 
     def kernel(sc, *refs):
-        w, d, out, rows, far = refs[n:]
-        for i in range(4):
-            far[i] = d[:, columns(sc, 12 + i)]
+        w, d, out, rows, far, live = refs[n:]
+        y, c = sc[16], sc[17]
+        for o in range(4):
+            for half, parity in enumerate((c, 1 - c)):
+                source = pl.ds(pl.multiple_of(((y - o) & 3) * 256 + parity * 128, 128), 128)
+                at = o * 256 + half * 128
+                for i in range(4):
+                    far[i, at:at + 128, :] = d[source, columns(sc, 12 + i)]
+        live[...] = jnp.where(c == 1, jnp.ones((8, 128), F32), jnp.zeros((8, 128), F32))
         left = jnp.concatenate([refs[i][k] for i in range(n) for k in range(2)], axis=1)
         right = jnp.concatenate([w[columns(sc, i), :] for i in range(2 * n)], axis=0)
         out[...] = dot(left, right)
@@ -99,8 +105,8 @@
 
     rest = 4096 - n * 512
     return call(
-        kernel, scalars, [*pairs, weight, dec], (shape((TOK, 128), F32), shape((rest, 128), BF16), shape((4, 1024, 256), BF16)),
-        (VMEM_SPEC,) * 3, name="encode",
+        kernel, scalars, [*pairs, weight, dec], (shape((TOK, 128), F32), shape((rest, 128), BF16), shape((4, 1024, 256), BF16), shape((8, 128), F32)),
+        (VMEM_SPEC,) * 4, name="encode",
     )
 
 
@@ -117,7 +123,22 @@
     )
 
 
-def assemble(scalars, mine, other):
+def by_distance(scalars, mine, other, live):
+    def kernel(sc, *refs):
+        acts, alive = refs[-1], refs[-2][0:1, :]
+        for o in range(4):
+            acts[:, o * 256:o * 256 + 128] = refs[o][...]
+            b = refs[4 + o][...]
+            if o == 0:
+                b = (b.astype(F32) * alive).astype(BF16)
+            acts[:, o * 256 + 128:o * 256 + 256] = b
+
+    return call(
+        kernel, None, [*mine, *other, live], shape((TOK, 1024), BF16), VMEM_SPEC, name="by_distance", after=(scalars,),
+    )
+
+
+def assemble(scalars, mine, other, after):
     def kernel(sc, *refs):
         acts, acts_t = refs[-2:]
         y, c = sc[16], sc[17]
@@ -132,7 +153,7 @@
 
     return call(
         kernel, scalars, [*mine, *other], (shape((TOK, 1024), BF16), shape((1024, TOK), BF16)), (VMEM_SPEC, VMEM_SPEC),
-        moved=4 * 1048576, name="assemble",
+        name="assemble", after=after,
     )
 
 
@@ -216,7 +237,11 @@
         for k in range(4):
             rows = slice(k * 256, k * 256 + 256)
             right = jnp.concatenate([w[rows, columns(sc, 2 * first + i)] for i in range(2 * n)], axis=1)
-            acc[k] = before[k] + lax.dot_general(left, right, (((1,), (1,)), ((), ())), preferred_element_type=F32)
+            both = before[k] + lax.dot_general(left, right, (((1,), (1,)), ((), ())), preferred_element_type=F32)
+            y, c = sc[16], sc[17]
+            even, odd = both[:, :128], both[:, 128:]
+            acc[(y - k) & 3, :, :128] = jnp.where(c == 0, even, odd)
+            acc[(y - k) & 3, :, 128:] = jnp.where(c == 0, odd, even)
         copies = write_columns(sc, a, rest[:m], 0, out, blocks, sems)
         copy.wait()
         for copy_out in copies:
@@ -276,6 +301,27 @@
     )
 
 
+def close(scalars, pairs, far, total, live):
+    n = len(pairs)
+
+    def kernel(sc, *refs):
+        w, before, alive, keep, send = refs[n:]
+        left = jnp.concatenate([refs[i][k] for i in range(n) for k in range(2)], axis=1)
+        for o in range(4):
+            right = jnp.concatenate([w[i, o * 256:o * 256 + 256, :] for i in range(2 * n)], axis=1)
+            acc = before[o] + lax.dot_general(left, right, (((1,), (1,)), ((), ())), preferred_element_type=F32)
+            keep[o] = acc[:, :128]
+            rest = acc[:, 128:]
+            if o == 0:
+                rest = rest * alive[0:1, :]
+            send[o] = rest.astype(BF16)
+
+    return call(
+        kernel, None, [*pairs, far, total, live], (shape((4, TOK, 128), F32), shape((4, TOK, 128), BF16)), (VMEM_SPEC,) * 2,
+        name="close", after=(scalars,),
+    )
+
+
 def flip(scalars, pairs, after):
     n = len(pairs)
 
@@ -388,14 +434,14 @@
     v1, v2 = long(v, 1), long(v, -1)
     inputs = (u, v, u1, v1, u2, v2, long(u1, 1), long(v2, -1))
 
-    early, rows, far = encode(scalars, inputs[:6], enc_weight[0], dec)
+    early, rows, far, live = encode(scalars, inputs[:6], enc_weight[0], dec)
     act = activate(scalars, inputs[6:], rows, early, gates, enc_bias)
 
     mine = [act] + [chips_y(act, o) for o in (1, 2, 3)]
     other = [other_core(m) for m in mine]
-    acts, acts_t = assemble(scalars, mine, other)
-
-    u_opp, v_opp = decode_far(scalars, acts, far)
+
+    u_opp, v_opp = decode_far(scalars, by_distance(scalars, mine, other, live), far)
+    acts, acts_t = assemble(scalars, mine, other, (u_opp,))
     from_left, from_right = long(u_opp, 1), long(v_opp, -1)
     sums = decode(scalars, acts, dec, (4, 5, 2, 3, 0, 1), (F32, BF16, BF16, F32, F32, F32), after=(u_opp,))
     flipped = flip(scalars, inputs, after=(sums[0],))
@@ -414,7 +460,7 @@
     u3, v3 = long(u1, 1), long(v2, -1)
     code, = code_grad(scalars, [u, v], 0, dec, None, False)
     code, dec_out, rebuilt = middle(scalars, [u1, v1, u2, v2], 2, dec, code, acts_t, [u, v], value)
-    keep, send = code_grad(scalars, [u3, v3], 6, dec, code, True)
+    keep, send = close(scalars, [u3, v3], far, code, live)
     own, *down = split(scalars, keep, other_core(send))
     back = [chips_y(part, -o) for o, part in zip((1, 2, 3), down)]
     dec_out = decoder_grad(scalars, acts_t, [u1, v1, u2, v2, u3, v3], 2, dec_out, after=(down[0],))

time: 142 us -> 141 us (level)
    pallas_call x20 -> x21, Pallas kernels: 28.9 us -> 28.5 us  [call(): pl.pallas_call(body, grid_spec=pltpu.PrefetchScalarGridSpec(num_scalar_pr...]
  transfers between devices with their start and end apart: 38 -> 38, of which waited for: 22 -> 22; matrix products, arithmetic and copies ran while one was open for 2% -> 2% of each run, Pallas kernels for 15% -> 16%
where the time goes in v5:
time: 141 us
  starting transfers between devices  63.9 us (45%)
  waiting for transfers between devices  40.3 us (29%)
  Pallas kernels  28.5 us (20%)
  local copies, waits for them, and re-layouts  6.84 us (5%)
    ppermute x18, starting transfers between devices, long(): return lax.ppermute(value, AXES, pairs_of(move))  35.2 us
    pallas_call x21, Pallas kernels, call(): pl.pallas_call(body, grid_spec=pltpu.PrefetchScalarGridSpec(num_scalar_pr...  28.5 us
    ppermute x18, waiting for transfers between devices, long(): return lax.ppermute(value, AXES, pairs_of(move))  18.2 us
    ppermute x9, starting transfers between devices, short(): return lax.ppermute(value, AXES, pairs_of(move))  14.3 us
    ppermute x6, starting transfers between devices, chips_y(): lax.ppermute(value, AXES, pairs_of(lambda y, c, z, x: (y + step, c, z, x)))  13.7 us
    ppermute x9, waiting for transfers between devices, short(): return lax.ppermute(value, AXES, pairs_of(move))  13.1 us
    ppermute x6, waiting for transfers between devices, chips_y(): lax.ppermute(value, AXES, pairs_of(lambda y, c, z, x: (y + step, c, z, x)))  5.72 us
    unnamed x14, local copies, waits for them, and re-layouts  4.36 us
  transfers between devices with their start and end apart: 38, of which 22 were waited for; matrix products, arithmetic and copies ran while one was open for 2% of the time, Pallas kernels for 16%

profile of v5, /device:TPU:0, one launch (start us, length us, event | category | flops | bytes accessed | tf_op | source)
XLA Modules:
  0.0 140.7 jit_solution(12168660478540986482)
XLA Ops:
  0.7 1.6 %collective-permute-start = (bf16[512,256]{1,0:T(8,128)(2,1)}, bf16[512,256]{1,0:T(8,128)(2,1)S(1)}, u32[]{:S(2)}, u32[]{:S(2)}) collective-permute-start(bf16[512,256]{1,0:T(8,128)(2,1)} %bitcast.19), channel_id=1, source_target_pairs={{0,1},{1,2},{2,3},{3,0},{4,5},{5,6},{6,7},{7,4},{8,9},{9,10},{10,1... | collective-permute-start | bytes 786440 | tf_op jit(solution)/shard_map/ppermute | solution.py:33
  2.3 1.7 %collective-permute-start.3 = (bf16[512,256]{1,0:T(8,128)(2,1)}, bf16[512,256]{1,0:T(8,128)(2,1)S(1)}, u32[]{:S(2)}, u32[]{:S(2)}) collective-permute-start(bf16[512,256]{1,0:T(8,128)(2,1)} %bitcast.20), channel_id=1, source_target_pairs={{0,3},{1,0},{2,1},{3,2},{4,7},{5,4},{6,5},{7,6},{8,11},{9,8},{10,9... | collective-permute-start | bytes 786440 | tf_op jit(solution)/shard_map/ppermute | solution.py:33
  4.0 1.9 %collective-permute-start.4 = (bf16[512,256]{1,0:T(8,128)(2,1)}, bf16[512,256]{1,0:T(8,128)(2,1)S(1)}, u32[]{:S(2)}, u32[]{:S(2)}) collective-permute-start(bf16[512,256]{1,0:T(8,128)(2,1)} %bitcast.21), channel_id=1, source_target_pairs={{0,2},{1,3},{2,0},{3,1},{4,6},{5,7},{6,4},{7,5},{8,10},{9,11},{10,... | collective-permute-start | bytes 786440 | tf_op jit(solution)/shard_map/ppermute | solution.py:33
  9.5 2.1 %collective-permute-start.1 = (bf16[2,512,256]{2,1,0:T(8,128)(2,1)S(1)}, bf16[2,512,256]{2,1,0:T(8,128)(2,1)S(1)}, u32[]{:S(2)}, u32[]{:S(2)}) collective-permute-start(bf16[2,512,256]{2,1,0:T(8,128)(2,1)S(1)} %pair.4.refs_1_), channel_id=1, source_target_pairs={{0,4},{1,5},{2,6},{3,7},{4,8},{5,9},{6,10},{7,11},{8,12},{9,13},{1... | collective-permute-start | bytes 1572872 | tf_op jit(solution)/shard_map/ppermute | solution.py:38
  12.5 4.2 %collective-permute-start.5 = (bf16[2,512,256]{2,1,0:T(8,128)(2,1)S(1)}, bf16[2,512,256]{2,1,0:T(8,128)(2,1)S(1)}, u32[]{:S(2)}, u32[]{:S(2)}) collective-permute-start(bf16[2,512,256]{2,1,0:T(8,128)(2,1)S(1)} %pair.5.refs_2_), channel_id=1, source_target_pairs={{0,12},{1,13},{2,14},{3,15},{4,0},{5,1},{6,2},{7,3},{8,4},{9,5},{1... | collective-permute-start | bytes 1572872 | tf_op jit(solution)/shard_map/ppermute | solution.py:38
  17.1 1.6 %collective-permute-start.7 = (bf16[2,512,256]{2,1,0:T(8,128)(2,1)S(1)}, bf16[2,512,256]{2,1,0:T(8,128)(2,1)S(1)}, u32[]{:S(2)}, u32[]{:S(2)}) collective-permute-start(bf16[2,512,256]{2,1,0:T(8,128)(2,1)S(1)} %pair.5.refs_2_), channel_id=1, source_target_pairs={{0,4},{1,5},{2,6},{3,7},{4,8},{5,9},{6,10},{7,11},{8,12},{9,13},{1... | collective-permute-start | bytes 1572872 | tf_op jit(solution)/shard_map/ppermute | solution.py:38
  18.7 2.2 %collective-permute-done.1.refs_3_ = bf16[2,512,256]{2,1,0:T(8,128)(2,1)S(1)} collective-permute-done((bf16[2,512,256]{2,1,0:T(8,128)(2,1)S(1)}, bf16[2,512,256]{2,1,0:T(8,128)(2,1)S(1)}, u32[]{:S(2)}, u32[]{:S(2)}) %collective-permute-start.1) | collective-permute-done | bytes 524320 | tf_op jit(solution)/shard_map/ppermute | solution.py:38
  20.9 2.5 %collective-permute-done.5.refs_6_ = bf16[2,512,256]{2,1,0:T(8,128)(2,1)S(1)} collective-permute-done((bf16[2,512,256]{2,1,0:T(8,128)(2,1)S(1)}, bf16[2,512,256]{2,1,0:T(8,128)(2,1)S(1)}, u32[]{:S(2)}, u32[]{:S(2)}) %collective-permute-start.5) | collective-permute-done | bytes 524320 | tf_op jit(solution)/shard_map/ppermute | solution.py:38
  23.4 3.7 %collective-permute-start.6 = (bf16[2,512,256]{2,1,0:T(8,128)(2,1)S(1)}, bf16[2,512,256]{2,1,0:T(8,128)(2,1)S(1)}, u32[]{:S(2)}, u32[]{:S(2)}) collective-permute-start(bf16[2,512,256]{2,1,0:T(8,128)(2,1)S(1)} %collective-permute-done.5.refs_6_), channel_id=1, source_target_pairs={{0,12},{1,13},{2,14},{3,15},{4,0},{5,1},{6,2},{7,3},{8,4},{9,5},{1... | collective-permute-start | bytes 1572872 | tf_op jit(solution)/shard_map/ppermute | solution.py:38
  27.1 1.5 %prepare.1.refs_4_.refs_1_ = f32[512,128]{1,0:T(8,128)S(1)} custom-call(s32[512,16]{1,0:T(8,128)S(1)} %dynamic-slice_bitcast_fusion.refs_5_.refs_0_, s32[128]{0:T(128)S(1)} %fusion.refs_2_.refs_0_.refs_1_.refs_6_.refs_9_.refs_4_.refs_8_.refs_5_), custom_call_target="tpu_custom_call" | custom-call | flops 1 | bytes 1 | tf_op jit(solution)/shard_map/prepare/pallas_call | solution.py:65
  29.0 3.4 %copy-done.2 = bf16[8,1,128,4096]{3,2,1,0:T(8,128)(2,1)S(1)} copy-done((bf16[8,1,128,4096]{3,2,1,0:T(8,128)(2,1)S(1)}, bf16[8,1,128,4096]{3,2,1,0:T(8,128)(2,1)}, u32[]{:S(2)}) %copy-start.2) | copy-done | bytes 8388632
  32.4 1.8 %encode.1 = (f32[512,128]{1,0:T(8,128)S(1)}, bf16[1024,128]{1,0:T(8,128)(2,1)S(1)}, bf16[4,1024,256]{2,1,0:T(8,128)(2,1)S(1)}, f32[8,128]{1,0:T(8,128)S(1)}) custom-call(s32[128]{0:T(128)S(1)} %fusion.refs_2_.refs_0_.refs_1_.refs_6_.refs_9_.refs_4_.refs_8_.refs_5_, bf16[2,512,256]{2,1,0:T(8,128)(2,1)S(1)} %pair.4.refs_1_, ...), custom_call_target="tpu_custom_call" | custom-call | flops 1 | bytes 1 | tf_op jit(solution)/shard_map/encode/pallas_call | solution.py:65
  35.1 3.8 %collective-permute-start.9 = (bf16[512,128]{1,0:T(8,128)(2,1)S(1)}, bf16[512,128]{1,0:T(8,128)(2,1)S(1)}, u32[]{:S(2)}, u32[]{:S(2)}) collective-permute-start(bf16[512,128]{1,0:T(8,128)(2,1)S(1)} %activate.1.refs_0_.refs_1_), channel_id=1, source_target_pairs={{0,32},{1,33},{2,34},{3,35},{4,36},{5,37},{6,38},{7,39},{8,40},{9,... | collective-permute-start | bytes 393224 | tf_op jit(solution)/shard_map/ppermute | solution.py:42
  38.8 4.8 %collective-permute-start.10 = (bf16[512,128]{1,0:T(8,128)(2,1)S(1)}, bf16[512,128]{1,0:T(8,128)(2,1)S(1)}, u32[]{:S(2)}, u32[]{:S(2)}) collective-permute-start(bf16[512,128]{1,0:T(8,128)(2,1)S(1)} %activate.1.refs_0_.refs_1_), channel_id=1, source_target_pairs={{0,64},{1,65},{2,66},{3,67},{4,68},{5,69},{6,70},{7,71},{8,72},{9,... | collective-permute-start | bytes 393224 | tf_op jit(solution)/shard_map/ppermute | solution.py:42
  43.6 1.3 collective-permute-start.11
  46.1 1.3 collective-permute-done.11.refs_3_.refs_4_
  47.5 1.3 collective-permute-done.15.refs_7_.refs_8_
  49.0 1.3 decode_far.1
  50.6 3.7 %collective-permute-start.17 = (bf16[2,512,256]{2,1,0:T(8,128)(2,1)S(1)}, bf16[2,512,256]{2,1,0:T(8,128)(2,1)S(1)}, u32[]{:S(2)}, u32[]{:S(2)}) collective-permute-start(bf16[2,512,256]{2,1,0:T(8,128)(2,1)S(1)} %get-tuple-element.46), channel_id=1, source_target_pairs={{0,12},{1,13},{2,14},{3,15},{4,0},{5,1},{6,2},{7,3},{8,4},{9,5},{1... | collective-permute-start | bytes 1572872 | tf_op jit(solution)/shard_map/ppermute | solution.py:38
  55.3 4.0 %decode.1 = (f32[2,512,256]{2,1,0:T(8,128)S(1)}, bf16[2,512,256]{2,1,0:T(8,128)(2,1)S(1)}, bf16[2,512,256]{2,1,0:T(8,128)(2,1)S(1)}, f32[2,512,256]{2,1,0:T(8,12...) custom-call(s32[128]{0:T(128)S(1)} %fusion.refs_2_.refs_0_.refs_1_.refs_6_.refs_9_.refs_4_.refs_8_.refs_5_, ...), custom_call_target="tpu_custom_call" | custom-call | flops 1 | bytes 1 | tf_op jit(solution)/shard_map/decode/pallas_call | solution.py:65
  59.3 1.7 %flip.1.refs_7_.refs_0_ = bf16[4096,512]{1,0:T(8,128)(2,1)S(1)} custom-call(s32[128]{0:T(128)S(1)} %fusion.refs_2_.refs_0_.refs_1_.refs_6_.refs_9_.refs_4_.refs_8_.refs_5_, bf16[2,512,256]{2,1,0:T(8,128)(2,1)S(1)} %pair.4.refs_1_, bf16[2,512,256]{2,1,0:T(8,128)(2,1)S(1)} %pair.5.refs_2_, bf16[2,512,256]{2,1,0:T(8,128)(2,1)S(1)} %collective-permute-done.1.refs_3_, ...), custom_call_target="tpu_custom_call" | custom-call | flops 1 | bytes 1 | tf_op jit(solution)/shard_map/flip/pallas_call | solution.py:65
  61.5 1.5 %collective-permute-start.20 = (bf16[3,512,256]{2,1,0:T(8,128)(2,1)S(1)}, bf16[3,512,256]{2,1,0:T(8,128)(2,1)S(1)}, u32[]{:S(2)}, u32[]{:S(2)}) collective-permute-start(bf16[3,512,256]{2,1,0:T(8,128)(2,1)S(1)} %get-tuple-element.50), channel_id=1, source_target_pairs={{0,4},{1,5},{2,6},{3,7},{4,8},{5,9},{6,10},{7,11},{8,12},{9,13},{1... | collective-permute-start | bytes 2359304 | tf_op jit(solution)/shard_map/ppermute | solution.py:38
  62.9 2.2 %collective-permute-start.21 = (bf16[3,512,256]{2,1,0:T(8,128)(2,1)S(1)}, bf16[3,512,256]{2,1,0:T(8,128)(2,1)S(1)}, u32[]{:S(2)}, u32[]{:S(2)}) collective-permute-start(bf16[3,512,256]{2,1,0:T(8,128)(2,1)S(1)} %get-tuple-element.51), channel_id=1, source_target_pairs={{0,12},{1,13},{2,14},{3,15},{4,0},{5,1},{6,2},{7,3},{8,4},{9,5},{1... | collective-permute-start | bytes 2359304 | tf_op jit(solution)/shard_map/ppermute | solution.py:38
  65.1 3.2 %collective-permute-start.19 = (bf16[512,256]{1,0:T(8,128)(2,1)S(1)}, bf16[512,256]{1,0:T(8,128)(2,1)S(1)}, u32[]{:S(2)}, u32[]{:S(2)}) collective-permute-start(bf16[512,256]{1,0:T(8,128)(2,1)S(1)} %get-tuple-element.48), channel_id=1, source_target_pairs={{0,12},{1,13},{2,14},{3,15},{4,0},{5,1},{6,2},{7,3},{8,4},{9,5},{1... | collective-permute-start | bytes 786440 | tf_op jit(solution)/shard_map/ppermute | solution.py:38
  68.3 6.7 %collective-permute-done.20.refs_2_ = bf16[3,512,256]{2,1,0:T(8,128)(2,1)S(1)} collective-permute-done((bf16[3,512,256]{2,1,0:T(8,128)(2,1)S(1)}, bf16[3,512,256]{2,1,0:T(8,128)(2,1)S(1)}, u32[]{:S(2)}, u32[]{:S(2)}) %collective-permute-start.20) | collective-permute-done | bytes 786464 | tf_op jit(solution)/shard_map/ppermute | solution.py:38
  75.2 2.4 %collective-permute-start.22 = (bf16[512,256]{1,0:T(8,128)(2,1)S(1)}, bf16[512,256]{1,0:T(8,128)(2,1)S(1)}, u32[]{:S(2)}, u32[]{:S(2)}) collective-permute-start(bf16[512,256]{1,0:T(8,128)(2,1)S(1)} %get-tuple-element.52), channel_id=1, source_target_pairs={{0,2},{1,3},{2,0},{3,1},{4,6},{5,7},{6,4},{7,5},{8,10},{9,11},{10,... | collective-permute-start | bytes 786440 | tf_op jit(solution)/shard_map/ppermute | solution.py:33
  78.3 2.5 %collective-permute-start.24 = (bf16[512,256]{1,0:T(8,128)(2,1)S(1)}, bf16[512,256]{1,0:T(8,128)(2,1)S(1)}, u32[]{:S(2)}, u32[]{:S(2)}) collective-permute-start(bf16[512,256]{1,0:T(8,128)(2,1)S(1)} %get-tuple-element.54), channel_id=1, source_target_pairs={{0,3},{1,0},{2,1},{3,2},{4,7},{5,4},{6,5},{7,6},{8,11},{9,8},{10,9... | collective-permute-start | bytes 786440 | tf_op jit(solution)/shard_map/ppermute | solution.py:33
  80.8 2.4 %collective-permute-done.22.refs_3_ = bf16[512,256]{1,0:T(8,128)(2,1)S(1)} collective-permute-done((bf16[512,256]{1,0:T(8,128)(2,1)S(1)}, bf16[512,256]{1,0:T(8,128)(2,1)S(1)}, u32[]{:S(2)}, u32[]{:S(2)}) %collective-permute-start.22) | collective-permute-done | bytes 262176 | tf_op jit(solution)/shard_map/ppermute | solution.py:33
  83.3 2.7 %collective-permute-done.23.refs_4_ = bf16[512,256]{1,0:T(8,128)(2,1)S(1)} collective-permute-done((bf16[512,256]{1,0:T(8,128)(2,1)S(1)}, bf16[512,256]{1,0:T(8,128)(2,1)S(1)}, u32[]{:S(2)}, u32[]{:S(2)}) %collective-permute-start.23) | collective-permute-done | bytes 262176 | tf_op jit(solution)/shard_map/ppermute | solution.py:33
  86.3 2.5 %collective-permute-start.27 = (bf16[512,256]{1,0:T(8,128)(2,1)S(1)}, bf16[512,256]{1,0:T(8,128)(2,1)S(1)}, u32[]{:S(2)}, u32[]{:S(2)}) collective-permute-start(bf16[512,256]{1,0:T(8,128)(2,1)S(1)} %get-tuple-element.55.refs_0_), channel_id=1, source_target_pairs={{0,3},{1,0},{2,1},{3,2},{4,7},{5,4},{6,5},{7,6},{8,11},{9,8},{10,9... | collective-permute-start | bytes 786440 | tf_op jit(solution)/shard_map/ppermute | solution.py:33
  89.8 5.7 %collective-permute-done.27.refs_0_ = bf16[512,256]{1,0:T(8,128)(2,1)S(1)} collective-permute-done((bf16[512,256]{1,0:T(8,128)(2,1)S(1)}, bf16[512,256]{1,0:T(8,128)(2,1)S(1)}, u32[]{:S(2)}, u32[]{:S(2)}) %collective-permute-start.27) | collective-permute-done | bytes 262176 | tf_op jit(solution)/shard_map/ppermute | solution.py:33
  95.5 1.2 collective-permute-done.28.refs_1_
  96.8 3.4 %collective-permute-start.31 = (bf16[2,512,256]{2,1,0:T(8,128)(2,1)S(1)}, bf16[2,512,256]{2,1,0:T(8,128)(2,1)S(1)}, u32[]{:S(2)}, u32[]{:S(2)}) collective-permute-start(bf16[2,512,256]{2,1,0:T(8,128)(2,1)S(1)} %pair.7.refs_2_.refs_10_), channel_id=1, source_target_pairs={{0,12},{1,13},{2,14},{3,15},{4,0},{5,1},{6,2},{7,3},{8,4},{9,5},{1... | collective-permute-start | bytes 1572872 | tf_op jit(solution)/shard_map/ppermute | solution.py:38
  100.2 1.5 %collective-permute-start.26 = (bf16[2,512,256]{2,1,0:T(8,128)(2,1)S(1)}, bf16[2,512,256]{2,1,0:T(8,128)(2,1)S(1)}, u32[]{:S(2)}, u32[]{:S(2)}) collective-permute-start(bf16[2,512,256]{2,1,0:T(8,128)(2,1)S(1)} %pair.6.refs_1_.refs_9_), channel_id=1, source_target_pairs={{0,4},{1,5},{2,6},{3,7},{4,8},{5,9},{6,10},{7,11},{8,12},{9,13},{1... | collective-permute-start | bytes 1572872 | tf_op jit(solution)/shard_map/ppermute | solution.py:38
  101.7 2.7 %collective-permute-start.29 = (bf16[2,512,256]{2,1,0:T(8,128)(2,1)S(1)}, bf16[2,512,256]{2,1,0:T(8,128)(2,1)S(1)}, u32[]{:S(2)}, u32[]{:S(2)}) collective-permute-start(bf16[2,512,256]{2,1,0:T(8,128)(2,1)S(1)} %pair.7.refs_2_.refs_10_), channel_id=1, source_target_pairs={{0,4},{1,5},{2,6},{3,7},{4,8},{5,9},{6,10},{7,11},{8,12},{9,13},{1... | collective-permute-start | bytes 1572872 | tf_op jit(solution)/shard_map/ppermute | solution.py:38
  105.0 1.9 %collective-permute-done.31.refs_4_.refs_5_ = bf16[2,512,256]{2,1,0:T(8,128)(2,1)S(1)} collective-permute-done((bf16[2,512,256]{2,1,0:T(8,128)(2,1)S(1)}, bf16[2,512,256]{2,1,0:T(8,128)(2,1)S(1)}, u32[]{:S(2)}, u32[]{:S(2)}) %collective-permute-start.31) | collective-permute-done | bytes 524320 | tf_op jit(solution)/shard_map/ppermute | solution.py:38
  106.9 3.7 %collective-permute-start.33 = (bf16[2,512,256]{2,1,0:T(8,128)(2,1)S(1)}, bf16[2,512,256]{2,1,0:T(8,128)(2,1)S(1)}, u32[]{:S(2)}, u32[]{:S(2)}) collective-permute-start(bf16[2,512,256]{2,1,0:T(8,128)(2,1)S(1)} %collective-permute-done.31.refs_4_.refs_5_), channel_id=1, source_target_pairs={{0,12},{1,13},{2,14},{3,15},{4,0},{5,1},{6,2},{7,3},{8,4},{9,5},{1... | collective-permute-start | bytes 1572872 | tf_op jit(solution)/shard_map/ppermute | solution.py:38
  111.2 1.8 %code_grad.1.refs_6_ = f32[4,512,256]{2,1,0:T(8,128)S(1)} custom-call(s32[128]{0:T(128)S(1)} %fusion.refs_2_.refs_0_.refs_1_.refs_6_.refs_9_.refs_4_.refs_8_.refs_5_, bf16[2,512,256]{2,1,0:T(8,128)(2,1)S(1)} %pair.6.refs_1_.refs_9_, bf16[2,512,256]{2,1,0:T(8,128)(2,1)S(1)} %pair.7.refs_2_.refs_10_, bf16[1024,4096]{1,0:T(8,128)(2,1)S(1)} %bitcast.16), custom_call_target="tpu_custom_call" | custom-call | flops 1 | bytes 1 | tf_op jit(solution)/shard_map/code_grad/pallas_call | solution.py:65
  113.0 3.3 %collective-permute-done.29.refs_2_.refs_3_ = bf16[2,512,256]{2,1,0:T(8,128)(2,1)S(1)} collective-permute-done((bf16[2,512,256]{2,1,0:T(8,128)(2,1)S(1)}, bf16[2,512,256]{2,1,0:T(8,128)(2,1)S(1)}, u32[]{:S(2)}, u32[]{:S(2)}) %collective-permute-start.29) | collective-permute-done | bytes 524320 | tf_op jit(solution)/shard_map/ppermute | solution.py:38
  116.3 5.1 %middle.1 = (f32[4,512,256]{2,1,0:T(8,128)S(1)}, bf16[1024,4096]{1,0:T(8,128)(2,1)}, f32[512,256]{1,0:T(8,128)}) custom-call(s32[128]{0:T(128)S(1)} %fusion.refs_2_.refs_0_.refs_1_.refs_6_.refs_9_.refs_4_.refs_8_.refs_5_, bf16[2,512,256]{2,1,0:T(8,128)(2,1)S(1)} %collective-permute-done.26.refs_1_.refs_2_, ...), custom_call_target="tpu_custom_call" | custom-call | flops 1 | bytes 1 | tf_op jit(solution)/shard_map/middle/pallas_call | solution.py:65
  121.9 1.3 close.1
  123.3 1.9 %collective-permute-done.34.refs_1_ = bf16[4,512,128]{2,1,0:T(8,128)(2,1)S(1)} collective-permute-done((bf16[4,512,128]{2,1,0:T(8,128)(2,1)S(1)}, bf16[4,512,128]{2,1,0:T(8,128)(2,1)S(1)}, u32[]{:S(2)}, u32[]{:S(2)}) %collective-permute-start.34) | collective-permute-done | bytes 524320 | tf_op jit(solution)/shard_map/ppermute | solution.py:46
  125.3 1.3 collective-permute-start.35
  126.6 1.3 collective-permute-start.36
  127.9 1.3 collective-permute-start.37
  129.2 5.3 %decoder_grad.1 = bf16[1024,4096]{1,0:T(8,128)(2,1)} custom-call(s32[128]{0:T(128)S(1)} %fusion.refs_2_.refs_0_.refs_1_.refs_6_.refs_9_.refs_4_.refs_8_.refs_5_, bf16[1024,512]{1,0:T(8,128)(2,1)S(1)} %get-tuple-element.56.refs_7_.refs_1_, bf16[2,512,256]{2,1,0:T(8,128)(2,1)S(1)} %collective-permute-done.26.refs_1_.refs_2_, ...), custom_call_target="tpu_custom_call", output_to_operand_aliasing={{}: (8, {})} | custom-call | flops 1 | bytes 1 | tf_op jit(solution)/shard_map/decoder_grad/pallas_call | solution.py:65
  135.5 2.8 %collective-permute-done.37.refs_5_ = bf16[512,128]{1,0:T(8,128)(2,1)S(1)} collective-permute-done((bf16[512,128]{1,0:T(8,128)(2,1)S(1)}, bf16[512,128]{1,0:T(8,128)(2,1)S(1)}, u32[]{:S(2)}, u32[]{:S(2)}) %collective-permute-start.37) | collective-permute-done | bytes 131104 | tf_op jit(solution)/shard_map/ppermute | solution.py:42
  138.4 2.1 %encoder_grad.1 = f32[4096,128]{1,0:T(8,128)} custom-call(bf16[4096,512]{1,0:T(8,128)(2,1)S(1)} %flip.1.refs_7_.refs_0_, f32[512,128]{1,0:T(8,128)S(1)} %prepare.1.refs_4_.refs_1_, f32[512,128]{1,0:T(8,128)S(1)} %get-tuple-element.64.refs_2_, bf16[512,128]{1,0:T(8,128)(2,1)S(1)} %collective-permute-done.35.refs_3_, ...), custom_call_target="tpu_custom_call" | custom-call | flops 1 | bytes 1 | tf_op jit(solution)/shard_map/encoder_grad/pallas_call | solution.py:65
  (67 shorter events, 14.6 us)
Async XLA Ops:
  0.6 7.6 %copy-start = (s32[1,512,256]{2,1,0:T(8,128)S(1)}, s32[1,512,256]{2,1,0:T(8,128)}, u32[]{:S(2)}) copy-start(s32[1,512,256]{2,1,0:T(8,128)} %param.11) | copy-start | bytes 1572868
  0.6 28.3 %copy-start.4 = (bf16[1,4096,128]{2,1,0:T(8,128)(2,1)S(1)}, bf16[1,4096,128]{2,1,0:T(8,128)(2,1)}, u32[]{:S(2)}) copy-start(bf16[1,4096,128]{2,1,0:T(8,128)(2,1)} %param.9) | copy-start | bytes 3145732
  0.7 7.9 %collective-permute-start = (bf16[512,256]{1,0:T(8,128)(2,1)}, bf16[512,256]{1,0:T(8,128)(2,1)S(1)}, u32[]{:S(2)}, u32[]{:S(2)}) collective-permute-start(bf16[512,256]{1,0:T(8,128)(2,1)} %bitcast.19), channel_id=1, source_target_pairs={{0,1},{1,2},{2,3},{3,0},{4,5},{5,6},{6,7},{7,4},{8,9},{9,10},{10,1... | collective-permute-start | bytes 786440 | tf_op jit(solution)/shard_map/ppermute | solution.py:33
  2.3 9.3 %collective-permute-start.3 = (bf16[512,256]{1,0:T(8,128)(2,1)}, bf16[512,256]{1,0:T(8,128)(2,1)S(1)}, u32[]{:S(2)}, u32[]{:S(2)}) collective-permute-start(bf16[512,256]{1,0:T(8,128)(2,1)} %bitcast.20), channel_id=1, source_target_pairs={{0,3},{1,0},{2,1},{3,2},{4,7},{5,4},{6,5},{7,6},{8,11},{9,8},{10,9... | collective-permute-start | bytes 786440 | tf_op jit(solution)/shard_map/ppermute | solution.py:33
  4.0 8.4 %collective-permute-start.4 = (bf16[512,256]{1,0:T(8,128)(2,1)}, bf16[512,256]{1,0:T(8,128)(2,1)S(1)}, u32[]{:S(2)}, u32[]{:S(2)}) collective-permute-start(bf16[512,256]{1,0:T(8,128)(2,1)} %bitcast.21), channel_id=1, source_target_pairs={{0,2},{1,3},{2,0},{3,1},{4,6},{5,7},{6,4},{7,5},{8,10},{9,11},{10,... | collective-permute-start | bytes 786440 | tf_op jit(solution)/shard_map/ppermute | solution.py:33
  8.5 1.0 copy-start.5
  9.5 11.3 %collective-permute-start.1 = (bf16[2,512,256]{2,1,0:T(8,128)(2,1)S(1)}, bf16[2,512,256]{2,1,0:T(8,128)(2,1)S(1)}, u32[]{:S(2)}, u32[]{:S(2)}) collective-permute-start(bf16[2,512,256]{2,1,0:T(8,128)(2,1)S(1)} %pair.4.refs_1_), channel_id=1, source_target_pairs={{0,4},{1,5},{2,6},{3,7},{4,8},{5,9},{6,10},{7,11},{8,12},{9,13},{1... | collective-permute-start | bytes 1572872 | tf_op jit(solution)/shard_map/ppermute | solution.py:38
  12.5 10.9 %collective-permute-start.5 = (bf16[2,512,256]{2,1,0:T(8,128)(2,1)S(1)}, bf16[2,512,256]{2,1,0:T(8,128)(2,1)S(1)}, u32[]{:S(2)}, u32[]{:S(2)}) collective-permute-start(bf16[2,512,256]{2,1,0:T(8,128)(2,1)S(1)} %pair.5.refs_2_), channel_id=1, source_target_pairs={{0,12},{1,13},{2,14},{3,15},{4,0},{5,1},{6,2},{7,3},{8,4},{9,5},{1... | collective-permute-start | bytes 1572872 | tf_op jit(solution)/shard_map/ppermute | solution.py:38
  16.7 12.3 %collective-permute-start.8 = (bf16[2,512,256]{2,1,0:T(8,128)(2,1)S(1)}, bf16[2,512,256]{2,1,0:T(8,128)(2,1)S(1)}, u32[]{:S(2)}, u32[]{:S(2)}) collective-permute-start(bf16[2,512,256]{2,1,0:T(8,128)(2,1)S(1)} %pair.4.refs_1_), channel_id=1, source_target_pairs={{0,12},{1,13},{2,14},{3,15},{4,0},{5,1},{6,2},{7,3},{8,4},{9,5},{1... | collective-permute-start | bytes 1572872 | tf_op jit(solution)/shard_map/ppermute | solution.py:38
  17.1 11.9 %collective-permute-start.7 = (bf16[2,512,256]{2,1,0:T(8,128)(2,1)S(1)}, bf16[2,512,256]{2,1,0:T(8,128)(2,1)S(1)}, u32[]{:S(2)}, u32[]{:S(2)}) collective-permute-start(bf16[2,512,256]{2,1,0:T(8,128)(2,1)S(1)} %pair.5.refs_2_), channel_id=1, source_target_pairs={{0,4},{1,5},{2,6},{3,7},{4,8},{5,9},{6,10},{7,11},{8,12},{9,13},{1... | collective-permute-start | bytes 1572872 | tf_op jit(solution)/shard_map/ppermute | solution.py:38
  20.9 13.3 %collective-permute-start.2 = (bf16[2,512,256]{2,1,0:T(8,128)(2,1)S(1)}, bf16[2,512,256]{2,1,0:T(8,128)(2,1)S(1)}, u32[]{:S(2)}, u32[]{:S(2)}) collective-permute-start(bf16[2,512,256]{2,1,0:T(8,128)(2,1)S(1)} %collective-permute-done.1.refs_3_), channel_id=1, source_target_pairs={{0,4},{1,5},{2,6},{3,7},{4,8},{5,9},{6,10},{7,11},{8,12},{9,13},{1... | collective-permute-start | bytes 1572872 | tf_op jit(solution)/shard_map/ppermute | solution.py:38
  23.4 11.2 %collective-permute-start.6 = (bf16[2,512,256]{2,1,0:T(8,128)(2,1)S(1)}, bf16[2,512,256]{2,1,0:T(8,128)(2,1)S(1)}, u32[]{:S(2)}, u32[]{:S(2)}) collective-permute-start(bf16[2,512,256]{2,1,0:T(8,128)(2,1)S(1)} %collective-permute-done.5.refs_6_), channel_id=1, source_target_pairs={{0,12},{1,13},{2,14},{3,15},{4,0},{5,1},{6,2},{7,3},{8,4},{9,5},{1... | collective-permute-start | bytes 1572872 | tf_op jit(solution)/shard_map/ppermute | solution.py:38
  29.0 3.4 %copy-start.2 = (bf16[8,1,128,4096]{3,2,1,0:T(8,128)(2,1)S(1)}, bf16[8,1,128,4096]{3,2,1,0:T(8,128)(2,1)}, u32[]{:S(2)}) copy-start(bf16[8,1,128,4096]{3,2,1,0:T(8,128)(2,1)} %param.12) | copy-start | bytes 25165828
  32.4 2.2 %copy-start.6 = (f32[1,128]{1,0:T(1,128)S(1)}, f32[1,128]{1,0:T(1,128)}, u32[]{:S(2)}) copy-start(f32[1,128]{1,0:T(1,128)} %refs_5_.1) | copy-start | bytes 1540
  34.6 20.7 %copy-start.3 = (bf16[8,1,128,4096]{3,2,1,0:T(8,128)(2,1)S(1)}, bf16[8,1,128,4096]{3,2,1,0:T(8,128)(2,1)}, u32[]{:S(2)}) copy-start(bf16[8,1,128,4096]{3,2,1,0:T(8,128)(2,1)} %param.12) | copy-start | bytes 25165828
  35.1 10.0 %collective-permute-start.9 = (bf16[512,128]{1,0:T(8,128)(2,1)S(1)}, bf16[512,128]{1,0:T(8,128)(2,1)S(1)}, u32[]{:S(2)}, u32[]{:S(2)}) collective-permute-start(bf16[512,128]{1,0:T(8,128)(2,1)S(1)} %activate.1.refs_0_.refs_1_), channel_id=1, source_target_pairs={{0,32},{1,33},{2,34},{3,35},{4,36},{5,37},{6,38},{7,39},{8,40},{9,... | collective-permute-start | bytes 393224 | tf_op jit(solution)/shard_map/ppermute | solution.py:42
  38.8 7.3 %collective-permute-start.10 = (bf16[512,128]{1,0:T(8,128)(2,1)S(1)}, bf16[512,128]{1,0:T(8,128)(2,1)S(1)}, u32[]{:S(2)}, u32[]{:S(2)}) collective-permute-start(bf16[512,128]{1,0:T(8,128)(2,1)S(1)} %activate.1.refs_0_.refs_1_), channel_id=1, source_target_pairs={{0,64},{1,65},{2,66},{3,67},{4,68},{5,69},{6,70},{7,71},{8,72},{9,... | collective-permute-start | bytes 393224 | tf_op jit(solution)/shard_map/ppermute | solution.py:42
  43.6 3.8 %collective-permute-start.11 = (bf16[512,128]{1,0:T(8,128)(2,1)S(1)}, bf16[512,128]{1,0:T(8,128)(2,1)S(1)}, u32[]{:S(2)}, u32[]{:S(2)}) collective-permute-start(bf16[512,128]{1,0:T(8,128)(2,1)S(1)} %activate.1.refs_0_.refs_1_), channel_id=1, source_target_pairs={{0,96},{1,97},{2,98},{3,99},{4,100},{5,101},{6,102},{7,103},{8,104... | collective-permute-start | bytes 393224 | tf_op jit(solution)/shard_map/ppermute | solution.py:42
  44.9 2.5 %collective-permute-start.12 = (bf16[512,128]{1,0:T(8,128)(2,1)S(1)}, bf16[512,128]{1,0:T(8,128)(2,1)S(1)}, u32[]{:S(2)}, u32[]{:S(2)}) collective-permute-start(bf16[512,128]{1,0:T(8,128)(2,1)S(1)} %activate.1.refs_0_.refs_1_), channel_id=1, source_target_pairs={{0,16},{1,17},{2,18},{3,19},{4,20},{5,21},{6,22},{7,23},{8,24},{9,... | collective-permute-start | bytes 393224 | tf_op jit(solution)/shard_map/ppermute | solution.py:46
  45.0 2.4 %collective-permute-start.13 = (bf16[512,128]{1,0:T(8,128)(2,1)S(1)}, bf16[512,128]{1,0:T(8,128)(2,1)S(1)}, u32[]{:S(2)}, u32[]{:S(2)}) collective-permute-start(bf16[512,128]{1,0:T(8,128)(2,1)S(1)} %collective-permute-done.9.refs_1_.refs_2_), channel_id=1, source_target_pairs={{0,16},{1,17},{2,18},{3,19},{4,20},{5,21},{6,22},{7,23},{8,24},{9,... | collective-permute-start | bytes 393224 | tf_op jit(solution)/shard_map/ppermute | solution.py:46
  46.1 1.3 collective-permute-start.14
  47.4 1.3 collective-permute-start.15
  50.3 10.9 %collective-permute-start.16 = (bf16[2,512,256]{2,1,0:T(8,128)(2,1)S(1)}, bf16[2,512,256]{2,1,0:T(8,128)(2,1)S(1)}, u32[]{:S(2)}, u32[]{:S(2)}) collective-permute-start(bf16[2,512,256]{2,1,0:T(8,128)(2,1)S(1)} %get-tuple-element.39.refs_9_.refs_3_), channel_id=1, source_target_pairs={{0,4},{1,5},{2,6},{3,7},{4,8},{5,9},{6,10},{7,11},{8,12},{9,13},{1... | collective-permute-start | bytes 1572872 | tf_op jit(solution)/shard_map/ppermute | solution.py:38
  50.6 10.6 %collective-permute-start.17 = (bf16[2,512,256]{2,1,0:T(8,128)(2,1)S(1)}, bf16[2,512,256]{2,1,0:T(8,128)(2,1)S(1)}, u32[]{:S(2)}, u32[]{:S(2)}) collective-permute-start(bf16[2,512,256]{2,1,0:T(8,128)(2,1)S(1)} %get-tuple-element.46), channel_id=1, source_target_pairs={{0,12},{1,13},{2,14},{3,15},{4,0},{5,1},{6,2},{7,3},{8,4},{9,5},{1... | collective-permute-start | bytes 1572872 | tf_op jit(solution)/shard_map/ppermute | solution.py:38
  61.5 13.5 %collective-permute-start.20 = (bf16[3,512,256]{2,1,0:T(8,128)(2,1)S(1)}, bf16[3,512,256]{2,1,0:T(8,128)(2,1)S(1)}, u32[]{:S(2)}, u32[]{:S(2)}) collective-permute-start(bf16[3,512,256]{2,1,0:T(8,128)(2,1)S(1)} %get-tuple-element.50), channel_id=1, source_target_pairs={{0,4},{1,5},{2,6},{3,7},{4,8},{5,9},{6,10},{7,11},{8,12},{9,13},{1... | collective-permute-start | bytes 2359304 | tf_op jit(solution)/shard_map/ppermute | solution.py:38
  62.9 12.0 %collective-permute-start.21 = (bf16[3,512,256]{2,1,0:T(8,128)(2,1)S(1)}, bf16[3,512,256]{2,1,0:T(8,128)(2,1)S(1)}, u32[]{:S(2)}, u32[]{:S(2)}) collective-permute-start(bf16[3,512,256]{2,1,0:T(8,128)(2,1)S(1)} %get-tuple-element.51), channel_id=1, source_target_pairs={{0,12},{1,13},{2,14},{3,15},{4,0},{5,1},{6,2},{7,3},{8,4},{9,5},{1... | collective-permute-start | bytes 2359304 | tf_op jit(solution)/shard_map/ppermute | solution.py:38
  65.1 15.7 %collective-permute-start.18 = (bf16[512,256]{1,0:T(8,128)(2,1)S(1)}, bf16[512,256]{1,0:T(8,128)(2,1)S(1)}, u32[]{:S(2)}, u32[]{:S(2)}) collective-permute-start(bf16[512,256]{1,0:T(8,128)(2,1)S(1)} %get-tuple-element.47), channel_id=1, source_target_pairs={{0,4},{1,5},{2,6},{3,7},{4,8},{5,9},{6,10},{7,11},{8,12},{9,13},{1... | collective-permute-start | bytes 786440 | tf_op jit(solution)/shard_map/ppermute | solution.py:38
  65.1 15.7 %collective-permute-start.19 = (bf16[512,256]{1,0:T(8,128)(2,1)S(1)}, bf16[512,256]{1,0:T(8,128)(2,1)S(1)}, u32[]{:S(2)}, u32[]{:S(2)}) collective-permute-start(bf16[512,256]{1,0:T(8,128)(2,1)S(1)} %get-tuple-element.48), channel_id=1, source_target_pairs={{0,12},{1,13},{2,14},{3,15},{4,0},{5,1},{6,2},{7,3},{8,4},{9,5},{1... | collective-permute-start | bytes 786440 | tf_op jit(solution)/shard_map/ppermute | solution.py:38
  75.2 8.0 %collective-permute-start.22 = (bf16[512,256]{1,0:T(8,128)(2,1)S(1)}, bf16[512,256]{1,0:T(8,128)(2,1)S(1)}, u32[]{:S(2)}, u32[]{:S(2)}) collective-permute-start(bf16[512,256]{1,0:T(8,128)(2,1)S(1)} %get-tuple-element.52), channel_id=1, source_target_pairs={{0,2},{1,3},{2,0},{3,1},{4,6},{5,7},{6,4},{7,5},{8,10},{9,11},{10,... | collective-permute-start | bytes 786440 | tf_op jit(solution)/shard_map/ppermute | solution.py:33
  77.6 8.4 %collective-permute-start.23 = (bf16[512,256]{1,0:T(8,128)(2,1)S(1)}, bf16[512,256]{1,0:T(8,128)(2,1)S(1)}, u32[]{:S(2)}, u32[]{:S(2)}) collective-permute-start(bf16[512,256]{1,0:T(8,128)(2,1)S(1)} %get-tuple-element.53), channel_id=1, source_target_pairs={{0,1},{1,2},{2,3},{3,0},{4,5},{5,6},{6,7},{7,4},{8,9},{9,10},{10,1... | collective-permute-start | bytes 786440 | tf_op jit(solution)/shard_map/ppermute | solution.py:33
  78.3 7.7 %collective-permute-start.24 = (bf16[512,256]{1,0:T(8,128)(2,1)S(1)}, bf16[512,256]{1,0:T(8,128)(2,1)S(1)}, u32[]{:S(2)}, u32[]{:S(2)}) collective-permute-start(bf16[512,256]{1,0:T(8,128)(2,1)S(1)} %get-tuple-element.54), channel_id=1, source_target_pairs={{0,3},{1,0},{2,1},{3,2},{4,7},{5,4},{6,5},{7,6},{8,11},{9,8},{10,9... | collective-permute-start | bytes 786440 | tf_op jit(solution)/shard_map/ppermute | solution.py:33
  86.3 9.2 %collective-permute-start.27 = (bf16[512,256]{1,0:T(8,128)(2,1)S(1)}, bf16[512,256]{1,0:T(8,128)(2,1)S(1)}, u32[]{:S(2)}, u32[]{:S(2)}) collective-permute-start(bf16[512,256]{1,0:T(8,128)(2,1)S(1)} %get-tuple-element.55.refs_0_), channel_id=1, source_target_pairs={{0,3},{1,0},{2,1},{3,2},{4,7},{5,4},{6,5},{7,6},{8,11},{9,8},{10,9... | collective-permute-start | bytes 786440 | tf_op jit(solution)/shard_map/ppermute | solution.py:33
  88.8 8.0 %collective-permute-start.28 = (bf16[512,256]{1,0:T(8,128)(2,1)S(1)}, bf16[512,256]{1,0:T(8,128)(2,1)S(1)}, u32[]{:S(2)}, u32[]{:S(2)}) collective-permute-start(bf16[512,256]{1,0:T(8,128)(2,1)S(1)} %get-tuple-element.55.refs_0_), channel_id=1, source_target_pairs={{0,2},{1,3},{2,0},{3,1},{4,6},{5,7},{6,4},{7,5},{8,10},{9,11},{10,... | collective-permute-start | bytes 786440 | tf_op jit(solution)/shard_map/ppermute | solution.py:33
  89.7 10.5 %collective-permute-start.25 = (bf16[512,256]{1,0:T(8,128)(2,1)S(1)}, bf16[512,256]{1,0:T(8,128)(2,1)S(1)}, u32[]{:S(2)}, u32[]{:S(2)}) collective-permute-start(bf16[512,256]{1,0:T(8,128)(2,1)S(1)} %get-tuple-element.55.refs_0_), channel_id=1, source_target_pairs={{0,1},{1,2},{2,3},{3,0},{4,5},{5,6},{6,7},{7,4},{8,9},{9,10},{10,1... | collective-permute-start | bytes 786440 | tf_op jit(solution)/shard_map/ppermute | solution.py:33
  96.8 10.1 %collective-permute-start.31 = (bf16[2,512,256]{2,1,0:T(8,128)(2,1)S(1)}, bf16[2,512,256]{2,1,0:T(8,128)(2,1)S(1)}, u32[]{:S(2)}, u32[]{:S(2)}) collective-permute-start(bf16[2,512,256]{2,1,0:T(8,128)(2,1)S(1)} %pair.7.refs_2_.refs_10_), channel_id=1, source_target_pairs={{0,12},{1,13},{2,14},{3,15},{4,0},{5,1},{6,2},{7,3},{8,4},{9,5},{1... | collective-permute-start | bytes 1572872 | tf_op jit(solution)/shard_map/ppermute | solution.py:38
  100.2 10.5 %collective-permute-start.26 = (bf16[2,512,256]{2,1,0:T(8,128)(2,1)S(1)}, bf16[2,512,256]{2,1,0:T(8,128)(2,1)S(1)}, u32[]{:S(2)}, u32[]{:S(2)}) collective-permute-start(bf16[2,512,256]{2,1,0:T(8,128)(2,1)S(1)} %pair.6.refs_1_.refs_9_), channel_id=1, source_target_pairs={{0,4},{1,5},{2,6},{3,7},{4,8},{5,9},{6,10},{7,11},{8,12},{9,13},{1... | collective-permute-start | bytes 1572872 | tf_op jit(solution)/shard_map/ppermute | solution.py:38
  101.7 14.6 %collective-permute-start.29 = (bf16[2,512,256]{2,1,0:T(8,128)(2,1)S(1)}, bf16[2,512,256]{2,1,0:T(8,128)(2,1)S(1)}, u32[]{:S(2)}, u32[]{:S(2)}) collective-permute-start(bf16[2,512,256]{2,1,0:T(8,128)(2,1)S(1)} %pair.7.refs_2_.refs_10_), channel_id=1, source_target_pairs={{0,4},{1,5},{2,6},{3,7},{4,8},{5,9},{6,10},{7,11},{8,12},{9,13},{1... | collective-permute-start | bytes 1572872 | tf_op jit(solution)/shard_map/ppermute | solution.py:38
  104.5 11.8 %collective-permute-start.30 = (bf16[2,512,256]{2,1,0:T(8,128)(2,1)S(1)}, bf16[2,512,256]{2,1,0:T(8,128)(2,1)S(1)}, u32[]{:S(2)}, u32[]{:S(2)}) collective-permute-start(bf16[2,512,256]{2,1,0:T(8,128)(2,1)S(1)} %pair.6.refs_1_.refs_9_), channel_id=1, source_target_pairs={{0,12},{1,13},{2,14},{3,15},{4,0},{5,1},{6,2},{7,3},{8,4},{9,5},{1... | collective-permute-start | bytes 1572872 | tf_op jit(solution)/shard_map/ppermute | solution.py:38
  106.9 14.5 %collective-permute-start.33 = (bf16[2,512,256]{2,1,0:T(8,128)(2,1)S(1)}, bf16[2,512,256]{2,1,0:T(8,128)(2,1)S(1)}, u32[]{:S(2)}, u32[]{:S(2)}) collective-permute-start(bf16[2,512,256]{2,1,0:T(8,128)(2,1)S(1)} %collective-permute-done.31.refs_4_.refs_5_), channel_id=1, source_target_pairs={{0,12},{1,13},{2,14},{3,15},{4,0},{5,1},{6,2},{7,3},{8,4},{9,5},{1... | collective-permute-start | bytes 1572872 | tf_op jit(solution)/shard_map/ppermute | solution.py:38
  110.7 11.2 %collective-permute-start.32 = (bf16[2,512,256]{2,1,0:T(8,128)(2,1)S(1)}, bf16[2,512,256]{2,1,0:T(8,128)(2,1)S(1)}, u32[]{:S(2)}, u32[]{:S(2)}) collective-permute-start(bf16[2,512,256]{2,1,0:T(8,128)(2,1)S(1)} %collective-permute-done.26.refs_1_.refs_2_), channel_id=1, source_target_pairs={{0,4},{1,5},{2,6},{3,7},{4,8},{5,9},{6,10},{7,11},{8,12},{9,13},{1... | collective-permute-start | bytes 1572872 | tf_op jit(solution)/shard_map/ppermute | solution.py:38
  123.2 2.0 %collective-permute-start.34 = (bf16[4,512,128]{2,1,0:T(8,128)(2,1)S(1)}, bf16[4,512,128]{2,1,0:T(8,128)(2,1)S(1)}, u32[]{:S(2)}, u32[]{:S(2)}) collective-permute-start(bf16[4,512,128]{2,1,0:T(8,128)(2,1)S(1)} %get-tuple-element.62), channel_id=1, source_target_pairs={{0,16},{1,17},{2,18},{3,19},{4,20},{5,21},{6,22},{7,23},{8,24},{9,... | collective-permute-start | bytes 1572872 | tf_op jit(solution)/shard_map/ppermute | solution.py:46
  125.3 9.2 %collective-permute-start.35 = (bf16[512,128]{1,0:T(8,128)(2,1)S(1)}, bf16[512,128]{1,0:T(8,128)(2,1)S(1)}, u32[]{:S(2)}, u32[]{:S(2)}) collective-permute-start(bf16[512,128]{1,0:T(8,128)(2,1)S(1)} %get-tuple-element.63.refs_9_), channel_id=1, source_target_pairs={{32,0},{33,1},{34,2},{35,3},{36,4},{37,5},{38,6},{39,7},{40,8},{41... | collective-permute-start | bytes 393224 | tf_op jit(solution)/shard_map/ppermute | solution.py:42
  126.6 8.9 %collective-permute-start.36 = (bf16[512,128]{1,0:T(8,128)(2,1)S(1)}, bf16[512,128]{1,0:T(8,128)(2,1)S(1)}, u32[]{:S(2)}, u32[]{:S(2)}) collective-permute-start(bf16[512,128]{1,0:T(8,128)(2,1)S(1)} %get-tuple-element.65), channel_id=1, source_target_pairs={{64,0},{65,1},{66,2},{67,3},{68,4},{69,5},{70,6},{71,7},{72,8},{73... | collective-permute-start | bytes 393224 | tf_op jit(solution)/shard_map/ppermute | solution.py:42
  127.9 10.4 %collective-permute-start.37 = (bf16[512,128]{1,0:T(8,128)(2,1)S(1)}, bf16[512,128]{1,0:T(8,128)(2,1)S(1)}, u32[]{:S(2)}, u32[]{:S(2)}) collective-permute-start(bf16[512,128]{1,0:T(8,128)(2,1)S(1)} %get-tuple-element.66), channel_id=1, source_target_pairs={{96,0},{97,1},{98,2},{99,3},{100,4},{101,5},{102,6},{103,7},{104,8... | collective-permute-start | bytes 393224 | tf_op jit(solution)/shard_map/ppermute | solution.py:42
  129.2 11.3 %copy-start.1 = (s32[1,512,256]{2,1,0:T(8,128)S(1)}, s32[1,512,256]{2,1,0:T(8,128)}, u32[]{:S(2)}) copy-start(s32[1,512,256]{2,1,0:T(8,128)} %param.11) | copy-start | bytes 1572868
